TPU v7x, 256 devices: a whole 4x4x8 slice. The times are simulated.
256 devices in a mesh: outer: 16 (over x, y_hi, core), inner: 16 (over y_lo, z).
Axes of the slice: x: 4, y: 4 (y_hi: 2, y_lo: 2; y = y_hi * 2 + y_lo), z: 8, core: 2. Of those that a mesh axis runs over, the one named last changes fastest.
Arguments:
- q_nope: bfloat16 [4096, 8192], P('inner', 'outer'), may hold values from -6 to 6
- q_rope: bfloat16 [4096, 4096], P('inner', 'outer'), may hold values from -8 to 8
- absorb_key: bfloat16 [64, 128, 512], P('outer'), may hold values from -0.5 to 0.5
- kv_latent: bfloat16 [4096, 576], P('inner'), may hold values from -8 to 8
- value_up: bfloat16 [64, 512, 128], P('outer'), may hold values from -0.75 to 0.75
- out_proj: bfloat16 [8192, 7168], P(None, 'outer'), may hold values from -0.0625 to 0.0625
Outputs:
- mixed: bfloat16 [4096, 7168], P('inner', 'outer')
All inputs are finite; a program needn't handle non-finite values.
Results may differ from a plain program's by a relative error of at most 0.012.
Values may be sent and summed in bfloat16 or wider, within the bound.
A program may use at most 64 MiB of HBM per device.

v0:
```python
import math

import jax
import jax.numpy as jnp
from jax import lax
from jax.sharding import PartitionSpec as P

NOPE = 128
ROPE = 64
VDIM = 128


def on_device(q_nope, q_rope, absorb_key, kv_latent, value_up, out_proj):
    row_count = q_nope.shape[0]
    head_count = absorb_key.shape[0]
    lat_width = absorb_key.shape[2]
    score_scale = 1.0 / math.sqrt(NOPE + ROPE)
    my_index = lax.axis_index("inner")
    local_rows = lax.iota(jnp.int32, row_count)
    positions = my_index * row_count + local_rows
    query_heads = q_nope.reshape(row_count, head_count, NOPE)
    absorbed = jnp.einsum(
        "thn,hnc->htc", query_heads, absorb_key, preferred_element_type=jnp.float32
    ).astype(jnp.bfloat16)
    rotary_heads = q_rope.reshape(row_count, head_count, ROPE).transpose(1, 0, 2)
    queries = jnp.concatenate([absorbed, rotary_heads], axis=2)
    last_position = jnp.max(positions)
    start_state = (
        jnp.full((head_count, row_count), -1e30, jnp.float32),
        jnp.zeros((head_count, row_count), jnp.float32),
        jnp.zeros((head_count, row_count, lat_width), jnp.float32),
    )
    shard_piece = lax.all_gather(kv_latent, "inner", axis=0, tiled=True)
    piece_len = shard_piece.shape[0]

    def compute(state):
        running_max, running_sum, accum = state
        scores = (
            jnp.einsum("hqc,kc->hqk", queries, shard_piece, preferred_element_type=jnp.float32)
            * score_scale
        )
        key_pos = lax.iota(jnp.int32, piece_len)
        visible = key_pos[None, None, :] <= positions[None, :, None]
        scores = jnp.where(visible, scores, jnp.float32(-1e30))
        new_max = jnp.maximum(running_max, jnp.max(scores, axis=2))
        weights = jnp.where(visible, jnp.exp(scores - new_max[:, :, None]), jnp.float32(0.0))
        new_sum = jnp.sum(weights, axis=2)
        update = jnp.einsum(
            "hqk,kc->hqc",
            weights.astype(jnp.bfloat16),
            shard_piece[:, :lat_width],
            preferred_element_type=jnp.float32,
        )
        return (new_max, new_sum, update)

    running_max, running_sum, accum = lax.cond(
        jnp.int32(0) > last_position, lambda state: state, compute, start_state
    )
    latent_out = (accum / running_sum[:, :, None]).astype(jnp.bfloat16)
    values = jnp.einsum(
        "hqc,hcv->hqv", latent_out, value_up, preferred_element_type=jnp.float32
    ).astype(jnp.bfloat16)
    flat_values = values.transpose(1, 0, 2).reshape(row_count, head_count * VDIM)
    mixed = jnp.dot(
        lax.all_gather(flat_values, "outer", axis=1, tiled=True),
        out_proj,
        preferred_element_type=jnp.float32,
    )
    return mixed.astype(jnp.bfloat16)


def solution(mesh):
    placed = (
        P("inner", "outer"),
        P("inner", "outer"),
        P("outer", None, None),
        P("inner", None),
        P("outer", None, None),
        P(None, "outer"),
    )
    return jax.shard_map(
        on_device, mesh=mesh, in_specs=placed, out_specs=P("inner", "outer"), check_vma=False
    )
```

profile of v0, /device:TPU:9, one launch (start us, length us, event | category | flops | bytes accessed | tf_op | source)
XLA Modules:
  0.0 188.7 jit_solution(6402841290724734801)
XLA Ops:
  6.5 0.0 copy-start
  6.5 0.0 all-gather.3.cloned.1.call-start
  6.5 1.9 %copy.16 = bf16[256,576]{1,0:T(8,128)(2,1)} copy(bf16[256,576]{0,1:T(8,128)(2,1)} %param.11) | data formatting | bytes 589824 | tf_op args[3]
  8.5 0.0 all-gather.3.cloned.1.call-update
  8.5 0.0 all-gather.5.cloned.1.call-start
  8.6 0.6 fusion.15
  9.8 1.0 copy.14
  10.8 0.2 copy.15
  11.0 0.0 copy-done
  11.0 1.4 convolution_convert_fusion
  12.4 1.2 pad_maximum_fusion
  13.6 68.7 %all-gather.3.cloned.1.call-done = bf16[4096,576]{1,0:T(8,128)(2,1)} async-done(((bf16[256,576]{1,0:T(8,128)(2,1)}), bf16[4096,576]{1,0:T(8,128)(2,1)}) %all-gather.3.cloned.1.call-update) | async-done | bytes 4718608 | tf_op jit(solution)/shard_map/all_gather | solution.py:33
  82.3 0.0 copy-start.2
  82.3 24.8 %conditional.1 = (f32[4,256]{1,0:T(4,128)S(1)}, f32[4,256,512]{2,1,0:T(8,128)S(1)}) conditional(s32[]{:T(128)} %convert_element_type.22, (s32[256]{0:T(256)S(1)}, bf16[4,256,576]{2,1,0:T(8,128)(2,1)}, bf16[4096,576]{1,0:T(8,128)(2,1)}) %tuple.13, () %tuple.14), branch_computations={%region_1.4_spmd, %region_4.5_spmd} | conditional | flops 9182379008 | bytes 70935600 | solution.py:56
  82.3 1.6 iota_compare_fusion
  84.0 10.2 %fusion = (f32[4,256]{1,0:T(4,128)S(1)}, f32[4,256,4096]{2,1,0:T(8,128)S(1)}) fusion(pred[256,4096]{1,0:T(8,128)(4,1)} %iota_compare_fusion, bf16[4,256,576]{2,1,0:T(8,128)(2,1)} %get-tuple-element.22, bf16[4096,576]{1,0:T(8,128)(2,1)} %get-tuple-element.13), kind=kOutput, calls=%fused_computation.2 | convolution fusion | flops 4844420096 | bytes 23728128 | tf_op jit(solution)/shard_map/cond/branch_0_fun/hqc,kc->hqk/dot_general | solution.py:39
  94.2 0.0 copy-start.1
  94.2 7.8 %fusion.3 = f32[4,256,512]{2,1,0:T(8,128)S(1)} fusion(f32[4,256,4096]{2,1,0:T(8,128)S(1)} %get-tuple-element.25, f32[4,256]{1,0:T(4,128)S(1)} %broadcast_maximum_fusion, pred[256,4096]{1,0:T(8,128)(4,1)} %iota_compare_fusion, bf16[4096,576]{1,0:T(8,128)(2,1)} %get-tuple-element.13), kind=kOutput, calls=%fused_computation.5 | convolution fusion | flops 4315938816 | bytes 24121344 | tf_op jit(solution)/shard_map/cond/branch_0_fun/hqk,kc->hqc/dot_general | solution.py:48
  102.1 0.0 copy-done.1
  102.1 5.0 %fusion.2 = f32[4,256]{1,0:T(4,128)S(1)} fusion(f32[4,256,4096]{2,1,0:T(8,128)S(1)} %get-tuple-element.25, f32[4,256]{1,0:T(4,128)S(1)} %broadcast_maximum_fusion, pred[256,4096]{1,0:T(8,128)(4,1)S(1)} %copy-done.1), kind=kLoop, calls=%fused_computation.4 | loop fusion | flops 20970496 | bytes 17833984 | tf_op jit(solution)/shard_map/cond/branch_0_fun/reduce_sum | solution.py:47
  107.1 0.0 copy-done.2
  107.1 1.3 convolution_convert_fusion.1
  108.5 0.0 all-gather.5.cloned.1.call-update
  108.5 66.3 %all-gather.5.cloned.1.call-done = bf16[256,8192]{0,1:T(8,128)(2,1)} async-done(((bf16[256,512]{0,1:T(8,128)(2,1)}), bf16[256,8192]{0,1:T(8,128)(2,1)}) %all-gather.5.cloned.1.call-update) | async-done | bytes 4194320 | tf_op jit(solution)/shard_map/all_gather | solution.py:65
  174.8 7.0 %convolution_convert_fusion.2 = bf16[256,448]{0,1:T(8,128)(2,1)} fusion(bf16[8192,448]{0,1:T(8,128)(2,1)} %param.13, bf16[256,8192]{0,1:T(8,128)(2,1)} %all-gather.5.cloned.1.call-done), kind=kOutput, calls=%fused_computation.20 | convolution fusion | flops 1879162880 | bytes 11763712 | tf_op jit(solution)/shard_map/dot_general | solution.py:64
  (2 shorter events, 0.0 us)
Async XLA Ops:
  6.5 4.5 %copy-start = (bf16[4,128,512]{2,1,0:T(8,128)(2,1)S(1)}, bf16[4,128,512]{2,1,0:T(8,128)(2,1)}, u32[]{:S(2)}) copy-start(bf16[4,128,512]{2,1,0:T(8,128)(2,1)} %param.10) | copy-start | bytes 1572868
  6.5 75.8 %all-gather.3.cloned.1.call-start = ((), (), s32[]{:S(2)}) async-start(), calls=%async_computation | async-start | bytes 5570560 | tf_op jit(solution)/shard_map/all_gather | solution.py:33
  8.5 166.3 %all-gather.5.cloned.1.call-start = ((), (), s32[]{:S(2)}) async-start(), calls=%async_computation.1 | async-start | bytes 4456448 | tf_op jit(solution)/shard_map/all_gather | solution.py:65
  82.3 24.8 %copy-start.2 = (bf16[4,512,128]{2,1,0:T(8,128)(2,1)S(1)}, bf16[4,512,128]{2,1,0:T(8,128)(2,1)}, u32[]{:S(2)}) copy-start(bf16[4,512,128]{2,1,0:T(8,128)(2,1)} %param.12) | copy-start | bytes 1572868
  94.2 7.8 %copy-start.1 = (pred[256,4096]{1,0:T(8,128)(4,1)S(1)}, pred[256,4096]{1,0:T(8,128)(4,1)}, u32[]{:S(2)}) copy-start(pred[256,4096]{1,0:T(8,128)(4,1)} %iota_compare_fusion) | copy-start | bytes 3145732 | tf_op jit(solution)/shard_map/cond
Sparse Core Ops, SparseCore 0:
  9.1 73.1 all-gather.2
  108.6 66.1 all-gather.4
where the time goes:
time: 191 us; the launch traced here: 189 us
  waiting for transfers between devices  135 us (71%)
  matrix products  27.8 us (15%)
  between operations  14.1 us (7%)
  other arithmetic  8.56 us (4%)
  local copies, waits for them, and re-layouts  3.12 us (2%)
    all_gather x1, waiting for transfers between devices, on_device(): shard_piece = lax.all_gather(kv_latent, 'inner', axis=0, tiled=True)  68.7 us
    all_gather x1, waiting for transfers between devices, on_device(): lax.all_gather(flat_values, 'outer', axis=1, tiled=True)  66.3 us
    dot_general x1, matrix products, compute(): jnp.einsum('hqc,kc->hqk', queries, shard_piece, preferred_element_type=jn...  10.2 us
    dot_general x1, matrix products, compute(): jnp.einsum('hqk,kc->hqc', weights.astype(jnp.bfloat16), shard_piece[:, :l...  7.81 us
    dot_general x1, matrix products, on_device(): jnp.dot(lax.all_gather(flat_values, 'outer', axis=1, tiled=True), out_pro...  7.03 us
    reduce_sum x1, other arithmetic, compute(): new_sum = jnp.sum(weights, axis=2)  5.05 us
  transfers between devices with their start and end apart: 2, of which 2 were waited for; matrix products, arithmetic and copies ran while one was open for 2% of the time, Pallas kernels for 0%

commit v1 on v0

v1 whole, which is shorter than its diff:
```python
import math

import jax
import jax.numpy as jnp
from jax import lax
from jax.experimental import pallas as pl
from jax.experimental.pallas import tpu as pltpu
from jax.sharding import PartitionSpec as P

NOPE = 128
ROPE = 64
VDIM = 128
LAT = 512
WIDE = LAT + ROPE
MESH = pl.DeviceIdType.MESH
NT = (((1,), (1,)), ((), ()))
SCALE = math.log2(math.e) / math.sqrt(NOPE + ROPE)
NX, NZ = 4, 8


def div(a, b):
    return a // b if isinstance(a, int) else lax.div(a, b)


def rem(a, b):
    return a % b if isinstance(a, int) else lax.rem(a, b)


def kernel(
    qn_hbm, qr_hbm, ak_hbm, kv_hbm, vu_hbm, wo_hbm, out_ref,
    qn, qr, ak, vu, wo, kvbuf, vbuf, query, peak, total, acc, mix,
    local_sem, kv_recv, send_z, send_y, sib_a, sib_b, v_recv, send_x, send_c, sib_v,
):
    heads, rows = query.shape[0], query.shape[1]
    o, i = lax.axis_index("outer"), lax.axis_index("inner")
    core, yh, x = rem(o, 2), rem(div(o, 2), 2), div(o, 4)
    yl, z = div(i, NZ), rem(i, NZ)

    def outer_of(x_, yh_, core_):
        return (x_ * 2 + yh_) * 2 + core_

    sibling = (outer_of(x, yh, 1 - core), i)
    z_up = (o, yl * NZ + rem(z + 1, NZ))
    z_down = (o, yl * NZ + rem(z + NZ - 1, NZ))
    y_up = (outer_of(x, rem(yh + yl, 2), core), (1 - yl) * NZ + z)
    y_down = (outer_of(x, rem(yh + 1 - yl, 2), core), (1 - yl) * NZ + z)
    y_far = (outer_of(x, 1 - yh, core), i)
    x_up = (outer_of(rem(x + 1, NX), yh, core), i)
    x_down = (outer_of(rem(x + NX - 1, NX), yh, core), i)

    locals_ = [
        pltpu.make_async_copy(kv_hbm.at[part], kvbuf.at[i, part], local_sem.at[part])
        for part in range(4)
    ]
    for n, (src, dst) in enumerate(
        [(qn_hbm, qn), (ak_hbm, ak), (qr_hbm, qr), (vu_hbm, vu), (wo_hbm, wo)]
    ):
        locals_.append(pltpu.make_async_copy(src, dst, local_sem.at[4 + n]))
    for copy in locals_:
        copy.start()

    barrier = pltpu.get_barrier_semaphore()
    partners = (sibling, z_up, z_down, y_up, y_down, y_far, x_up, x_down)
    for partner in partners:
        pl.semaphore_signal(barrier, inc=1, device_id=partner, device_id_type=MESH)
    pl.semaphore_wait(barrier, len(partners))

    def kv_copy(j, k, send_sem, target):
        piece = kvbuf.at[j, 2 * core + k]
        return pltpu.make_async_remote_copy(
            src_ref=piece, dst_ref=piece, send_sem=send_sem,
            recv_sem=kv_recv.at[j, 2 * core + k], device_id=target, device_id_type=MESH,
        )

    def kv_arrived(j, part):
        piece = kvbuf.at[j, part]
        pltpu.make_async_remote_copy(
            src_ref=piece, dst_ref=piece, send_sem=send_z.at[0, 0],
            recv_sem=kv_recv.at[j, part], device_id=sibling, device_id_type=MESH,
        ).wait_recv()

    def z_of(r):
        step = div(r + 1, 2) * (1 - 2 * rem(r, 2))
        return rem(z + step + NZ, NZ)

    y_target = (y_up, y_down)

    for part in range(4):
        locals_[part].wait()
    for k in range(2):
        kv_copy(i, k, send_z.at[0, k], z_up).start()
        kv_copy(i, k, send_z.at[7, k], z_down).start()
    for k in range(2):
        @pl.when(yl == 0)
        def _():
            kv_copy(i, k, send_y.at[0, k], y_target[k]).start()

    def z_forwards(r, k):
        return (r <= 4) | (r == 5 + k)

    def z_target(r):
        return (o, yl * NZ + rem(z + 2 * rem(r, 2) - 1 + NZ, NZ))

    def relay_a(r):
        j = yl * NZ + z_of(r)
        for k in range(2):
            kv_arrived(j, 2 * core + k)

            @pl.when(z_forwards(r, k))
            def _():
                kv_copy(j, k, send_z.at[r, k], z_target(r)).start()

            @pl.when(yl == 0)
            def _():
                kv_copy(j, k, send_y.at[r, k], y_target[k]).start()

            kv_copy(j, k, sib_a.at[r, k], sibling).start()

    def relay_b(r):
        j = z_of(r)
        for k in range(2):
            kv_arrived(j, 2 * core + k)
            kv_copy(j, k, sib_b.at[r, k], sibling).start()

    locals_[4].wait()
    locals_[5].wait()
    locals_[6].wait()
    for h in range(heads):
        query[h, :, :LAT] = jnp.dot(
            qn[:, h * NOPE : (h + 1) * NOPE], ak[h], preferred_element_type=jnp.float32
        ).astype(jnp.bfloat16)
        query[h, :, LAT:] = qr[:, h * ROPE : (h + 1) * ROPE]

    def attend(j, first):
        keys = kvbuf[j].reshape(rows, WIDE)
        latent = keys[:, :LAT]

        def scores(h):
            s = lax.dot_general(query[h], keys, NT, preferred_element_type=jnp.float32) * SCALE
            if first:
                row = lax.broadcasted_iota(jnp.int32, s.shape, 0)
                col = lax.broadcasted_iota(jnp.int32, s.shape, 1)
                s = jnp.where(col <= row, s, jnp.float32(-1e30))
            return s

        def fold(h, s):
            top = jnp.max(s, axis=1, keepdims=True)
            if first:
                new = jnp.broadcast_to(top, (rows, 128))
            else:
                old = peak[h]
                new = jnp.maximum(old, top)
            w = jnp.exp2(s - jnp.concatenate([new] * (rows // 128), axis=1))
            part = w[:, :128]
            for n in range(1, rows // 128):
                part = part + w[:, n * 128 : (n + 1) * 128]
            update = jnp.dot(w.astype(jnp.bfloat16), latent, preferred_element_type=jnp.float32)
            peak[h] = new
            if first:
                total[h] = part
                acc[h] = update
            else:
                shrink = jnp.exp2(old - new)
                total[h] = total[h] * shrink + part
                acc[h] = acc[h] * jnp.concatenate([shrink] * (LAT // 128), axis=1) + update

        s = scores(0)
        for h in range(heads):
            ahead = scores(h + 1) if h + 1 < heads else None
            fold(h, s)
            s = ahead

    attend(i, True)

    @pl.when(yl == 1)
    def _():
        relay_b(0)

    def round_(r, carry):
        @pl.when(r < 7)
        def _():
            relay_a(r + 1)

        @pl.when((r < 7) & (yl == 1))
        def _():
            relay_b(r + 1)

        def side(ab, carry):
            j = (1 - ab) * (yl * NZ) + z_of(r)
            held = ((ab == 0) & (r > 0)) | ((ab == 1) & (yl == 1))

            @pl.when(held)
            def _():
                for k in range(2):
                    kv_arrived(j, 2 * (1 - core) + k)

            @pl.when(held & (j < i))
            def _():
                attend(j, False)

            return carry

        return lax.fori_loop(0, 2, side, carry)

    lax.fori_loop(0, 8, round_, 0)

    def block(e):
        n, dy = rem(e, 4), div(e, 4)
        dx = n + div(n, 2) * (1 - 2 * rem(n, 2))
        return rem(x + dx, NX), rem(yh + dy, 2)

    def v_copy(e, k, send_sem, target):
        xx, yy = block(e)
        slot = outer_of(xx, yy, core)
        piece = vbuf.at[slot, k]
        return pltpu.make_async_remote_copy(
            src_ref=piece, dst_ref=piece, send_sem=send_sem,
            recv_sem=v_recv.at[slot, k], device_id=target, device_id_type=MESH,
        )

    def v_arrived(slot, k):
        piece = vbuf.at[slot, k]
        pltpu.make_async_remote_copy(
            src_ref=piece, dst_ref=piece, send_sem=send_c.at[0],
            recv_sem=v_recv.at[slot, k], device_id=sibling, device_id_type=MESH,
        ).wait_recv()

    def own_slot(e):
        xx, yy = block(e)
        return outer_of(xx, yy, core)

    def sib_slot(e):
        xx, yy = block(e)
        return outer_of(xx, yy, 1 - core)

    locals_[7].wait()

    def send(e, k, way):
        sem = {
            "far": lambda: send_c.at[k], "up": lambda: send_x.at[e, k, 0],
            "down": lambda: send_x.at[e, k, 1], "sib": lambda: sib_v.at[e, k],
        }[way]()
        target = {"far": y_far, "up": x_up, "down": x_down, "sib": sibling}[way]
        return v_copy(e, k, sem, target)

    for h in range(heads):
        whole = jnp.sum(total[h], axis=1, keepdims=True)
        latent_out = (acc[h] * (1.0 / whole)).astype(jnp.bfloat16)
        vbuf[o, h // 2, :, (h % 2) * VDIM : (h % 2 + 1) * VDIM] = jnp.dot(
            latent_out, vu[h], preferred_element_type=jnp.float32
        ).astype(jnp.bfloat16)
        if h % 2 == 1:
            k = h // 2
            send(0, k, "far").start()
            send(0, k, "up").start()
            send(0, k, "down").start()
            send(0, k, "sib").start()

    locals_[8].wait()
    mix[...] = jnp.zeros_like(mix)

    def project(slot):
        for k in range(2):
            depth = heads * VDIM // 2
            start = pl.multiple_of((slot * 2 + k) * depth, depth)
            mix[...] += jnp.dot(
                vbuf[slot, k], wo[pl.ds(start, depth), :], preferred_element_type=jnp.float32
            )

    def relay_v(e):
        def came(e, k):
            v_arrived(own_slot(e), k)
            send(e, k, "sib").start()

        if e == 1:
            came(1, 0)
            came(1, 1)
            send(1, 1, "down").start()
        if e == 2:
            came(2, 0)
            send(2, 0, "up").start()
            came(2, 1)
        if e == 3:
            for k in range(2):
                v_arrived(own_slot(4), k)
                send(4, k, "up").start()
                send(4, k, "down").start()
                send(4, k, "sib").start()
            came(3, 0)
            came(3, 1)
        if e == 5:
            came(5, 0)
            came(5, 1)
            send(5, 1, "down").start()
        if e == 6:
            came(6, 0)
            send(6, 0, "up").start()
            came(6, 1)
        if e == 7:
            came(7, 0)
            came(7, 1)

    def event(e, carry):
        for n in (1, 2, 3, 5, 6, 7):
            @pl.when(e == n)
            def _():
                relay_v(n)

        @pl.when(e > 0)
        def _():
            project(own_slot(e - 1))
            for k in range(2):
                v_arrived(sib_slot(e - 1), k)
            project(sib_slot(e - 1))

        return carry

    lax.fori_loop(0, 9, event, 0)
    out_ref[...] = mix[...].astype(jnp.bfloat16)

    for e in range(8):
        for k in range(2):
            ways = ["sib"]
            if e == 0:
                ways += ["far"]
            if e in (0, 4):
                ways += ["up", "down"]
            if (e, k) in ((2, 0), (6, 0)):
                ways += ["up"]
            if (e, k) in ((1, 1), (5, 1)):
                ways += ["down"]
            for way in ways:
                send(e, k, way).wait_send()
    for k in range(2):
        kv_copy(i, k, send_z.at[0, k], z_up).wait_send()
        kv_copy(i, k, send_z.at[7, k], z_down).wait_send()

    def drain(r, carry):
        for k in range(2):
            @pl.when((r > 0) & z_forwards(r, k))
            def _():
                kv_copy(yl * NZ + z_of(r), k, send_z.at[r, k], z_target(r)).wait_send()

            @pl.when(yl == 0)
            def _():
                kv_copy(yl * NZ + z_of(r), k, send_y.at[r, k], y_target[k]).wait_send()

            @pl.when(r > 0)
            def _():
                kv_copy(yl * NZ + z_of(r), k, sib_a.at[r, k], sibling).wait_send()

            @pl.when(yl == 1)
            def _():
                kv_copy(z_of(r), k, sib_b.at[r, k], sibling).wait_send()

        return carry

    lax.fori_loop(0, 8, drain, 0)


def on_device(q_nope, q_rope, absorb_key, kv_latent, value_up, out_proj):
    rows = q_nope.shape[0]
    heads = absorb_key.shape[0]
    columns = out_proj.shape[1]
    kv_parts = kv_latent.reshape(4, rows // 4, WIDE)
    dma = pltpu.SemaphoreType.DMA
    return pl.pallas_call(
        kernel,
        out_shape=jax.ShapeDtypeStruct((rows, columns), jnp.bfloat16),
        in_specs=[pl.BlockSpec(memory_space=pl.ANY)] * 6,
        out_specs=pl.BlockSpec(memory_space=pltpu.VMEM),
        scratch_shapes=[
            pltpu.VMEM(q_nope.shape, jnp.bfloat16),
            pltpu.VMEM(q_rope.shape, jnp.bfloat16),
            pltpu.VMEM(absorb_key.shape, jnp.bfloat16),
            pltpu.VMEM(value_up.shape, jnp.bfloat16),
            pltpu.VMEM(out_proj.shape, jnp.bfloat16),
            pltpu.VMEM((16, 4, rows // 4, WIDE), jnp.bfloat16),
            pltpu.VMEM((16, 2, rows, heads * VDIM // 2), jnp.bfloat16),
            pltpu.VMEM((heads, rows, WIDE), jnp.bfloat16),
            pltpu.VMEM((heads, rows, 128), jnp.float32),
            pltpu.VMEM((heads, rows, 128), jnp.float32),
            pltpu.VMEM((heads, rows, LAT), jnp.float32),
            pltpu.VMEM((rows, columns), jnp.float32),
            dma((9,)),
            dma((16, 4)),
            dma((8, 2)),
            dma((8, 2)),
            dma((8, 2)),
            dma((8, 2)),
            dma((16, 2)),
            dma((8, 2, 2)),
            dma((2,)),
            dma((8, 2)),
        ],
        compiler_params=pltpu.CompilerParams(
            collective_id=0, has_side_effects=True, vmem_limit_bytes=56 * 1024 * 1024
        ),
        cost_estimate=pl.CostEstimate(
            flops=12 * 10**9, bytes_accessed=10 * 10**6, transcendentals=4 * 10**6
        ),
    )(q_nope, q_rope, absorb_key, kv_parts, value_up, out_proj)


def solution(mesh):
    placed = (
        P("inner", "outer"),
        P("inner", "outer"),
        P("outer", None, None),
        P("inner", None),
        P("outer", None, None),
        P(None, "outer"),
    )
    return jax.shard_map(
        on_device, mesh=mesh, in_specs=placed, out_specs=P("inner", "outer"), check_vma=False
    )
```

time: 191 us -> 76.9 us (0.40)
  waiting for transfers between devices: 135 us -> 0 us
  Pallas kernels: 0 us -> 61.2 us
  matrix products: 27.8 us -> 0 us
  between operations: 14.1 us -> 0.01 us
  local copies, waits for them, and re-layouts: 3.12 us -> 15.2 us
  other arithmetic: 8.56 us -> 0 us
    all_gather x2 -> x0, waiting for transfers between devices: 135 us -> none  [the longest x1 68.7 us: on_device(): shard_piece = lax.all_gather(kv_latent, 'inner', axis=0, tiled=True)]
    pallas_call x0 -> x1, Pallas kernels: none -> 61.2 us  [on_device(): pl.pallas_call(kernel, out_shape=jax.ShapeDtypeStruct((rows, columns), jn...]
    dot_general x5 -> x0, matrix products: 27.8 us -> none  [the longest x1 10.2 us: compute(): jnp.einsum('hqc,kc->hqk', queries, shard_piece, preferred_element_type=jn...]
    unnamed x6 -> x2, local copies, waits for them, and re-layouts: 2.94 us -> 13.5 us
    reduce_sum x1 -> x0, other arithmetic: 5.05 us -> none  [compute(): new_sum = jnp.sum(weights, axis=2)]
  transfers between devices with their start and end apart: 2 -> 0, of which waited for: 2 -> 0; matrix products, arithmetic and copies ran while one was open for 2% -> 0% of each run, Pallas kernels for 0% -> 0%
where the time goes in v1:
time: 76.9 us; the launch traced here: 76.5 us
  Pallas kernels  61.2 us (80%)
  local copies, waits for them, and re-layouts  15.2 us (20%)
    pallas_call x1, Pallas kernels, on_device(): pl.pallas_call(kernel, out_shape=jax.ShapeDtypeStruct((rows, columns), jn...  61.2 us
    unnamed x2, local copies, waits for them, and re-layouts  13.5 us
    pallas_call x1, local copies, waits for them, and re-layouts, on_device(): pl.pallas_call(kernel, out_shape=jax.ShapeDtypeStruct((rows, columns), jn...  1.78 us

profile of v1, /device:TPU:9, one launch (start us, length us, event | category | flops | bytes accessed | tf_op | source)
XLA Modules:
  0.0 76.5 jit_solution(5171726247405511004)
XLA Ops:
  0.0 1.9 %copy.7 = bf16[256,576]{1,0:T(8,128)(2,1)} copy(bf16[256,576]{0,1:T(8,128)(2,1)} %param.9) | data formatting | bytes 589824 | tf_op args[3]
  1.9 11.6 %copy.8.wo_hbm = bf16[8192,448]{1,0:T(8,128)(2,1)} copy(bf16[8192,448]{0,1:T(8,128)(2,1)} %param.11) | data formatting | bytes 14680064 | tf_op args[5]
  13.5 61.2 %shard_map.64 = bf16[256,448]{1,0:T(8,128)(2,1)} custom-call(bf16[256,512]{1,0:T(8,128)(2,1)} %qn_hbm.1, bf16[256,256]{1,0:T(8,128)(2,1)} %qr_hbm.1, bf16[4,128,512]{2,1,0:T(8,128)(2,1)} %ak_hbm.1, bf16[4,64,576]{2,1,0:T(8,128)(2,1)} %bitcast.1, bf16[4,512,128]{2,1,0:T(8,128)(2,1)} %vu_hbm.1, bf16[8192,448]{1,0:T(8,128)(2,1)} %copy.8.wo_hbm), custom_call_target="tpu_custom_call" | custom-call | flops 12000000000 | bytes 10000000 | tf_op jit(solution)/shard_map/pallas_call | solution.py:367
  74.7 1.8 %copy.9 = bf16[256,448]{0,1:T(8,128)(2,1)} copy(bf16[256,448]{1,0:T(8,128)(2,1)} %shard_map.64) | data formatting | bytes 458752 | tf_op jit(solution)/shard_map/pallas_call | solution.py:367

commit v2 on v1

--- a/solution.py
+++ b/solution.py
@@ -132,11 +132,11 @@
         query[h, :, LAT:] = qr[:, h * ROPE : (h + 1) * ROPE]
 
     def attend(j, first):
-        keys = kvbuf[j].reshape(rows, WIDE)
-        latent = keys[:, :LAT]
+        keys = kvbuf[j].reshape(WIDE, rows)
+        latent = keys[:LAT]
 
         def scores(h):
-            s = lax.dot_general(query[h], keys, NT, preferred_element_type=jnp.float32) * SCALE
+            s = jnp.dot(query[h], keys, preferred_element_type=jnp.float32) * SCALE
             if first:
                 row = lax.broadcasted_iota(jnp.int32, s.shape, 0)
                 col = lax.broadcasted_iota(jnp.int32, s.shape, 1)
@@ -154,7 +154,9 @@
             part = w[:, :128]
             for n in range(1, rows // 128):
                 part = part + w[:, n * 128 : (n + 1) * 128]
-            update = jnp.dot(w.astype(jnp.bfloat16), latent, preferred_element_type=jnp.float32)
+            update = lax.dot_general(
+                w.astype(jnp.bfloat16), latent, NT, preferred_element_type=jnp.float32
+            )
             peak[h] = new
             if first:
                 total[h] = part
@@ -181,11 +183,11 @@
         def _():
             relay_a(r + 1)
 
-        @pl.when((r < 7) & (yl == 1))
-        def _():
-            relay_b(r + 1)
-
         def side(ab, carry):
+            @pl.when((ab == 1) & (r < 7) & (yl == 1))
+            def _():
+                relay_b(r + 1)
+
             j = (1 - ab) * (yl * NZ) + z_of(r)
             held = ((ab == 0) & (r > 0)) | ((ab == 1) & (yl == 1))
 
@@ -260,12 +262,14 @@
     mix[...] = jnp.zeros_like(mix)
 
     def project(slot):
+        depth = heads * VDIM // 2
+        term = mix[...]
         for k in range(2):
-            depth = heads * VDIM // 2
             start = pl.multiple_of((slot * 2 + k) * depth, depth)
-            mix[...] += jnp.dot(
-                vbuf[slot, k], wo[pl.ds(start, depth), :], preferred_element_type=jnp.float32
+            term = term + lax.dot_general(
+                wo[:, pl.ds(start, depth)], vbuf[slot, k], NT, preferred_element_type=jnp.float32
             )
+        mix[...] = term
 
     def relay_v(e):
         def came(e, k):
@@ -362,11 +366,12 @@
     rows = q_nope.shape[0]
     heads = absorb_key.shape[0]
     columns = out_proj.shape[1]
-    kv_parts = kv_latent.reshape(4, rows // 4, WIDE)
+    kv_parts = kv_latent.T.reshape(4, WIDE // 4, rows)
+    out_proj = out_proj.T
     dma = pltpu.SemaphoreType.DMA
-    return pl.pallas_call(
+    mixed = pl.pallas_call(
         kernel,
-        out_shape=jax.ShapeDtypeStruct((rows, columns), jnp.bfloat16),
+        out_shape=jax.ShapeDtypeStruct((columns, rows), jnp.bfloat16),
         in_specs=[pl.BlockSpec(memory_space=pl.ANY)] * 6,
         out_specs=pl.BlockSpec(memory_space=pltpu.VMEM),
         scratch_shapes=[
@@ -375,13 +380,13 @@
             pltpu.VMEM(absorb_key.shape, jnp.bfloat16),
             pltpu.VMEM(value_up.shape, jnp.bfloat16),
             pltpu.VMEM(out_proj.shape, jnp.bfloat16),
-            pltpu.VMEM((16, 4, rows // 4, WIDE), jnp.bfloat16),
+            pltpu.VMEM((16, 4, WIDE // 4, rows), jnp.bfloat16),
             pltpu.VMEM((16, 2, rows, heads * VDIM // 2), jnp.bfloat16),
             pltpu.VMEM((heads, rows, WIDE), jnp.bfloat16),
             pltpu.VMEM((heads, rows, 128), jnp.float32),
             pltpu.VMEM((heads, rows, 128), jnp.float32),
             pltpu.VMEM((heads, rows, LAT), jnp.float32),
-            pltpu.VMEM((rows, columns), jnp.float32),
+            pltpu.VMEM((columns, rows), jnp.float32),
             dma((9,)),
             dma((16, 4)),
             dma((8, 2)),
@@ -400,6 +405,7 @@
             flops=12 * 10**9, bytes_accessed=10 * 10**6, transcendentals=4 * 10**6
         ),
     )(q_nope, q_rope, absorb_key, kv_parts, value_up, out_proj)
+    return mixed.T
 
 
 def solution(mesh):

time: 76.9 us -> 62.4 us (0.81)
  local copies, waits for them, and re-layouts: 15.2 us -> 1.64 us
    unnamed x2 -> x1, local copies, waits for them, and re-layouts: 13.5 us -> 1.64 us
    pallas_call x1 -> x0, local copies, waits for them, and re-layouts: 1.78 us -> none  [on_device(): pl.pallas_call(kernel, out_shape=jax.ShapeDtypeStruct((rows, columns), jn...]
where the time goes in v2:
time: 62.4 us; the launch traced here: 62.1 us
  Pallas kernels  60.5 us (97%)
  local copies, waits for them, and re-layouts  1.64 us (3%)
    pallas_call x1, Pallas kernels, on_device(): pl.pallas_call(kernel, out_shape=jax.ShapeDtypeStruct((columns, rows), jn...  60.5 us
    unnamed x1, local copies, waits for them, and re-layouts  1.64 us

profile of v2, /device:TPU:9, one launch (start us, length us, event | category | flops | bytes accessed | tf_op | source)
XLA Modules:
  0.0 62.1 jit_solution(7889248457488927690)
XLA Ops:
  0.0 60.5 %shard_map.64 = bf16[448,256]{1,0:T(8,128)(2,1)} custom-call(bf16[256,512]{1,0:T(8,128)(2,1)} %qn_hbm.1, bf16[256,256]{1,0:T(8,128)(2,1)} %qr_hbm.1, bf16[4,128,512]{2,1,0:T(8,128)(2,1)} %ak_hbm.1, bf16[4,144,256]{2,1,0:T(8,128)(2,1)} %bitcast.7, bf16[4,512,128]{2,1,0:T(8,128)(2,1)} %vu_hbm.1, bf16[448,8192]{1,0:T(8,128)(2,1)} %bitcast.6), custom_call_target="tpu_custom_call" | custom-call | flops 12000000000 | bytes 10000000 | tf_op jit(solution)/shard_map/pallas_call | solution.py:372
  60.5 1.6 %copy.8 = bf16[256,448]{0,1:T(8,128)(2,1)} copy(bf16[256,448]{0,1:T(8,128)(2,1)} %bitcast.5) | data formatting | bytes 458752

commit v3 on v2

--- a/solution.py
+++ b/solution.py
@@ -223,7 +223,7 @@
     def v_arrived(slot, k):
         piece = vbuf.at[slot, k]
         pltpu.make_async_remote_copy(
-            src_ref=piece, dst_ref=piece, send_sem=send_c.at[0],
+            src_ref=piece, dst_ref=piece, send_sem=send_c.at[0, 0],
             recv_sem=v_recv.at[slot, k], device_id=sibling, device_id_type=MESH,
         ).wait_recv()
 
@@ -239,7 +239,7 @@
 
     def send(e, k, way):
         sem = {
-            "far": lambda: send_c.at[k], "up": lambda: send_x.at[e, k, 0],
+            "far": lambda: send_c.at[e, k], "up": lambda: send_x.at[e, k, 0],
             "down": lambda: send_x.at[e, k, 1], "sib": lambda: sib_v.at[e, k],
         }[way]()
         target = {"far": y_far, "up": x_up, "down": x_down, "sib": sibling}[way]
@@ -272,37 +272,29 @@
         mix[...] = term
 
     def relay_v(e):
-        def came(e, k):
+        def came(e, k, *ways):
             v_arrived(own_slot(e), k)
+            for way in ways:
+                send(e, k, way).start()
             send(e, k, "sib").start()
 
         if e == 1:
-            came(1, 0)
-            came(1, 1)
-            send(1, 1, "down").start()
+            came(1, 0, "far")
+            came(1, 1, "down", "far")
         if e == 2:
-            came(2, 0)
-            send(2, 0, "up").start()
+            came(2, 0, "up")
             came(2, 1)
         if e == 3:
-            for k in range(2):
-                v_arrived(own_slot(4), k)
-                send(4, k, "up").start()
-                send(4, k, "down").start()
-                send(4, k, "sib").start()
+            came(4, 0, "up")
+            came(4, 1, "up")
             came(3, 0)
             came(3, 1)
         if e == 5:
-            came(5, 0)
-            came(5, 1)
-            send(5, 1, "down").start()
-        if e == 6:
-            came(6, 0)
-            send(6, 0, "up").start()
-            came(6, 1)
-        if e == 7:
-            came(7, 0)
-            came(7, 1)
+            came(5, 0, "down")
+            came(5, 1, "down")
+        if e >= 6:
+            came(e, 0)
+            came(e, 1)
 
     def event(e, carry):
         for n in (1, 2, 3, 5, 6, 7):
@@ -325,13 +317,11 @@
     for e in range(8):
         for k in range(2):
             ways = ["sib"]
-            if e == 0:
+            if e <= 1:
                 ways += ["far"]
-            if e in (0, 4):
-                ways += ["up", "down"]
-            if (e, k) in ((2, 0), (6, 0)):
+            if e in (0, 4) or (e, k) == (2, 0):
                 ways += ["up"]
-            if (e, k) in ((1, 1), (5, 1)):
+            if e in (0, 5) or (e, k) == (1, 1):
                 ways += ["down"]
             for way in ways:
                 send(e, k, way).wait_send()
@@ -395,7 +385,7 @@
             dma((8, 2)),
             dma((16, 2)),
             dma((8, 2, 2)),
-            dma((2,)),
+            dma((2, 2)),
             dma((8, 2)),
         ],
         compiler_params=pltpu.CompilerParams(

time: 62.4 us -> 62.7 us (level); the launches traced: 62.1 us -> 61.5 us
  Pallas kernels: 60.5 us -> 59.8 us
    pallas_call x1, Pallas kernels: 60.5 us -> 59.8 us  [on_device(): pl.pallas_call(kernel, out_shape=jax.ShapeDtypeStruct((columns, rows), jn...]
where the time goes in v3:
time: 62.7 us; the launch traced here: 61.5 us
  Pallas kernels  59.8 us (95%)
  local copies, waits for them, and re-layouts  1.64 us (3%)
    pallas_call x1, Pallas kernels, on_device(): pl.pallas_call(kernel, out_shape=jax.ShapeDtypeStruct((columns, rows), jn...  59.8 us
    unnamed x1, local copies, waits for them, and re-layouts  1.64 us

profile of v3, /device:TPU:9, one launch (start us, length us, event | category | flops | bytes accessed | tf_op | source)
XLA Modules:
  0.0 61.5 jit_solution(12466445490693914270)
XLA Ops:
  0.0 59.8 %shard_map.64 = bf16[448,256]{1,0:T(8,128)(2,1)} custom-call(bf16[256,512]{1,0:T(8,128)(2,1)} %qn_hbm.1, bf16[256,256]{1,0:T(8,128)(2,1)} %qr_hbm.1, bf16[4,128,512]{2,1,0:T(8,128)(2,1)} %ak_hbm.1, bf16[4,144,256]{2,1,0:T(8,128)(2,1)} %bitcast.7, bf16[4,512,128]{2,1,0:T(8,128)(2,1)} %vu_hbm.1, bf16[448,8192]{1,0:T(8,128)(2,1)} %bitcast.6), custom_call_target="tpu_custom_call" | custom-call | flops 12000000000 | bytes 10000000 | tf_op jit(solution)/shard_map/pallas_call | solution.py:362
  59.8 1.6 %copy.8 = bf16[256,448]{0,1:T(8,128)(2,1)} copy(bf16[256,448]{0,1:T(8,128)(2,1)} %bitcast.5) | data formatting | bytes 458752

commit v4 on v3

--- a/solution.py
+++ b/solution.py
@@ -75,52 +75,74 @@
     def kv_arrived(j, part):
         piece = kvbuf.at[j, part]
         pltpu.make_async_remote_copy(
-            src_ref=piece, dst_ref=piece, send_sem=send_z.at[0, 0],
+            src_ref=piece, dst_ref=piece, send_sem=send_z.at[0, 0, 0],
             recv_sem=kv_recv.at[j, part], device_id=sibling, device_id_type=MESH,
         ).wait_recv()
 
-    def z_of(r):
-        step = div(r + 1, 2) * (1 - 2 * rem(r, 2))
-        return rem(z + step + NZ, NZ)
-
-    y_target = (y_up, y_down)
+    def ring(d, side):
+        return rem(z + (d if side else NZ - d), NZ)
+
+    def z_forwards(d, side, k):
+        return (d <= 2) | ((d == 3) & (k == side))
+
+    def held_a(d, side, k):
+        return (d <= 3) | ((d == 4) & (k == side))
+
+    def held_b(d, side, k):
+        return ((d == 0) & (side == 0)) | ((d >= 1) & (d <= 3)) | ((d == 4) & (k == side))
+
+    def z_send(d, side, k):
+        return kv_copy(yl * NZ + ring(d, side), k, send_z.at[side, d, k], (z_up, z_down)[side])
+
+    def y_send(d, side, k):
+        target = (outer_of(x, rem(yh + k, 2), core), NZ + z)
+        return kv_copy(ring(d, side), k, send_y.at[side, d, k], target)
+
+    def sib_a_send(d, side, k):
+        return kv_copy(yl * NZ + ring(d, side), k, sib_a.at[side, d, k], sibling)
+
+    def sib_b_send(d, side, k):
+        return kv_copy(ring(d, side), k, sib_b.at[side, d, k], sibling)
+
+    def relay_a(d, k):
+        for side in range(2):
+            j = yl * NZ + ring(d, side)
+
+            @pl.when(held_a(d, side, k))
+            def _():
+                kv_arrived(j, 2 * core + k)
+
+                @pl.when(z_forwards(d, side, k))
+                def _():
+                    z_send(d, side, k).start()
+
+                @pl.when(yl == 0)
+                def _():
+                    y_send(d, side, k).start()
+
+                @pl.when(j < i)
+                def _():
+                    sib_a_send(d, side, k).start()
+
+    def relay_b(d, k):
+        for side in range(2):
+            @pl.when(held_b(d, side, k))
+            def _():
+                kv_arrived(ring(d, side), 2 * core + k)
+                sib_b_send(d, side, k).start()
 
     for part in range(4):
         locals_[part].wait()
-    for k in range(2):
-        kv_copy(i, k, send_z.at[0, k], z_up).start()
-        kv_copy(i, k, send_z.at[7, k], z_down).start()
-    for k in range(2):
+
+    def own(k):
+        for side in range(2):
+            z_send(0, side, k).start()
+
         @pl.when(yl == 0)
         def _():
-            kv_copy(i, k, send_y.at[0, k], y_target[k]).start()
-
-    def z_forwards(r, k):
-        return (r <= 4) | (r == 5 + k)
-
-    def z_target(r):
-        return (o, yl * NZ + rem(z + 2 * rem(r, 2) - 1 + NZ, NZ))
-
-    def relay_a(r):
-        j = yl * NZ + z_of(r)
-        for k in range(2):
-            kv_arrived(j, 2 * core + k)
-
-            @pl.when(z_forwards(r, k))
-            def _():
-                kv_copy(j, k, send_z.at[r, k], z_target(r)).start()
-
-            @pl.when(yl == 0)
-            def _():
-                kv_copy(j, k, send_y.at[r, k], y_target[k]).start()
-
-            kv_copy(j, k, sib_a.at[r, k], sibling).start()
-
-    def relay_b(r):
-        j = z_of(r)
-        for k in range(2):
-            kv_arrived(j, 2 * core + k)
-            kv_copy(j, k, sib_b.at[r, k], sibling).start()
+            y_send(0, 0, k).start()
+
+    own(0)
 
     locals_[4].wait()
     locals_[5].wait()
@@ -131,7 +153,7 @@
         ).astype(jnp.bfloat16)
         query[h, :, LAT:] = qr[:, h * ROPE : (h + 1) * ROPE]
 
-    def attend(j, first):
+    def attend(j, first, some):
         keys = kvbuf[j].reshape(WIDE, rows)
         latent = keys[:LAT]
 
@@ -166,45 +188,47 @@
                 total[h] = total[h] * shrink + part
                 acc[h] = acc[h] * jnp.concatenate([shrink] * (LAT // 128), axis=1) + update
 
-        s = scores(0)
-        for h in range(heads):
-            ahead = scores(h + 1) if h + 1 < heads else None
+        s = scores(some[0])
+        for h in some:
+            ahead = scores(h + 1) if h < some[-1] else None
             fold(h, s)
             s = ahead
 
-    attend(i, True)
-
-    @pl.when(yl == 1)
-    def _():
-        relay_b(0)
-
-    def round_(r, carry):
-        @pl.when(r < 7)
+    own(1)
+    attend(i, True, range(heads))
+
+    def swapped(j):
+        for k in range(2):
+            kv_arrived(j, 2 * (1 - core) + k)
+
+    def half_step(n, carry):
+        d, k = div(n, 2) + 1, rem(n, 2)
+
+        @pl.when(d <= 4)
         def _():
-            relay_a(r + 1)
-
-        def side(ab, carry):
-            @pl.when((ab == 1) & (r < 7) & (yl == 1))
-            def _():
-                relay_b(r + 1)
-
-            j = (1 - ab) * (yl * NZ) + z_of(r)
-            held = ((ab == 0) & (r > 0)) | ((ab == 1) & (yl == 1))
-
-            @pl.when(held)
-            def _():
-                for k in range(2):
-                    kv_arrived(j, 2 * (1 - core) + k)
-
-            @pl.when(held & (j < i))
-            def _():
-                attend(j, False)
+            relay_a(d, k)
+
+        def group(ab, carry):
+            @pl.when((ab == 1) & (yl == 1))
+            def _():
+                relay_b(d - 1, k)
+
+            dd = d - 1 - ab
+            j = (1 - ab) * (yl * NZ) + rem(z + dd * (2 * k - 1) + NZ, NZ)
+            in_a = (ab == 0) & (((dd >= 1) & (dd <= 3)) | ((dd == 4) & (k == 0) & (yl == 1)))
+            in_b = (ab == 1) & (yl == 1) & (((dd >= 1) & (dd <= 3)) | ((dd == 0) & (k == 0)))
+
+            @pl.when((in_a | in_b) & (j < i))
+            def _():
+                swapped(j)
+                attend(j, False, range(heads))
 
             return carry
 
-        return lax.fori_loop(0, 2, side, carry)
-
-    lax.fori_loop(0, 8, round_, 0)
+        return lax.fori_loop(0, 2, group, carry)
+
+    lax.fori_loop(0, 10, half_step, 0)
+    last = rem(z + 4, NZ)
 
     def block(e):
         n, dy = rem(e, 4), div(e, 4)
@@ -245,111 +269,96 @@
         target = {"far": y_far, "up": x_up, "down": x_down, "sib": sibling}[way]
         return v_copy(e, k, sem, target)
 
-    for h in range(heads):
-        whole = jnp.sum(total[h], axis=1, keepdims=True)
-        latent_out = (acc[h] * (1.0 / whole)).astype(jnp.bfloat16)
-        vbuf[o, h // 2, :, (h % 2) * VDIM : (h % 2 + 1) * VDIM] = jnp.dot(
-            latent_out, vu[h], preferred_element_type=jnp.float32
-        ).astype(jnp.bfloat16)
-        if h % 2 == 1:
-            k = h // 2
-            send(0, k, "far").start()
-            send(0, k, "up").start()
-            send(0, k, "down").start()
-            send(0, k, "sib").start()
+    for k in range(2):
+        pair = (2 * k, 2 * k + 1)
+
+        @pl.when(last < i)
+        def _():
+            if k == 0:
+                swapped(last)
+            attend(last, False, pair)
+
+        for h in pair:
+            whole = jnp.sum(total[h], axis=1, keepdims=True)
+            latent_out = (acc[h] * (1.0 / whole)).astype(jnp.bfloat16)
+            vbuf[o, k, :, (h % 2) * VDIM : (h % 2 + 1) * VDIM] = jnp.dot(
+                latent_out, vu[h], preferred_element_type=jnp.float32
+            ).astype(jnp.bfloat16)
+        for way in ("up", "down", "far", "sib"):
+            send(0, k, way).start()
 
     locals_[8].wait()
     mix[...] = jnp.zeros_like(mix)
 
-    def project(slot):
+    def project(e):
         depth = heads * VDIM // 2
         term = mix[...]
+        for slot in (own_slot(e), sib_slot(e)):
+            for k in range(2):
+                start = pl.multiple_of((slot * 2 + k) * depth, depth)
+                term = term + lax.dot_general(
+                    wo[:, pl.ds(start, depth)], vbuf[slot, k], NT,
+                    preferred_element_type=jnp.float32,
+                )
+        mix[...] = term
+
+    came = (
+        ((1, 0, "far"), (2, 0, "up"), (4, 0, "up")),
+        ((1, 1, "down", "far"), (2, 1), (4, 1, "up")),
+        ((3, 0), (5, 0, "down"), (3, 1)),
+        ((6, 0), (5, 1, "down")),
+        ((6, 1),),
+        ((7, 0),),
+        ((7, 1),),
+    )
+
+    def event(t, carry):
+        for n, items in enumerate(came):
+            @pl.when(t == n)
+            def _():
+                for e, k, *ways in items:
+                    v_arrived(own_slot(e), k)
+                    for way in (*ways, "sib"):
+                        send(e, k, way).start()
+
         for k in range(2):
-            start = pl.multiple_of((slot * 2 + k) * depth, depth)
-            term = term + lax.dot_general(
-                wo[:, pl.ds(start, depth)], vbuf[slot, k], NT, preferred_element_type=jnp.float32
-            )
-        mix[...] = term
-
-    def relay_v(e):
-        def came(e, k, *ways):
-            v_arrived(own_slot(e), k)
-            for way in ways:
-                send(e, k, way).start()
-            send(e, k, "sib").start()
-
-        if e == 1:
-            came(1, 0, "far")
-            came(1, 1, "down", "far")
-        if e == 2:
-            came(2, 0, "up")
-            came(2, 1)
-        if e == 3:
-            came(4, 0, "up")
-            came(4, 1, "up")
-            came(3, 0)
-            came(3, 1)
-        if e == 5:
-            came(5, 0, "down")
-            came(5, 1, "down")
-        if e >= 6:
-            came(e, 0)
-            came(e, 1)
-
-    def event(e, carry):
-        for n in (1, 2, 3, 5, 6, 7):
-            @pl.when(e == n)
-            def _():
-                relay_v(n)
-
-        @pl.when(e > 0)
-        def _():
-            project(own_slot(e - 1))
-            for k in range(2):
-                v_arrived(sib_slot(e - 1), k)
-            project(sib_slot(e - 1))
-
+            v_arrived(sib_slot(t), k)
+        project(t)
         return carry
 
-    lax.fori_loop(0, 9, event, 0)
+    lax.fori_loop(0, 8, event, 0)
     out_ref[...] = mix[...].astype(jnp.bfloat16)
 
-    for e in range(8):
-        for k in range(2):
-            ways = ["sib"]
-            if e <= 1:
-                ways += ["far"]
-            if e in (0, 4) or (e, k) == (2, 0):
-                ways += ["up"]
-            if e in (0, 5) or (e, k) == (1, 1):
-                ways += ["down"]
-            for way in ways:
+    for k in range(2):
+        for way in ("up", "down", "far", "sib"):
+            send(0, k, way).wait_send()
+    for items in came:
+        for e, k, *ways in items:
+            for way in (*ways, "sib"):
                 send(e, k, way).wait_send()
-    for k in range(2):
-        kv_copy(i, k, send_z.at[0, k], z_up).wait_send()
-        kv_copy(i, k, send_z.at[7, k], z_down).wait_send()
-
-    def drain(r, carry):
-        for k in range(2):
-            @pl.when((r > 0) & z_forwards(r, k))
-            def _():
-                kv_copy(yl * NZ + z_of(r), k, send_z.at[r, k], z_target(r)).wait_send()
-
-            @pl.when(yl == 0)
-            def _():
-                kv_copy(yl * NZ + z_of(r), k, send_y.at[r, k], y_target[k]).wait_send()
-
-            @pl.when(r > 0)
-            def _():
-                kv_copy(yl * NZ + z_of(r), k, sib_a.at[r, k], sibling).wait_send()
-
-            @pl.when(yl == 1)
-            def _():
-                kv_copy(z_of(r), k, sib_b.at[r, k], sibling).wait_send()
+
+    def drain(n, carry):
+        d, k = div(n, 2), rem(n, 2)
+        for side in range(2):
+            @pl.when(z_forwards(d, side, k))
+            def _():
+                z_send(d, side, k).wait_send()
+
+            @pl.when((yl == 0) & held_b(d, side, k))
+            def _():
+                y_send(d, side, k).wait_send()
+
+            @pl.when((d >= 1) & held_a(d, side, k) & (yl * NZ + ring(d, side) < i))
+            def _():
+                sib_a_send(d, side, k).wait_send()
+
+            @pl.when((yl == 1) & held_b(d, side, k))
+            def _():
+                sib_b_send(d, side, k).wait_send()
 
         return carry
 
-    lax.fori_loop(0, 8, drain, 0)
+    lax.fori_loop(0, 10, drain, 0)
 
 
 def on_device(q_nope, q_rope, absorb_key, kv_latent, value_up, out_proj):
@@ -379,10 +388,10 @@
             pltpu.VMEM((columns, rows), jnp.float32),
             dma((9,)),
             dma((16, 4)),
-            dma((8, 2)),
-            dma((8, 2)),
-            dma((8, 2)),
-            dma((8, 2)),
+            dma((2, 4, 2)),
+            dma((2, 5, 2)),
+            dma((2, 5, 2)),
+            dma((2, 5, 2)),
             dma((16, 2)),
             dma((8, 2, 2)),
             dma((2, 2)),

time: 62.7 us -> 56.6 us (0.903); the launches traced: 61.5 us -> 56.5 us
  Pallas kernels: 59.8 us -> 54.8 us
    pallas_call x1, Pallas kernels: 59.8 us -> 54.8 us  [on_device(): pl.pallas_call(kernel, out_shape=jax.ShapeDtypeStruct((columns, rows), jn...]
where the time goes in v4:
time: 56.6 us; the launch traced here: 56.5 us
  Pallas kernels  54.8 us (97%)
  local copies, waits for them, and re-layouts  1.64 us (3%)
    pallas_call x1, Pallas kernels, on_device(): pl.pallas_call(kernel, out_shape=jax.ShapeDtypeStruct((columns, rows), jn...  54.8 us
    unnamed x1, local copies, waits for them, and re-layouts  1.64 us

profile of v4, /device:TPU:9, one launch (start us, length us, event | category | flops | bytes accessed | tf_op | source)
XLA Modules:
  0.0 56.5 jit_solution(618258558694389288)
XLA Ops:
  0.0 54.8 %shard_map.64 = bf16[448,256]{1,0:T(8,128)(2,1)} custom-call(bf16[256,512]{1,0:T(8,128)(2,1)} %qn_hbm.1, bf16[256,256]{1,0:T(8,128)(2,1)} %qr_hbm.1, bf16[4,128,512]{2,1,0:T(8,128)(2,1)} %ak_hbm.1, bf16[4,144,256]{2,1,0:T(8,128)(2,1)} %bitcast.7, bf16[4,512,128]{2,1,0:T(8,128)(2,1)} %vu_hbm.1, bf16[448,8192]{1,0:T(8,128)(2,1)} %bitcast.6), custom_call_target="tpu_custom_call" | custom-call | flops 12000000000 | bytes 10000000 | tf_op jit(solution)/shard_map/pallas_call | solution.py:371
  54.9 1.6 %copy.8 = bf16[256,448]{0,1:T(8,128)(2,1)} copy(bf16[256,448]{0,1:T(8,128)(2,1)} %bitcast.5) | data formatting | bytes 458752

commit v5 on v4

--- a/solution.py
+++ b/solution.py
@@ -29,7 +29,8 @@
 def kernel(
     qn_hbm, qr_hbm, ak_hbm, kv_hbm, vu_hbm, wo_hbm, out_ref,
     qn, qr, ak, vu, wo, kvbuf, vbuf, query, peak, total, acc, mix,
-    local_sem, kv_recv, send_z, send_y, sib_a, sib_b, v_recv, send_x, send_c, sib_v,
+    local_sem, kv_recv, send_z, send_y, sib_a, sib_b, far_z, far_y, far_x, far_sib,
+    v_recv, send_x, send_c, sib_v,
 ):
     heads, rows = query.shape[0], query.shape[1]
     o, i = lax.axis_index("outer"), lax.axis_index("inner")
@@ -47,6 +48,9 @@
     y_far = (outer_of(x, 1 - yh, core), i)
     x_up = (outer_of(rem(x + 1, NX), yh, core), i)
     x_down = (outer_of(rem(x + NX - 1, NX), yh, core), i)
+
+    x_far = (outer_of(rem(x + 2, NX), yh, core), i)
+    far_target = tuple((o, yl * NZ + rem(z + n, NZ)) for n in (3, NZ - 3, 4))
 
     locals_ = [
         pltpu.make_async_copy(kv_hbm.at[part], kvbuf.at[i, part], local_sem.at[part])
@@ -60,17 +64,20 @@
         copy.start()
 
     barrier = pltpu.get_barrier_semaphore()
-    partners = (sibling, z_up, z_down, y_up, y_down, y_far, x_up, x_down)
+    partners = (sibling, z_up, z_down, *far_target, y_up, y_down, y_far, x_up, x_down, x_far)
     for partner in partners:
         pl.semaphore_signal(barrier, inc=1, device_id=partner, device_id_type=MESH)
     pl.semaphore_wait(barrier, len(partners))
 
-    def kv_copy(j, k, send_sem, target):
-        piece = kvbuf.at[j, 2 * core + k]
+    def part_copy(j, part, send_sem, target):
+        piece = kvbuf.at[j, part]
         return pltpu.make_async_remote_copy(
             src_ref=piece, dst_ref=piece, send_sem=send_sem,
-            recv_sem=kv_recv.at[j, 2 * core + k], device_id=target, device_id_type=MESH,
+            recv_sem=kv_recv.at[j, part], device_id=target, device_id_type=MESH,
         )
+
+    def kv_copy(j, k, send_sem, target):
+        return part_copy(j, 2 * core + k, send_sem, target)
 
     def kv_arrived(j, part):
         piece = kvbuf.at[j, part]
@@ -82,14 +89,8 @@
     def ring(d, side):
         return rem(z + (d if side else NZ - d), NZ)
 
-    def z_forwards(d, side, k):
-        return (d <= 2) | ((d == 3) & (k == side))
-
-    def held_a(d, side, k):
-        return (d <= 3) | ((d == 4) & (k == side))
-
-    def held_b(d, side, k):
-        return ((d == 0) & (side == 0)) | ((d >= 1) & (d <= 3)) | ((d == 4) & (k == side))
+    def held_b(d, side):
+        return (d <= 2) & ((d >= 1) | (side == 0))
 
     def z_send(d, side, k):
         return kv_copy(yl * NZ + ring(d, side), k, send_z.at[side, d, k], (z_up, z_down)[side])
@@ -107,29 +108,77 @@
     def relay_a(d, k):
         for side in range(2):
             j = yl * NZ + ring(d, side)
-
-            @pl.when(held_a(d, side, k))
-            def _():
-                kv_arrived(j, 2 * core + k)
-
-                @pl.when(z_forwards(d, side, k))
-                def _():
-                    z_send(d, side, k).start()
-
-                @pl.when(yl == 0)
-                def _():
-                    y_send(d, side, k).start()
+            kv_arrived(j, 2 * core + k)
+
+            @pl.when(d == 1)
+            def _():
+                z_send(d, side, k).start()
+
+            @pl.when(yl == 0)
+            def _():
+                y_send(d, side, k).start()
+
+            @pl.when(j < i)
+            def _():
+                sib_a_send(d, side, k).start()
+
+    def relay_b(d, k):
+        for side in range(2):
+            @pl.when(held_b(d, side))
+            def _():
+                kv_arrived(ring(d, side), 2 * core + k)
+                sib_b_send(d, side, k).start()
+
+    far_hops = ((3, 0), (3, 1), (4, 0))
+    far_core = (1, 0, rem(z, 2))
+
+    def far_shard(f, group):
+        return group * NZ + ring(*far_hops[f])
+
+    def far_z_send(f):
+        return part_copy(i, x, far_z.at[f], far_target[f])
+
+    def far_y_send(f):
+        way = (0, 1, rem(x, 2))[f]
+        target = (outer_of(x, rem(yh + way, 2), core), NZ + z)
+        return part_copy(far_shard(f, 0), x, far_y.at[f], target)
+
+    def far_x_sends(f, group, ab):
+        return [
+            part_copy(far_shard(f, group), x, far_x.at[ab, f, n], target)
+            for n, target in enumerate((x_up, x_down, x_far))
+        ]
+
+    def far_sib_send(f, group, ab, n):
+        return part_copy(far_shard(f, group), rem(x + n, NX), far_sib.at[ab, f, n], sibling)
+
+    def far_first(group, ab):
+        for f in range(3):
+            j = far_shard(f, group)
+
+            @pl.when(core == far_core[f])
+            def _():
+                kv_arrived(j, x)
+                if ab == 0:
+                    @pl.when(yl == 0)
+                    def _():
+                        far_y_send(f).start()
 
                 @pl.when(j < i)
                 def _():
-                    sib_a_send(d, side, k).start()
-
-    def relay_b(d, k):
-        for side in range(2):
-            @pl.when(held_b(d, side, k))
-            def _():
-                kv_arrived(ring(d, side), 2 * core + k)
-                sib_b_send(d, side, k).start()
+                    for copy in far_x_sends(f, group, ab):
+                        copy.start()
+                    far_sib_send(f, group, ab, 0).start()
+
+    def far_rest(group, ab):
+        for f in range(3):
+            j = far_shard(f, group)
+
+            @pl.when((core == far_core[f]) & (j < i))
+            def _():
+                for n in range(1, NX):
+                    kv_arrived(j, rem(x + n, NX))
+                    far_sib_send(f, group, ab, n).start()
 
     for part in range(4):
         locals_[part].wait()
@@ -143,6 +192,10 @@
             y_send(0, 0, k).start()
 
     own(0)
+    for f in range(3):
+        @pl.when(core == far_core[f])
+        def _():
+            far_z_send(f).start()
 
     locals_[4].wait()
     locals_[5].wait()
@@ -197,21 +250,44 @@
     own(1)
     attend(i, True, range(heads))
 
-    def swapped(j):
-        for k in range(2):
-            kv_arrived(j, 2 * (1 - core) + k)
+    def swapped(j, far, owner):
+        @pl.when(jnp.logical_not(far))
+        def _():
+            for k in range(2):
+                kv_arrived(j, 2 * (1 - core) + k)
+
+        @pl.when(far & (core != owner))
+        def _():
+            for part in range(4):
+                kv_arrived(j, part)
 
     def half_step(n, carry):
         d, k = div(n, 2) + 1, rem(n, 2)
 
-        @pl.when(d <= 4)
+        @pl.when(d <= 2)
         def _():
             relay_a(d, k)
+
+        @pl.when(n == 1)
+        def _():
+            far_first(yl, 0)
+
+        @pl.when(n == 4)
+        def _():
+            far_rest(yl, 0)
 
         def group(ab, carry):
             @pl.when((ab == 1) & (yl == 1))
             def _():
                 relay_b(d - 1, k)
+
+                @pl.when(n == 4)
+                def _():
+                    far_first(0, 1)
+
+                @pl.when(n == 6)
+                def _():
+                    far_rest(0, 1)
 
             dd = d - 1 - ab
             j = (1 - ab) * (yl * NZ) + rem(z + dd * (2 * k - 1) + NZ, NZ)
@@ -220,7 +296,7 @@
 
             @pl.when((in_a | in_b) & (j < i))
             def _():
-                swapped(j)
+                swapped(j, dd >= 3, jnp.where(dd == 3, 1 - k, far_core[2]))
                 attend(j, False, range(heads))
 
             return carry
@@ -275,7 +351,7 @@
         @pl.when(last < i)
         def _():
             if k == 0:
-                swapped(last)
+                swapped(last, last >= 0, far_core[2])
             attend(last, False, pair)
 
         for h in pair:
@@ -340,25 +416,48 @@
     def drain(n, carry):
         d, k = div(n, 2), rem(n, 2)
         for side in range(2):
-            @pl.when(z_forwards(d, side, k))
+            @pl.when(d <= 1)
             def _():
                 z_send(d, side, k).wait_send()
 
-            @pl.when((yl == 0) & held_b(d, side, k))
+            @pl.when((yl == 0) & held_b(d, side))
             def _():
                 y_send(d, side, k).wait_send()
 
-            @pl.when((d >= 1) & held_a(d, side, k) & (yl * NZ + ring(d, side) < i))
+            @pl.when((d >= 1) & (yl * NZ + ring(d, side) < i))
             def _():
                 sib_a_send(d, side, k).wait_send()
 
-            @pl.when((yl == 1) & held_b(d, side, k))
+            @pl.when((yl == 1) & held_b(d, side))
             def _():
                 sib_b_send(d, side, k).wait_send()
 
         return carry
 
-    lax.fori_loop(0, 10, drain, 0)
+    lax.fori_loop(0, 6, drain, 0)
+
+    for f in range(3):
+        @pl.when(core == far_core[f])
+        def _():
+            far_z_send(f).wait_send()
+
+            @pl.when(yl == 0)
+            def _():
+                far_y_send(f).wait_send()
+
+            @pl.when(far_shard(f, yl) < i)
+            def _():
+                for copy in far_x_sends(f, yl, 0):
+                    copy.wait_send()
+                for n in range(NX):
+                    far_sib_send(f, yl, 0, n).wait_send()
+
+            @pl.when(yl == 1)
+            def _():
+                for copy in far_x_sends(f, 0, 1):
+                    copy.wait_send()
+                for n in range(NX):
+                    far_sib_send(f, 0, 1, n).wait_send()
 
 
 def on_device(q_nope, q_rope, absorb_key, kv_latent, value_up, out_proj):
@@ -388,10 +487,14 @@
             pltpu.VMEM((columns, rows), jnp.float32),
             dma((9,)),
             dma((16, 4)),
-            dma((2, 4, 2)),
-            dma((2, 5, 2)),
-            dma((2, 5, 2)),
-            dma((2, 5, 2)),
+            dma((2, 2, 2)),
+            dma((2, 3, 2)),
+            dma((2, 3, 2)),
+            dma((2, 3, 2)),
+            dma((3,)),
+            dma((3,)),
+            dma((2, 3, 3)),
+            dma((2, 3, 4)),
             dma((16, 2)),
             dma((8, 2, 2)),
             dma((2, 2)),

time: 56.6 us -> 61.5 us (1.087); the launches traced: 56.5 us -> 60.7 us
  Pallas kernels: 54.8 us -> 59.1 us
    pallas_call x1, Pallas kernels: 54.8 us -> 59.1 us  [on_device(): pl.pallas_call(kernel, out_shape=jax.ShapeDtypeStruct((columns, rows), jn...]
where the time goes in v5:
time: 61.5 us; the launch traced here: 60.7 us
  Pallas kernels  59.1 us (96%)
  local copies, waits for them, and re-layouts  1.64 us (3%)
    pallas_call x1, Pallas kernels, on_device(): pl.pallas_call(kernel, out_shape=jax.ShapeDtypeStruct((columns, rows), jn...  59.1 us
    unnamed x1, local copies, waits for them, and re-layouts  1.64 us

profile of v5, /device:TPU:9, one launch (start us, length us, event | category | flops | bytes accessed | tf_op | source)
XLA Modules:
  0.0 60.7 jit_solution(12346638743155773612)
XLA Ops:
  0.0 59.1 %shard_map.64 = bf16[448,256]{1,0:T(8,128)(2,1)} custom-call(bf16[256,512]{1,0:T(8,128)(2,1)} %qn_hbm.1, bf16[256,256]{1,0:T(8,128)(2,1)} %qr_hbm.1, bf16[4,128,512]{2,1,0:T(8,128)(2,1)} %ak_hbm.1, bf16[4,144,256]{2,1,0:T(8,128)(2,1)} %bitcast.7, bf16[4,512,128]{2,1,0:T(8,128)(2,1)} %vu_hbm.1, bf16[448,8192]{1,0:T(8,128)(2,1)} %bitcast.6), custom_call_target="tpu_custom_call" | custom-call | flops 12000000000 | bytes 10000000 | tf_op jit(solution)/shard_map/pallas_call | solution.py:470
  59.1 1.6 %copy.8 = bf16[256,448]{0,1:T(8,128)(2,1)} copy(bf16[256,448]{0,1:T(8,128)(2,1)} %bitcast.5) | data formatting | bytes 458752

commit v6 on v4

--- a/solution.py
+++ b/solution.py
@@ -303,11 +303,12 @@
         mix[...] = term
 
     came = (
-        ((1, 0, "far"), (2, 0, "up"), (4, 0, "up")),
-        ((1, 1, "down", "far"), (2, 1), (4, 1, "up")),
-        ((3, 0), (5, 0, "down"), (3, 1)),
-        ((6, 0), (5, 1, "down")),
-        ((6, 1),),
+        ((1, 0), (2, 0, "up")),
+        ((1, 1, "down"), (2, 1)),
+        ((4, 0, "up", "down"), (3, 0), (3, 1)),
+        ((4, 1, "up", "down"),),
+        ((5, 0), (6, 0, "up")),
+        ((5, 1, "down"), (6, 1)),
         ((7, 0),),
         ((7, 1),),
     )

time: 56.6 us -> 60.4 us (1.067)
  Pallas kernels: 54.8 us -> 58.7 us
    pallas_call x1, Pallas kernels: 54.8 us -> 58.7 us  [on_device(): pl.pallas_call(kernel, out_shape=jax.ShapeDtypeStruct((columns, rows), jn...]
where the time goes in v6:
time: 60.4 us; the launch traced here: 60.3 us
  Pallas kernels  58.7 us (97%)
  local copies, waits for them, and re-layouts  1.64 us (3%)
    pallas_call x1, Pallas kernels, on_device(): pl.pallas_call(kernel, out_shape=jax.ShapeDtypeStruct((columns, rows), jn...  58.7 us
    unnamed x1, local copies, waits for them, and re-layouts  1.64 us

profile of v6, /device:TPU:9, one launch (start us, length us, event | category | flops | bytes accessed | tf_op | source)
XLA Modules:
  0.0 60.3 jit_solution(8099077958125433912)
XLA Ops:
  0.0 58.7 %shard_map.64 = bf16[448,256]{1,0:T(8,128)(2,1)} custom-call(bf16[256,512]{1,0:T(8,128)(2,1)} %qn_hbm.1, bf16[256,256]{1,0:T(8,128)(2,1)} %qr_hbm.1, bf16[4,128,512]{2,1,0:T(8,128)(2,1)} %ak_hbm.1, bf16[4,144,256]{2,1,0:T(8,128)(2,1)} %bitcast.7, bf16[4,512,128]{2,1,0:T(8,128)(2,1)} %vu_hbm.1, bf16[448,8192]{1,0:T(8,128)(2,1)} %bitcast.6), custom_call_target="tpu_custom_call" | custom-call | flops 12000000000 | bytes 10000000 | tf_op jit(solution)/shard_map/pallas_call | solution.py:372
  58.7 1.6 %copy.8 = bf16[256,448]{0,1:T(8,128)(2,1)} copy(bf16[256,448]{0,1:T(8,128)(2,1)} %bitcast.5) | data formatting | bytes 458752

commit v7 on v4

--- a/solution.py
+++ b/solution.py
@@ -31,7 +31,7 @@
     qn, qr, ak, vu, wo, kvbuf, vbuf, query, peak, total, acc, mix,
     local_sem, kv_recv, send_z, send_y, sib_a, sib_b, v_recv, send_x, send_c, sib_v,
 ):
-    heads, rows = query.shape[0], query.shape[1]
+    heads, rows = ak.shape[0], qn.shape[0]
     o, i = lax.axis_index("outer"), lax.axis_index("inner")
     core, yh, x = rem(o, 2), rem(div(o, 2), 2), div(o, 4)
     yl, z = div(i, NZ), rem(i, NZ)
@@ -148,54 +148,52 @@
     locals_[5].wait()
     locals_[6].wait()
     for h in range(heads):
-        query[h, :, :LAT] = jnp.dot(
+        query[h * rows : (h + 1) * rows, :LAT] = jnp.dot(
             qn[:, h * NOPE : (h + 1) * NOPE], ak[h], preferred_element_type=jnp.float32
         ).astype(jnp.bfloat16)
-        query[h, :, LAT:] = qr[:, h * ROPE : (h + 1) * ROPE]
-
-    def attend(j, first, some):
+        query[h * rows : (h + 1) * rows, LAT:] = qr[:, h * ROPE : (h + 1) * ROPE]
+
+    def attend(j, first, pairs):
         keys = kvbuf[j].reshape(WIDE, rows)
-        latent = keys[:LAT]
-
-        def scores(h):
-            s = jnp.dot(query[h], keys, preferred_element_type=jnp.float32) * SCALE
+        latent = keys[:LAT].T
+
+        def scores(pair):
+            own_rows = query[pair * 2 * rows : (pair + 1) * 2 * rows]
+            s = jnp.dot(own_rows, keys, preferred_element_type=jnp.float32) * SCALE
             if first:
-                row = lax.broadcasted_iota(jnp.int32, s.shape, 0)
+                row = rem(lax.broadcasted_iota(jnp.int32, s.shape, 0), rows)
                 col = lax.broadcasted_iota(jnp.int32, s.shape, 1)
                 s = jnp.where(col <= row, s, jnp.float32(-1e30))
             return s
 
-        def fold(h, s):
+        def fold(pair, s):
+            at = slice(pair * 2 * rows, (pair + 1) * 2 * rows)
             top = jnp.max(s, axis=1, keepdims=True)
             if first:
-                new = jnp.broadcast_to(top, (rows, 128))
+                new = jnp.broadcast_to(top, (2 * rows, 128))
             else:
-                old = peak[h]
+                old = peak[at]
                 new = jnp.maximum(old, top)
             w = jnp.exp2(s - jnp.concatenate([new] * (rows // 128), axis=1))
             part = w[:, :128]
             for n in range(1, rows // 128):
                 part = part + w[:, n * 128 : (n + 1) * 128]
-            update = lax.dot_general(
-                w.astype(jnp.bfloat16), latent, NT, preferred_element_type=jnp.float32
-            )
-            peak[h] = new
+            update = jnp.dot(w.astype(jnp.bfloat16), latent, preferred_element_type=jnp.float32)
+            peak[at] = new
             if first:
-                total[h] = part
-                acc[h] = update
+                total[at] = part
+                acc[at] = update
             else:
                 shrink = jnp.exp2(old - new)
-                total[h] = total[h] * shrink + part
-                acc[h] = acc[h] * jnp.concatenate([shrink] * (LAT // 128), axis=1) + update
-
-        s = scores(some[0])
-        for h in some:
-            ahead = scores(h + 1) if h < some[-1] else None
-            fold(h, s)
-            s = ahead
+                total[at] = total[at] * shrink + part
+                acc[at] = acc[at] * jnp.concatenate([shrink] * (LAT // 128), axis=1) + update
+
+        s = [scores(pair) for pair in pairs]
+        for pair, pair_scores in zip(pairs, s):
+            fold(pair, pair_scores)
 
     own(1)
-    attend(i, True, range(heads))
+    attend(i, True, (0, 1))
 
     def swapped(j):
         for k in range(2):
@@ -221,7 +219,7 @@
             @pl.when((in_a | in_b) & (j < i))
             def _():
                 swapped(j)
-                attend(j, False, range(heads))
+                attend(j, False, (0, 1))
 
             return carry
 
@@ -276,18 +274,18 @@
         def _():
             if k == 0:
                 swapped(last)
-            attend(last, False, pair)
+            attend(last, False, (k,))
 
         for h in pair:
-            whole = jnp.sum(total[h], axis=1, keepdims=True)
-            latent_out = (acc[h] * (1.0 / whole)).astype(jnp.bfloat16)
+            at = slice(h * rows, (h + 1) * rows)
+            whole = jnp.sum(total[at], axis=1, keepdims=True)
+            latent_out = (acc[at] * (1.0 / whole)).astype(jnp.bfloat16)
             vbuf[o, k, :, (h % 2) * VDIM : (h % 2 + 1) * VDIM] = jnp.dot(
                 latent_out, vu[h], preferred_element_type=jnp.float32
             ).astype(jnp.bfloat16)
         for way in ("up", "down", "far", "sib"):
             send(0, k, way).start()
 
-    locals_[8].wait()
     mix[...] = jnp.zeros_like(mix)
 
     def project(e):
@@ -320,6 +318,10 @@
                     v_arrived(own_slot(e), k)
                     for way in (*ways, "sib"):
                         send(e, k, way).start()
+
+        @pl.when(t == 0)
+        def _():
+            locals_[8].wait()
 
         for k in range(2):
             v_arrived(sib_slot(t), k)
@@ -381,10 +383,10 @@
             pltpu.VMEM(out_proj.shape, jnp.bfloat16),
             pltpu.VMEM((16, 4, WIDE // 4, rows), jnp.bfloat16),
             pltpu.VMEM((16, 2, rows, heads * VDIM // 2), jnp.bfloat16),
-            pltpu.VMEM((heads, rows, WIDE), jnp.bfloat16),
-            pltpu.VMEM((heads, rows, 128), jnp.float32),
-            pltpu.VMEM((heads, rows, 128), jnp.float32),
-            pltpu.VMEM((heads, rows, LAT), jnp.float32),
+            pltpu.VMEM((heads * rows, WIDE), jnp.bfloat16),
+            pltpu.VMEM((heads * rows, 128), jnp.float32),
+            pltpu.VMEM((heads * rows, 128), jnp.float32),
+            pltpu.VMEM((heads * rows, LAT), jnp.float32),
             pltpu.VMEM((columns, rows), jnp.float32),
             dma((9,)),
             dma((16, 4)),

time: 56.6 us -> 56.6 us (level)
  no operation moved by 1% of the time
where the time goes in v7:
time: 56.6 us; the launch traced here: 56.5 us
  Pallas kernels  54.8 us (97%)
  local copies, waits for them, and re-layouts  1.64 us (3%)
    pallas_call x1, Pallas kernels, on_device(): pl.pallas_call(kernel, out_shape=jax.ShapeDtypeStruct((columns, rows), jn...  54.8 us
    unnamed x1, local copies, waits for them, and re-layouts  1.64 us

profile of v7, /device:TPU:9, one launch (start us, length us, event | category | flops | bytes accessed | tf_op | source)
XLA Modules:
  0.0 56.5 jit_solution(8170950729806486215)
XLA Ops:
  0.0 54.8 %shard_map.64 = bf16[448,256]{1,0:T(8,128)(2,1)} custom-call(bf16[256,512]{1,0:T(8,128)(2,1)} %qn_hbm.1, bf16[256,256]{1,0:T(8,128)(2,1)} %qr_hbm.1, bf16[4,128,512]{2,1,0:T(8,128)(2,1)} %ak_hbm.1, bf16[4,144,256]{2,1,0:T(8,128)(2,1)} %bitcast.7, bf16[4,512,128]{2,1,0:T(8,128)(2,1)} %vu_hbm.1, bf16[448,8192]{1,0:T(8,128)(2,1)} %bitcast.6), custom_call_target="tpu_custom_call" | custom-call | flops 12000000000 | bytes 10000000 | tf_op jit(solution)/shard_map/pallas_call | solution.py:373
  54.8 1.6 %copy.8 = bf16[256,448]{0,1:T(8,128)(2,1)} copy(bf16[256,448]{0,1:T(8,128)(2,1)} %bitcast.5) | data formatting | bytes 458752

commit v8 on v7

v8 whole, which is shorter than its diff:
```python
import math

import jax
import jax.numpy as jnp
from jax import lax
from jax.experimental import pallas as pl
from jax.experimental.pallas import tpu as pltpu
from jax.sharding import PartitionSpec as P

NOPE = 128
ROPE = 64
VDIM = 128
LAT = 512
WIDE = LAT + ROPE
MESH = pl.DeviceIdType.MESH
NT = (((1,), (1,)), ((), ()))
SCALE = math.log2(math.e) / math.sqrt(NOPE + ROPE)
NX, NZ = 4, 8


def div(a, b):
    return a // b if isinstance(a, int) else lax.div(a, b)


def rem(a, b):
    return a % b if isinstance(a, int) else lax.rem(a, b)


def kernel(
    qn_hbm, qr_hbm, ak_hbm, kv_hbm, vu_hbm, wo_hbm, out_ref,
    qn, qr, ak, vu, wo, kvbuf, vbuf, query, peak, total, acc, mix, out_away, out_here,
    local_sem, q_sem, kv_recv, send_z, send_y, sib_a, sib_b, v_recv, send_x, send_c, sib_v, out_sem,
):
    heads, rows = ak.shape[0], qn.shape[1]
    span = 2 * rows
    o, i = lax.axis_index("outer"), lax.axis_index("inner")
    core, yh, x = rem(o, 2), rem(div(o, 2), 2), div(o, 4)
    yl, z = div(i, NZ), rem(i, NZ)

    def outer_of(x_, yh_, core_):
        return (x_ * 2 + yh_) * 2 + core_

    sibling = (outer_of(x, yh, 1 - core), i)
    z_up = (o, yl * NZ + rem(z + 1, NZ))
    z_down = (o, yl * NZ + rem(z + NZ - 1, NZ))
    y_up = (outer_of(x, rem(yh + yl, 2), core), (1 - yl) * NZ + z)
    y_down = (outer_of(x, rem(yh + 1 - yl, 2), core), (1 - yl) * NZ + z)
    y_far = (outer_of(x, 1 - yh, core), i)
    x_up = (outer_of(rem(x + 1, NX), yh, core), i)
    x_down = (outer_of(rem(x + NX - 1, NX), yh, core), i)
    partner = (o, (1 - yl) * NZ + z)

    locals_ = [
        pltpu.make_async_copy(src, dst, local_sem.at[n])
        for n, (src, dst) in enumerate(
            [
                (kv_hbm, kvbuf.at[i]), (qn_hbm.at[yl], qn.at[yl]), (qr_hbm.at[yl], qr.at[yl]),
                (ak_hbm, ak), (vu_hbm, vu), (wo_hbm, wo),
            ]
        )
    ]
    for copy in locals_:
        copy.start()
    peak[...] = jnp.full_like(peak, -1e30)
    total[...] = jnp.zeros_like(total)
    acc[...] = jnp.zeros_like(acc)
    mix[...] = jnp.zeros_like(mix)

    barrier = pltpu.get_barrier_semaphore()
    others = (sibling, z_up, z_down, y_up, y_down, y_far, x_up, x_down)
    for other in others:
        pl.semaphore_signal(barrier, inc=1, device_id=other, device_id_type=MESH)
    pl.semaphore_wait(barrier, len(others))

    def remote(src, dst, send_sem, recv_sem, target):
        return pltpu.make_async_remote_copy(
            src_ref=src, dst_ref=dst, send_sem=send_sem, recv_sem=recv_sem,
            device_id=target, device_id_type=MESH,
        )

    q_swap = [
        remote(src.at[1 - yl], dst.at[yl], q_sem.at[n, 0], q_sem.at[n, 1], partner)
        for n, (src, dst) in enumerate([(qn_hbm, qn), (qr_hbm, qr)])
    ]

    def kv_copy(j, k, send_sem, target):
        piece = kvbuf.at[j, 2 * core + k]
        return remote(piece, piece, send_sem, kv_recv.at[j, 2 * core + k], target)

    def kv_arrived(j, part):
        piece = kvbuf.at[j, part]
        remote(piece, piece, send_z.at[0, 0, 0], kv_recv.at[j, part], sibling).wait_recv()

    def ring(d, side):
        return rem(z + (d if side else NZ - d), NZ)

    def z_forwards(d, side, k):
        return (d <= 2) | ((d == 3) & (k == side))

    def held_a(d, side, k):
        return (d <= 3) | ((d == 4) & (k == side))

    def held_b(d, side, k):
        return ((d == 0) & (side == 0)) | ((d >= 1) & (d <= 3)) | ((d == 4) & (k == side))

    def need_a(zz):
        return (yl == 0) | (zz <= z)

    def need_b(zz):
        return (yl == 1) | (zz <= z)

    def z_send(d, side, k):
        return kv_copy(yl * NZ + ring(d, side), k, send_z.at[side, d, k], (z_up, z_down)[side])

    def y_send(d, side, k):
        yh_there = rem(yh + yl + k * (1 - 2 * yl) + 2, 2)
        target = (outer_of(x, yh_there, core), (1 - yl) * NZ + z)
        return kv_copy(yl * NZ + ring(d, side), k, send_y.at[side, d, k], target)

    def sib_a_send(d, side, k):
        return kv_copy(yl * NZ + ring(d, side), k, sib_a.at[side, d, k], sibling)

    def sib_b_send(d, side, k):
        return kv_copy((1 - yl) * NZ + ring(d, side), k, sib_b.at[side, d, k], sibling)

    def relay_a(d, k):
        for side in range(2):
            zz = ring(d, side)

            @pl.when(held_a(d, side, k))
            def _():
                kv_arrived(yl * NZ + zz, 2 * core + k)

                @pl.when(z_forwards(d, side, k))
                def _():
                    z_send(d, side, k).start()

                @pl.when(need_a(zz))
                def _():
                    y_send(d, side, k).start()
                    sib_a_send(d, side, k).start()

    def relay_b(d, k):
        for side in range(2):
            zz = ring(d, side)

            @pl.when(held_b(d, side, k) & need_b(zz))
            def _():
                kv_arrived((1 - yl) * NZ + zz, 2 * core + k)
                sib_b_send(d, side, k).start()

    def own(k):
        for side in range(2):
            z_send(0, side, k).start()
        y_send(0, 0, k).start()

    locals_[0].wait()
    own(0)
    for copy in q_swap:
        copy.start()

    def absorb(g):
        for h in range(heads):
            query[g, h * rows : (h + 1) * rows, :LAT] = jnp.dot(
                qn[g, :, h * NOPE : (h + 1) * NOPE], ak[h], preferred_element_type=jnp.float32
            ).astype(jnp.bfloat16)
            query[g, h * rows : (h + 1) * rows, LAT:] = qr[g, :, h * ROPE : (h + 1) * ROPE]

    def attend(j, g, masked):
        keys = kvbuf[j].reshape(WIDE, span)
        latent = keys[:LAT].T
        half = heads // 2 * rows

        def scores(pair):
            own_rows = query[g, pair * half : (pair + 1) * half]
            s = jnp.dot(own_rows, keys, preferred_element_type=jnp.float32) * SCALE
            if masked:
                row = rem(lax.broadcasted_iota(jnp.int32, s.shape, 0), rows) + yl * rows
                col = lax.broadcasted_iota(jnp.int32, s.shape, 1)
                s = jnp.where(col <= row, s, jnp.float32(-1e30))
            return s

        def fold(pair, s):
            at = slice(pair * half, (pair + 1) * half)
            old = peak[g, at]
            new = jnp.maximum(old, jnp.max(s, axis=1, keepdims=True))
            shrink = jnp.exp2(old - new)
            w = jnp.exp2(s - jnp.concatenate([new] * (span // 128), axis=1))
            part = w[:, :128]
            for n in range(1, span // 128):
                part = part + w[:, n * 128 : (n + 1) * 128]
            update = jnp.dot(w.astype(jnp.bfloat16), latent, preferred_element_type=jnp.float32)
            peak[g, at] = new
            total[g, at] = total[g, at] * shrink + part
            acc[g, at] = acc[g, at] * jnp.concatenate([shrink] * (LAT // 128), axis=1) + update

        s = [scores(0), scores(1)]
        for pair in range(2):
            fold(pair, s[pair])

    locals_[1].wait()
    locals_[2].wait()
    locals_[3].wait()
    absorb(yl)
    own(1)
    locals_[4].wait()

    def block(e):
        n, dy = rem(e, 4), div(e, 4)
        dx = n + div(n, 2) * (1 - 2 * rem(n, 2))
        return rem(x + dx, NX), rem(yh + dy, 2)

    def own_slot(e):
        xx, yy = block(e)
        return outer_of(xx, yy, core)

    def sib_slot(e):
        xx, yy = block(e)
        return outer_of(xx, yy, 1 - core)

    def v_arrived(slot, g):
        piece = vbuf.at[slot, g]
        remote(piece, piece, send_c.at[0, 0], v_recv.at[slot, g], sibling).wait_recv()

    def send(e, g, way):
        sem = {
            "far": lambda: send_c.at[e, g], "up": lambda: send_x.at[e, g, 0],
            "down": lambda: send_x.at[e, g, 1], "sib": lambda: sib_v.at[e, g],
        }[way]()
        target = {"far": y_far, "up": x_up, "down": x_down, "sib": sibling}[way]
        slot = own_slot(e)
        piece = vbuf.at[slot, g]
        return remote(piece, piece, sem, v_recv.at[slot, g], target)

    came = (((1, "far"), (2,), (4, "up")), ((3,), (5, "down"), (6,)), ((7,),))

    def relay_v(g, items):
        for e, *ways in items:
            v_arrived(own_slot(e), g)
            if e == 1:
                @pl.when(core == 1)
                def _():
                    send(1, g, "down").start()
            if e == 2:
                @pl.when(core == 0)
                def _():
                    send(2, g, "up").start()
            for way in (*ways, "sib"):
                send(e, g, way).start()

    def finish(g):
        for h in range(heads):
            at = slice(h * rows, (h + 1) * rows)
            whole = jnp.sum(total[g, at], axis=1, keepdims=True)
            latent_out = (acc[g, at] * (1.0 / whole)).astype(jnp.bfloat16)
            vbuf[o, g, :, h * VDIM : (h + 1) * VDIM] = jnp.dot(
                latent_out, vu[h], preferred_element_type=jnp.float32
            ).astype(jnp.bfloat16)
        for way in ("up", "down", "far", "sib"):
            send(0, g, way).start()

    def project(g, e):
        depth = heads * VDIM
        term = mix[g]
        for slot in (own_slot(e), sib_slot(e)):
            start = pl.multiple_of(slot * depth, depth)
            term = term + lax.dot_general(
                wo[:, pl.ds(start, depth)], vbuf[slot, g], NT, preferred_element_type=jnp.float32
            )
        mix[g] = term

    out_swap = remote(out_away, out_here, out_sem.at[0], out_sem.at[1], partner)

    def deliver(g):
        @pl.when(g == yl)
        def _():
            out_ref[:, pl.ds(pl.multiple_of(yl * rows, rows), rows)] = mix[g].astype(jnp.bfloat16)

        @pl.when(g != yl)
        def _():
            out_away[...] = mix[g].astype(jnp.bfloat16)
            out_swap.start()

    far_hop = jnp.minimum(z, 4)
    early_step, late_step = 2 * far_hop + 2 * yl, 10

    def step_of(g):
        return (1 - g) * early_step + g * late_step

    def values_step(g, n):
        since = n - step_of(g)
        for stage, items in enumerate(came):
            @pl.when(since == 2 + 2 * stage)
            def _():
                relay_v(g, items)

    def project_step(g, n):
        since = n - step_of(g)
        stage = div(since - 3 + 16, 2) - 8
        active = (since >= 3) & (since <= 7) & (rem(since + 16, 2) == 1)

        @pl.when(active)
        def _():
            def one(e, carry):
                v_arrived(sib_slot(e), g)
                project(g, e)
                return carry

            first = 3 * jnp.minimum(stage, 1) + 4 * (stage - jnp.minimum(stage, 1))
            count = 3 + jnp.minimum(stage, 1) - 3 * (stage - jnp.minimum(stage, 1))
            lax.fori_loop(first, first + count, one, 0)

        @pl.when(since == 8)
        def _():
            deliver(g)

    def step(n, carry):
        d, k = div(n, 2) + 1, rem(n, 2)

        @pl.when(d <= 4)
        def _():
            relay_a(d, k)

        def values_of(g, carry):
            values_step(g, n)
            return carry

        lax.fori_loop(0, 2, values_of, 0)

        @pl.when(n == 2)
        def _():
            for copy in q_swap:
                copy.wait_recv()
            absorb(1 - yl)
            locals_[5].wait()

        def source(ab, carry):
            dd = d - 1 - rem(ab, 2)
            key_group = yl + rem(ab, 2) * (1 - 2 * yl)
            zz = rem(z + dd * (2 * k - 1) + NZ, NZ)
            zz = jnp.where(ab == 2, z, zz)
            j = key_group * NZ + zz
            middle = (dd >= 1) & (dd <= 3)
            in_a = (ab == 0) & (middle | ((dd == 4) & (k == 0)))
            in_b = (ab == 1) & (middle | (((dd == 0) | (dd == 4)) & (k == 0)))
            in_own = (ab == 2) & (n == 2)

            @pl.when((in_a & need_a(zz)) | (in_b & need_b(zz)))
            def _():
                for part in range(2):
                    kv_arrived(j, 2 * (1 - core) + part)

            @pl.when((ab <= 1) & (dd == 0) & (k == 0))
            def _():
                attend(j, key_group, True)

            def group(g, carry):
                below = (key_group == 0) & (g == 1)

                @pl.when((in_a | in_b | in_own) & (below | ((zz < z) & (g >= key_group))))
                def _():
                    attend(j, g, False)

                @pl.when((n == step_of(g)) & (ab == jnp.maximum(g, yl)))
                def _():
                    finish(g)

                return carry

            lax.fori_loop(0, 2, group, 0)

            @pl.when((ab == 1) & (d <= 5))
            def _():
                relay_b(d - 1, k)

            return carry

        lax.fori_loop(0, 3, source, 0)

        def project_of(g, carry):
            project_step(g, n)
            return carry

        lax.fori_loop(0, 2, project_of, 0)
        return carry

    lax.fori_loop(0, late_step + 9, step, 0)

    out_swap.wait_recv()
    out_ref[:, pl.ds(pl.multiple_of((1 - yl) * rows, rows), rows)] = out_here[...]

    out_swap.wait_send()
    for copy in q_swap:
        copy.wait_send()

    def drain_v(g, carry):
        for way in ("up", "down", "far", "sib"):
            send(0, g, way).wait_send()
        for items in came:
            for e, *ways in items:
                if e == 1:
                    @pl.when(core == 1)
                    def _():
                        send(1, g, "down").wait_send()
                if e == 2:
                    @pl.when(core == 0)
                    def _():
                        send(2, g, "up").wait_send()
                for way in (*ways, "sib"):
                    send(e, g, way).wait_send()
        return carry

    lax.fori_loop(0, 2, drain_v, 0)

    def drain(n, carry):
        d, k = div(n, 2), rem(n, 2)
        for side in range(2):
            zz = ring(d, side)

            @pl.when(z_forwards(d, side, k))
            def _():
                z_send(d, side, k).wait_send()

            @pl.when(held_b(d, side, k) & need_a(zz))
            def _():
                y_send(d, side, k).wait_send()

            @pl.when((d >= 1) & held_a(d, side, k) & need_a(zz))
            def _():
                sib_a_send(d, side, k).wait_send()

            @pl.when(held_b(d, side, k) & need_b(zz))
            def _():
                sib_b_send(d, side, k).wait_send()

        return carry

    lax.fori_loop(0, 10, drain, 0)


def on_device(q_nope, q_rope, absorb_key, kv_latent, value_up, out_proj):
    rows = q_nope.shape[0]
    half = rows // 2
    heads = absorb_key.shape[0]
    columns = out_proj.shape[1]
    kv_parts = kv_latent.T.reshape(4, WIDE // 4, rows)
    out_proj = out_proj.T
    q_nope = q_nope.reshape(2, half, heads * NOPE)
    q_rope = q_rope.reshape(2, half, heads * ROPE)
    dma = pltpu.SemaphoreType.DMA
    bf16, f32 = jnp.bfloat16, jnp.float32
    mixed = pl.pallas_call(
        kernel,
        out_shape=jax.ShapeDtypeStruct((columns, rows), bf16),
        in_specs=[pl.BlockSpec(memory_space=pl.ANY)] * 6,
        out_specs=pl.BlockSpec(memory_space=pltpu.VMEM),
        scratch_shapes=[
            pltpu.VMEM(q_nope.shape, bf16),
            pltpu.VMEM(q_rope.shape, bf16),
            pltpu.VMEM(absorb_key.shape, bf16),
            pltpu.VMEM(value_up.shape, bf16),
            pltpu.VMEM(out_proj.shape, bf16),
            pltpu.VMEM((16, 4, WIDE // 4, rows), bf16),
            pltpu.VMEM((16, 2, half, heads * VDIM), bf16),
            pltpu.VMEM((2, heads * half, WIDE), bf16),
            pltpu.VMEM((2, heads * half, 128), f32),
            pltpu.VMEM((2, heads * half, 128), f32),
            pltpu.VMEM((2, heads * half, LAT), f32),
            pltpu.VMEM((2, columns, half), f32),
            pltpu.VMEM((columns, half), bf16),
            pltpu.VMEM((columns, half), bf16),
            dma((6,)),
            dma((2, 2)),
            dma((16, 4)),
            dma((2, 4, 2)),
            dma((2, 5, 2)),
            dma((2, 5, 2)),
            dma((2, 5, 2)),
            dma((16, 2)),
            dma((8, 2, 2)),
            dma((2, 2)),
            dma((8, 2)),
            dma((2,)),
        ],
        compiler_params=pltpu.CompilerParams(
            collective_id=0, has_side_effects=True, vmem_limit_bytes=56 * 1024 * 1024
        ),
        cost_estimate=pl.CostEstimate(
            flops=12 * 10**9, bytes_accessed=10 * 10**6, transcendentals=4 * 10**6
        ),
    )(q_nope, q_rope, absorb_key, kv_parts, value_up, out_proj)
    return mixed.T


def solution(mesh):
    placed = (
        P("inner", "outer"),
        P("inner", "outer"),
        P("outer", None, None),
        P("inner", None),
        P("outer", None, None),
        P(None, "outer"),
    )
    return jax.shard_map(
        on_device, mesh=mesh, in_specs=placed, out_specs=P("inner", "outer"), check_vma=False
    )
```

time: 56.6 us -> 68.1 us (1.20)
  the two profiles are of different devices: /device:TPU:9 before, /device:TPU:240 now
where the time goes in v8:
time: 68.1 us; the launch traced here: 68 us
  Pallas kernels  66.3 us (97%)
  local copies, waits for them, and re-layouts  1.64 us (2%)
    pallas_call x1, Pallas kernels, on_device(): pl.pallas_call(kernel, out_shape=jax.ShapeDtypeStruct((columns, rows), bf...  66.3 us
    unnamed x1, local copies, waits for them, and re-layouts  1.64 us

profile of v8, /device:TPU:240, one launch (start us, length us, event | category | flops | bytes accessed | tf_op | source)
XLA Modules:
  0.0 68.0 jit_solution(16205995835766949703)
XLA Ops:
  0.0 66.3 %shard_map.64 = bf16[448,256]{1,0:T(8,128)(2,1)} custom-call(bf16[2,128,512]{2,1,0:T(8,128)(2,1)} %bitcast.10, bf16[2,128,256]{2,1,0:T(8,128)(2,1)} %bitcast.11, bf16[4,128,512]{2,1,0:T(8,128)(2,1)} %ak_hbm.1, bf16[4,144,256]{2,1,0:T(8,128)(2,1)} %bitcast.9, bf16[4,512,128]{2,1,0:T(8,128)(2,1)} %vu_hbm.1, bf16[448,8192]{1,0:T(8,128)(2,1)} %bitcast.8), custom_call_target="tpu_custom_call" | custom-call | flops 12000000000 | bytes 10000000 | tf_op jit(solution)/shard_map/pallas_call | solution.py:452
  66.3 1.6 %copy.8 = bf16[256,448]{0,1:T(8,128)(2,1)} copy(bf16[256,448]{0,1:T(8,128)(2,1)} %bitcast.7) | data formatting | bytes 458752

commit v9 on v7

--- a/solution.py
+++ b/solution.py
@@ -13,7 +13,6 @@
 LAT = 512
 WIDE = LAT + ROPE
 MESH = pl.DeviceIdType.MESH
-NT = (((1,), (1,)), ((), ()))
 SCALE = math.log2(math.e) / math.sqrt(NOPE + ROPE)
 NX, NZ = 4, 8
 
@@ -147,46 +146,51 @@
     locals_[4].wait()
     locals_[5].wait()
     locals_[6].wait()
+    qr_across = qr[...].T
     for h in range(heads):
-        query[h * rows : (h + 1) * rows, :LAT] = jnp.dot(
+        at = slice(h * rows, (h + 1) * rows)
+        query[:LAT, at] = jnp.dot(
             qn[:, h * NOPE : (h + 1) * NOPE], ak[h], preferred_element_type=jnp.float32
-        ).astype(jnp.bfloat16)
-        query[h * rows : (h + 1) * rows, LAT:] = qr[:, h * ROPE : (h + 1) * ROPE]
+        ).astype(jnp.bfloat16).T
+        query[LAT:, at] = qr_across[h * ROPE : (h + 1) * ROPE]
 
     def attend(j, first, pairs):
-        keys = kvbuf[j].reshape(WIDE, rows)
-        latent = keys[:LAT].T
+        latent = kvbuf[j].reshape(WIDE, rows)
+        keys = latent.T
+        width = 2 * rows
 
         def scores(pair):
-            own_rows = query[pair * 2 * rows : (pair + 1) * 2 * rows]
-            s = jnp.dot(own_rows, keys, preferred_element_type=jnp.float32) * SCALE
+            at = slice(pair * width, (pair + 1) * width)
+            s = jnp.dot(keys, query[:, at], preferred_element_type=jnp.float32) * SCALE
             if first:
-                row = rem(lax.broadcasted_iota(jnp.int32, s.shape, 0), rows)
-                col = lax.broadcasted_iota(jnp.int32, s.shape, 1)
-                s = jnp.where(col <= row, s, jnp.float32(-1e30))
-            return s
+                key = lax.broadcasted_iota(jnp.int32, s.shape, 0)
+                row = rem(lax.broadcasted_iota(jnp.int32, s.shape, 1), rows)
+                s = jnp.where(key <= row, s, jnp.float32(-1e30))
+            return s.reshape(rows // 8, 8, width)
 
         def fold(pair, s):
-            at = slice(pair * 2 * rows, (pair + 1) * 2 * rows)
-            top = jnp.max(s, axis=1, keepdims=True)
+            at = slice(pair * width, (pair + 1) * width)
+            top = jnp.max(jnp.max(s, axis=0), axis=0, keepdims=True)
             if first:
-                new = jnp.broadcast_to(top, (2 * rows, 128))
+                new = jnp.broadcast_to(top, (8, width))
             else:
-                old = peak[at]
+                old = peak[:, at]
                 new = jnp.maximum(old, top)
-            w = jnp.exp2(s - jnp.concatenate([new] * (rows // 128), axis=1))
-            part = w[:, :128]
-            for n in range(1, rows // 128):
-                part = part + w[:, n * 128 : (n + 1) * 128]
-            update = jnp.dot(w.astype(jnp.bfloat16), latent, preferred_element_type=jnp.float32)
-            peak[at] = new
+            w = jnp.exp2(s - new[None])
+            part = jnp.sum(w, axis=0)
+            update = jnp.dot(
+                latent[:LAT], w.reshape(rows, width).astype(jnp.bfloat16),
+                preferred_element_type=jnp.float32,
+            )
+            peak[:, at] = new
             if first:
-                total[at] = part
-                acc[at] = update
+                total[:, at] = part
+                acc[:, at] = update
             else:
                 shrink = jnp.exp2(old - new)
-                total[at] = total[at] * shrink + part
-                acc[at] = acc[at] * jnp.concatenate([shrink] * (LAT // 128), axis=1) + update
+                total[:, at] = total[:, at] * shrink + part
+                grown = acc[:, at].reshape(LAT // 8, 8, width) * shrink[None]
+                acc[:, at] = grown.reshape(LAT, width) + update
 
         s = [scores(pair) for pair in pairs]
         for pair, pair_scores in zip(pairs, s):
@@ -278,10 +282,10 @@
 
         for h in pair:
             at = slice(h * rows, (h + 1) * rows)
-            whole = jnp.sum(total[at], axis=1, keepdims=True)
-            latent_out = (acc[at] * (1.0 / whole)).astype(jnp.bfloat16)
-            vbuf[o, k, :, (h % 2) * VDIM : (h % 2 + 1) * VDIM] = jnp.dot(
-                latent_out, vu[h], preferred_element_type=jnp.float32
+            whole = jnp.sum(total[:, at], axis=0, keepdims=True)
+            latent_out = (acc[:, at] * (1.0 / whole)).astype(jnp.bfloat16)
+            vbuf[o, k, (h % 2) * VDIM : (h % 2 + 1) * VDIM, :] = jnp.dot(
+                vu[h].T, latent_out, preferred_element_type=jnp.float32
             ).astype(jnp.bfloat16)
         for way in ("up", "down", "far", "sib"):
             send(0, k, way).start()
@@ -289,15 +293,14 @@
     mix[...] = jnp.zeros_like(mix)
 
     def project(e):
-        depth = heads * VDIM // 2
+        depth = heads * VDIM
         term = mix[...]
         for slot in (own_slot(e), sib_slot(e)):
-            for k in range(2):
-                start = pl.multiple_of((slot * 2 + k) * depth, depth)
-                term = term + lax.dot_general(
-                    wo[:, pl.ds(start, depth)], vbuf[slot, k], NT,
-                    preferred_element_type=jnp.float32,
-                )
+            start = pl.multiple_of(slot * depth, depth)
+            term = term + jnp.dot(
+                wo[:, pl.ds(start, depth)], vbuf[slot].reshape(depth, rows),
+                preferred_element_type=jnp.float32,
+            )
         mix[...] = term
 
     came = (
@@ -382,11 +385,11 @@
             pltpu.VMEM(value_up.shape, jnp.bfloat16),
             pltpu.VMEM(out_proj.shape, jnp.bfloat16),
             pltpu.VMEM((16, 4, WIDE // 4, rows), jnp.bfloat16),
-            pltpu.VMEM((16, 2, rows, heads * VDIM // 2), jnp.bfloat16),
-            pltpu.VMEM((heads * rows, WIDE), jnp.bfloat16),
-            pltpu.VMEM((heads * rows, 128), jnp.float32),
-            pltpu.VMEM((heads * rows, 128), jnp.float32),
-            pltpu.VMEM((heads * rows, LAT), jnp.float32),
+            pltpu.VMEM((16, 2, heads * VDIM // 2, rows), jnp.bfloat16),
+            pltpu.VMEM((WIDE, heads * rows), jnp.bfloat16),
+            pltpu.VMEM((8, heads * rows), jnp.float32),
+            pltpu.VMEM((8, heads * rows), jnp.float32),
+            pltpu.VMEM((LAT, heads * rows), jnp.float32),
             pltpu.VMEM((columns, rows), jnp.float32),
             dma((9,)),
             dma((16, 4)),

time: 56.6 us -> 56.3 us (level)
  no operation moved by 1% of the time
where the time goes in v9:
time: 56.3 us; the launch traced here: 56.2 us
  Pallas kernels  54.5 us (97%)
  local copies, waits for them, and re-layouts  1.64 us (3%)
    pallas_call x1, Pallas kernels, on_device(): pl.pallas_call(kernel, out_shape=jax.ShapeDtypeStruct((columns, rows), jn...  54.5 us
    unnamed x1, local copies, waits for them, and re-layouts  1.64 us

profile of v9, /device:TPU:9, one launch (start us, length us, event | category | flops | bytes accessed | tf_op | source)
XLA Modules:
  0.0 56.2 jit_solution(928233275648551697)
XLA Ops:
  0.0 54.5 %shard_map.64 = bf16[448,256]{1,0:T(8,128)(2,1)} custom-call(bf16[256,512]{1,0:T(8,128)(2,1)} %qn_hbm.1, bf16[256,256]{1,0:T(8,128)(2,1)} %qr_hbm.1, bf16[4,128,512]{2,1,0:T(8,128)(2,1)} %ak_hbm.1, bf16[4,144,256]{2,1,0:T(8,128)(2,1)} %bitcast.7, bf16[4,512,128]{2,1,0:T(8,128)(2,1)} %vu_hbm.1, bf16[448,8192]{1,0:T(8,128)(2,1)} %bitcast.6), custom_call_target="tpu_custom_call" | custom-call | flops 12000000000 | bytes 10000000 | tf_op jit(solution)/shard_map/pallas_call | solution.py:376
  54.6 1.6 %copy.8 = bf16[256,448]{0,1:T(8,128)(2,1)} copy(bf16[256,448]{0,1:T(8,128)(2,1)} %bitcast.5) | data formatting | bytes 458752

commit v10 on v9

--- a/solution.py
+++ b/solution.py
@@ -38,14 +38,17 @@
     def outer_of(x_, yh_, core_):
         return (x_ * 2 + yh_) * 2 + core_
 
+    def wrap(n, size):
+        return jnp.where(n >= size, n - size, n)
+
     sibling = (outer_of(x, yh, 1 - core), i)
-    z_up = (o, yl * NZ + rem(z + 1, NZ))
-    z_down = (o, yl * NZ + rem(z + NZ - 1, NZ))
-    y_up = (outer_of(x, rem(yh + yl, 2), core), (1 - yl) * NZ + z)
-    y_down = (outer_of(x, rem(yh + 1 - yl, 2), core), (1 - yl) * NZ + z)
+    z_up = (o, yl * NZ + wrap(z + 1, NZ))
+    z_down = (o, yl * NZ + wrap(z + NZ - 1, NZ))
+    y_up = (outer_of(x, wrap(yh + yl, 2), core), (1 - yl) * NZ + z)
+    y_down = (outer_of(x, wrap(yh + 1 - yl, 2), core), (1 - yl) * NZ + z)
     y_far = (outer_of(x, 1 - yh, core), i)
-    x_up = (outer_of(rem(x + 1, NX), yh, core), i)
-    x_down = (outer_of(rem(x + NX - 1, NX), yh, core), i)
+    x_up = (outer_of(wrap(x + 1, NX), yh, core), i)
+    x_down = (outer_of(wrap(x + NX - 1, NX), yh, core), i)
 
     locals_ = [
         pltpu.make_async_copy(kv_hbm.at[part], kvbuf.at[i, part], local_sem.at[part])
@@ -64,11 +67,13 @@
         pl.semaphore_signal(barrier, inc=1, device_id=partner, device_id_type=MESH)
     pl.semaphore_wait(barrier, len(partners))
 
+    mine, others = 2 * core, 2 * (1 - core)
+
     def kv_copy(j, k, send_sem, target):
-        piece = kvbuf.at[j, 2 * core + k]
+        piece = kvbuf.at[j, mine + k]
         return pltpu.make_async_remote_copy(
             src_ref=piece, dst_ref=piece, send_sem=send_sem,
-            recv_sem=kv_recv.at[j, 2 * core + k], device_id=target, device_id_type=MESH,
+            recv_sem=kv_recv.at[j, mine + k], device_id=target, device_id_type=MESH,
         )
 
     def kv_arrived(j, part):
@@ -79,7 +84,7 @@
         ).wait_recv()
 
     def ring(d, side):
-        return rem(z + (d if side else NZ - d), NZ)
+        return wrap(z + (d if side else NZ - d), NZ)
 
     def z_forwards(d, side, k):
         return (d <= 2) | ((d == 3) & (k == side))
@@ -88,58 +93,66 @@
         return (d <= 3) | ((d == 4) & (k == side))
 
     def held_b(d, side, k):
-        return ((d == 0) & (side == 0)) | ((d >= 1) & (d <= 3)) | ((d == 4) & (k == side))
-
-    def z_send(d, side, k):
-        return kv_copy(yl * NZ + ring(d, side), k, send_z.at[side, d, k], (z_up, z_down)[side])
-
-    def y_send(d, side, k):
-        target = (outer_of(x, rem(yh + k, 2), core), NZ + z)
-        return kv_copy(ring(d, side), k, send_y.at[side, d, k], target)
-
-    def sib_a_send(d, side, k):
-        return kv_copy(yl * NZ + ring(d, side), k, sib_a.at[side, d, k], sibling)
-
-    def sib_b_send(d, side, k):
-        return kv_copy(ring(d, side), k, sib_b.at[side, d, k], sibling)
+        return (d <= 3) | ((d == 4) & (k == side))
+
+    first_a = yl * NZ
+
+    def z_send(j, d, side, k):
+        return kv_copy(j, k, send_z.at[side, d, k], (z_up, z_down)[side])
+
+    o_far = outer_of(x, 1 - yh, core)
+
+    def y_send(j, d, side, k):
+        return kv_copy(j, k, send_y.at[side, d, k], (jnp.where(k == 0, o, o_far), NZ + z))
+
+    def sib_a_send(j, d, side, k):
+        return kv_copy(j, k, sib_a.at[side, d, k], sibling)
+
+    def sib_b_send(j, d, side, k):
+        return kv_copy(j, k, sib_b.at[side, d, k], sibling)
 
     def relay_a(d, k):
         for side in range(2):
-            j = yl * NZ + ring(d, side)
-
             @pl.when(held_a(d, side, k))
             def _():
-                kv_arrived(j, 2 * core + k)
+                j = first_a + ring(d, side)
+                kv_arrived(j, mine + k)
 
                 @pl.when(z_forwards(d, side, k))
                 def _():
-                    z_send(d, side, k).start()
+                    z_send(j, d, side, k).start()
 
                 @pl.when(yl == 0)
                 def _():
-                    y_send(d, side, k).start()
+                    y_send(j, d, side, k).start()
 
                 @pl.when(j < i)
                 def _():
-                    sib_a_send(d, side, k).start()
+                    sib_a_send(j, d, side, k).start()
 
     def relay_b(d, k):
+        @pl.when(d == 0)
+        def _():
+            kv_arrived(z, mine + k)
+            sib_b_send(z, 0, 0, k).start()
+
         for side in range(2):
-            @pl.when(held_b(d, side, k))
+            @pl.when((d >= 1) & held_b(d, side, k))
             def _():
-                kv_arrived(ring(d, side), 2 * core + k)
-                sib_b_send(d, side, k).start()
+                j = ring(d, side)
+                kv_arrived(j, mine + k)
+                sib_b_send(j, d, side, k).start()
 
     for part in range(4):
         locals_[part].wait()
 
     def own(k):
         for side in range(2):
-            z_send(0, side, k).start()
+            z_send(i, 0, side, k).start()
 
         @pl.when(yl == 0)
         def _():
-            y_send(0, 0, k).start()
+            y_send(i, 0, 0, k).start()
 
     own(0)
 
@@ -164,8 +177,8 @@
             s = jnp.dot(keys, query[:, at], preferred_element_type=jnp.float32) * SCALE
             if first:
                 key = lax.broadcasted_iota(jnp.int32, s.shape, 0)
-                row = rem(lax.broadcasted_iota(jnp.int32, s.shape, 1), rows)
-                s = jnp.where(key <= row, s, jnp.float32(-1e30))
+                row = lax.broadcasted_iota(jnp.int32, s.shape, 1)
+                s = jnp.where(key <= jnp.where(row >= rows, row - rows, row), s, jnp.float32(-1e30))
             return s.reshape(rows // 8, 8, width)
 
         def fold(pair, s):
@@ -201,50 +214,44 @@
 
     def swapped(j):
         for k in range(2):
-            kv_arrived(j, 2 * (1 - core) + k)
-
-    def half_step(n, carry):
-        d, k = div(n, 2) + 1, rem(n, 2)
-
-        @pl.when(d <= 4)
-        def _():
-            relay_a(d, k)
-
-        def group(ab, carry):
-            @pl.when((ab == 1) & (yl == 1))
+            kv_arrived(j, others + k)
+
+    def hop(d, carry):
+        def half_step(k, carry):
+            @pl.when(d <= 4)
             def _():
-                relay_b(d - 1, k)
-
-            dd = d - 1 - ab
-            j = (1 - ab) * (yl * NZ) + rem(z + dd * (2 * k - 1) + NZ, NZ)
-            in_a = (ab == 0) & (((dd >= 1) & (dd <= 3)) | ((dd == 4) & (k == 0) & (yl == 1)))
-            in_b = (ab == 1) & (yl == 1) & (((dd >= 1) & (dd <= 3)) | ((dd == 0) & (k == 0)))
-
-            @pl.when((in_a | in_b) & (j < i))
-            def _():
-                swapped(j)
-                attend(j, False, (0, 1))
-
-            return carry
-
-        return lax.fori_loop(0, 2, group, carry)
-
-    lax.fori_loop(0, 10, half_step, 0)
-    last = rem(z + 4, NZ)
-
-    def block(e):
-        n, dy = rem(e, 4), div(e, 4)
-        dx = n + div(n, 2) * (1 - 2 * rem(n, 2))
-        return rem(x + dx, NX), rem(yh + dy, 2)
-
-    def v_copy(e, k, send_sem, target):
-        xx, yy = block(e)
-        slot = outer_of(xx, yy, core)
-        piece = vbuf.at[slot, k]
-        return pltpu.make_async_remote_copy(
-            src_ref=piece, dst_ref=piece, send_sem=send_sem,
-            recv_sem=v_recv.at[slot, k], device_id=target, device_id_type=MESH,
-        )
+                relay_a(d, k)
+
+            def group(ab, carry):
+                @pl.when((ab == 1) & (yl == 1))
+                def _():
+                    relay_b(d - 1, k)
+
+                dd = d - 1 - ab
+                j = jnp.where(ab == 0, first_a, 0) + wrap(jnp.where(k == 0, z + NZ - dd, z + dd), NZ)
+                in_a = (ab == 0) & (((dd >= 1) & (dd <= 3)) | ((dd == 4) & (k == 0) & (yl == 1)))
+                in_b = (ab == 1) & (yl == 1) & (((dd >= 1) & (dd <= 3)) | ((dd == 0) & (k == 0)))
+
+                @pl.when((in_a | in_b) & (j < i))
+                def _():
+                    swapped(j)
+                    attend(j, False, (0, 1))
+
+                return carry
+
+            return lax.fori_loop(0, 2, group, carry)
+
+        return lax.fori_loop(0, 2, half_step, carry)
+
+    lax.fori_loop(1, 6, hop, 0)
+    last = wrap(z + 4, NZ)
+
+    own_slots, sib_slots = [], []
+    for there in (yh, 1 - yh):
+        for dx in (0, 1, 3, 2):
+            place = outer_of(wrap(x + dx, NX), there, 0)
+            own_slots.append(place + core)
+            sib_slots.append(place + 1 - core)
 
     def v_arrived(slot, k):
         piece = vbuf.at[slot, k]
@@ -253,14 +260,6 @@
             recv_sem=v_recv.at[slot, k], device_id=sibling, device_id_type=MESH,
         ).wait_recv()
 
-    def own_slot(e):
-        xx, yy = block(e)
-        return outer_of(xx, yy, core)
-
-    def sib_slot(e):
-        xx, yy = block(e)
-        return outer_of(xx, yy, 1 - core)
-
     locals_[7].wait()
 
     def send(e, k, way):
@@ -269,7 +268,11 @@
             "down": lambda: send_x.at[e, k, 1], "sib": lambda: sib_v.at[e, k],
         }[way]()
         target = {"far": y_far, "up": x_up, "down": x_down, "sib": sibling}[way]
-        return v_copy(e, k, sem, target)
+        piece = vbuf.at[own_slots[e], k]
+        return pltpu.make_async_remote_copy(
+            src_ref=piece, dst_ref=piece, send_sem=sem,
+            recv_sem=v_recv.at[own_slots[e], k], device_id=target, device_id_type=MESH,
+        )
 
     for k in range(2):
         pair = (2 * k, 2 * k + 1)
@@ -292,10 +295,10 @@
 
     mix[...] = jnp.zeros_like(mix)
 
-    def project(e):
+    def project(slots):
         depth = heads * VDIM
         term = mix[...]
-        for slot in (own_slot(e), sib_slot(e)):
+        for slot in slots:
             start = pl.multiple_of(slot * depth, depth)
             term = term + jnp.dot(
                 wo[:, pl.ds(start, depth)], vbuf[slot].reshape(depth, rows),
@@ -318,7 +321,7 @@
             @pl.when(t == n)
             def _():
                 for e, k, *ways in items:
-                    v_arrived(own_slot(e), k)
+                    v_arrived(own_slots[e], k)
                     for way in (*ways, "sib"):
                         send(e, k, way).start()
 
@@ -326,9 +329,12 @@
         def _():
             locals_[8].wait()
 
+        n = jnp.where(t >= 4, t - 4, t)
+        dx = jnp.where(n == 2, 3, jnp.where(n == 3, 2, n))
+        place = outer_of(wrap(x + dx, NX), jnp.where(t >= 4, 1 - yh, yh), 0)
         for k in range(2):
-            v_arrived(sib_slot(t), k)
-        project(t)
+            v_arrived(place + 1 - core, k)
+        project((place + core, place + 1 - core))
         return carry
 
     lax.fori_loop(0, 8, event, 0)
@@ -342,28 +348,45 @@
             for way in (*ways, "sib"):
                 send(e, k, way).wait_send()
 
-    def drain(n, carry):
-        d, k = div(n, 2), rem(n, 2)
+    for k in range(2):
         for side in range(2):
-            @pl.when(z_forwards(d, side, k))
-            def _():
-                z_send(d, side, k).wait_send()
-
-            @pl.when((yl == 0) & held_b(d, side, k))
-            def _():
-                y_send(d, side, k).wait_send()
-
-            @pl.when((d >= 1) & held_a(d, side, k) & (yl * NZ + ring(d, side) < i))
-            def _():
-                sib_a_send(d, side, k).wait_send()
-
-            @pl.when((yl == 1) & held_b(d, side, k))
-            def _():
-                sib_b_send(d, side, k).wait_send()
+            z_send(i, 0, side, k).wait_send()
+
+        @pl.when(yl == 0)
+        def _():
+            y_send(i, 0, 0, k).wait_send()
+
+        @pl.when(yl == 1)
+        def _():
+            sib_b_send(z, 0, 0, k).wait_send()
+
+    def drain(d, carry):
+        for k in range(2):
+            for side in range(2):
+                @pl.when(held_a(d, side, k))
+                def _():
+                    zz = ring(d, side)
+                    j = first_a + zz
+
+                    @pl.when(z_forwards(d, side, k))
+                    def _():
+                        z_send(j, d, side, k).wait_send()
+
+                    @pl.when(yl == 0)
+                    def _():
+                        y_send(j, d, side, k).wait_send()
+
+                    @pl.when(j < i)
+                    def _():
+                        sib_a_send(j, d, side, k).wait_send()
+
+                    @pl.when(yl == 1)
+                    def _():
+                        sib_b_send(zz, d, side, k).wait_send()
 
         return carry
 
-    lax.fori_loop(0, 10, drain, 0)
+    lax.fori_loop(1, 5, drain, 0)
 
 
 def on_device(q_nope, q_rope, absorb_key, kv_latent, value_up, out_proj):

time: 56.3 us -> 56.1 us (level)
  no operation moved by 1% of the time
where the time goes in v10:
time: 56.1 us; the launch traced here: 56 us
  Pallas kernels  54.3 us (97%)
  local copies, waits for them, and re-layouts  1.64 us (3%)
    pallas_call x1, Pallas kernels, on_device(): pl.pallas_call(kernel, out_shape=jax.ShapeDtypeStruct((columns, rows), jn...  54.3 us
    unnamed x1, local copies, waits for them, and re-layouts  1.64 us

profile of v10, /device:TPU:9, one launch (start us, length us, event | category | flops | bytes accessed | tf_op | source)
XLA Modules:
  0.0 56.0 jit_solution(3135361051689812614)
XLA Ops:
  0.0 54.3 %shard_map.64 = bf16[448,256]{1,0:T(8,128)(2,1)} custom-call(bf16[256,512]{1,0:T(8,128)(2,1)} %qn_hbm.1, bf16[256,256]{1,0:T(8,128)(2,1)} %qr_hbm.1, bf16[4,128,512]{2,1,0:T(8,128)(2,1)} %ak_hbm.1, bf16[4,144,256]{2,1,0:T(8,128)(2,1)} %bitcast.7, bf16[4,512,128]{2,1,0:T(8,128)(2,1)} %vu_hbm.1, bf16[448,8192]{1,0:T(8,128)(2,1)} %bitcast.6), custom_call_target="tpu_custom_call" | custom-call | flops 12000000000 | bytes 10000000 | tf_op jit(solution)/shard_map/pallas_call | solution.py:399
  54.3 1.6 %copy.8 = bf16[256,448]{0,1:T(8,128)(2,1)} copy(bf16[256,448]{0,1:T(8,128)(2,1)} %bitcast.5) | data formatting | bytes 458752

commit v11 on v10

--- a/solution.py
+++ b/solution.py
@@ -223,10 +223,6 @@
                 relay_a(d, k)
 
             def group(ab, carry):
-                @pl.when((ab == 1) & (yl == 1))
-                def _():
-                    relay_b(d - 1, k)
-
                 dd = d - 1 - ab
                 j = jnp.where(ab == 0, first_a, 0) + wrap(jnp.where(k == 0, z + NZ - dd, z + dd), NZ)
                 in_a = (ab == 0) & (((dd >= 1) & (dd <= 3)) | ((dd == 4) & (k == 0) & (yl == 1)))
@@ -236,6 +232,10 @@
                 def _():
                     swapped(j)
                     attend(j, False, (0, 1))
+
+                @pl.when((ab == 1) & (yl == 1))
+                def _():
+                    relay_b(d - 1, k)
 
                 return carry
 
@@ -287,11 +287,11 @@
             at = slice(h * rows, (h + 1) * rows)
             whole = jnp.sum(total[:, at], axis=0, keepdims=True)
             latent_out = (acc[:, at] * (1.0 / whole)).astype(jnp.bfloat16)
-            vbuf[o, k, (h % 2) * VDIM : (h % 2 + 1) * VDIM, :] = jnp.dot(
+            vbuf[o, h] = jnp.dot(
                 vu[h].T, latent_out, preferred_element_type=jnp.float32
             ).astype(jnp.bfloat16)
-        for way in ("up", "down", "far", "sib"):
-            send(0, k, way).start()
+            for way in ("up", "down", "far", "sib"):
+                send(0, h, way).start()
 
     mix[...] = jnp.zeros_like(mix)
 
@@ -306,15 +306,17 @@
             )
         mix[...] = term
 
+    def near(k):
+        return ((1, k, "far", *(("down",) if k % 2 else ())), (2, k, *(() if k % 2 else ("up",))), (4, k, "up"))
+
+    def middle(k):
+        return ((3, k), (5, k, "down"), (6, k))
+
     came = (
-        ((1, 0, "far"), (2, 0, "up"), (4, 0, "up")),
-        ((1, 1, "down", "far"), (2, 1), (4, 1, "up")),
-        ((3, 0), (5, 0, "down"), (3, 1)),
-        ((6, 0), (5, 1, "down")),
-        ((6, 1),),
-        ((7, 0),),
-        ((7, 1),),
+        near(0) + near(1), near(2) + near(3), middle(0), middle(1), middle(2), middle(3) + ((7, 0),),
+        ((7, 1),), ((7, 2),), ((7, 3),),
     )
+    projected = (0, 1, 2, 4, None, 3, 5, 6, 7)
 
     def event(t, carry):
         for n, items in enumerate(came):
@@ -329,18 +331,23 @@
         def _():
             locals_[8].wait()
 
-        n = jnp.where(t >= 4, t - 4, t)
-        dx = jnp.where(n == 2, 3, jnp.where(n == 3, 2, n))
-        place = outer_of(wrap(x + dx, NX), jnp.where(t >= 4, 1 - yh, yh), 0)
-        for k in range(2):
-            v_arrived(place + 1 - core, k)
-        project((place + core, place + 1 - core))
+        @pl.when((t > 0) & (t != 1 + projected.index(None)))
+        def _():
+            own_slot, sib_slot = own_slots[0], sib_slots[0]
+            for n, e in enumerate(projected):
+                if e:
+                    own_slot = jnp.where(t == n + 1, own_slots[e], own_slot)
+                    sib_slot = jnp.where(t == n + 1, sib_slots[e], sib_slot)
+            for k in range(heads):
+                v_arrived(sib_slot, k)
+            project((own_slot, sib_slot))
+
         return carry
 
-    lax.fori_loop(0, 8, event, 0)
+    lax.fori_loop(0, len(projected) + 1, event, 0)
     out_ref[...] = mix[...].astype(jnp.bfloat16)
 
-    for k in range(2):
+    for k in range(heads):
         for way in ("up", "down", "far", "sib"):
             send(0, k, way).wait_send()
     for items in came:
@@ -408,7 +415,7 @@
             pltpu.VMEM(value_up.shape, jnp.bfloat16),
             pltpu.VMEM(out_proj.shape, jnp.bfloat16),
             pltpu.VMEM((16, 4, WIDE // 4, rows), jnp.bfloat16),
-            pltpu.VMEM((16, 2, heads * VDIM // 2, rows), jnp.bfloat16),
+            pltpu.VMEM((16, heads, VDIM, rows), jnp.bfloat16),
             pltpu.VMEM((WIDE, heads * rows), jnp.bfloat16),
             pltpu.VMEM((8, heads * rows), jnp.float32),
             pltpu.VMEM((8, heads * rows), jnp.float32),
@@ -420,10 +427,10 @@
             dma((2, 5, 2)),
             dma((2, 5, 2)),
             dma((2, 5, 2)),
-            dma((16, 2)),
-            dma((8, 2, 2)),
-            dma((2, 2)),
-            dma((8, 2)),
+            dma((16, heads)),
+            dma((8, heads, 2)),
+            dma((2, heads)),
+            dma((8, heads)),
         ],
         compiler_params=pltpu.CompilerParams(
             collective_id=0, has_side_effects=True, vmem_limit_bytes=56 * 1024 * 1024

time: 56.1 us -> 58.6 us (1.045); the launches traced: 56 us -> 57.6 us
  Pallas kernels: 54.3 us -> 56 us
    pallas_call x1, Pallas kernels: 54.3 us -> 56 us  [on_device(): pl.pallas_call(kernel, out_shape=jax.ShapeDtypeStruct((columns, rows), jn...]
where the time goes in v11:
time: 58.6 us; the launch traced here: 57.6 us
  Pallas kernels  56 us (96%)
  local copies, waits for them, and re-layouts  1.64 us (3%)
    pallas_call x1, Pallas kernels, on_device(): pl.pallas_call(kernel, out_shape=jax.ShapeDtypeStruct((columns, rows), jn...  56 us
    unnamed x1, local copies, waits for them, and re-layouts  1.64 us

profile of v11, /device:TPU:9, one launch (start us, length us, event | category | flops | bytes accessed | tf_op | source)
XLA Modules:
  0.0 57.6 jit_solution(373262406447302084)
XLA Ops:
  0.0 56.0 %shard_map.64 = bf16[448,256]{1,0:T(8,128)(2,1)} custom-call(bf16[256,512]{1,0:T(8,128)(2,1)} %qn_hbm.1, bf16[256,256]{1,0:T(8,128)(2,1)} %qr_hbm.1, bf16[4,128,512]{2,1,0:T(8,128)(2,1)} %ak_hbm.1, bf16[4,144,256]{2,1,0:T(8,128)(2,1)} %bitcast.7, bf16[4,512,128]{2,1,0:T(8,128)(2,1)} %vu_hbm.1, bf16[448,8192]{1,0:T(8,128)(2,1)} %bitcast.6), custom_call_target="tpu_custom_call" | custom-call | flops 12000000000 | bytes 10000000 | tf_op jit(solution)/shard_map/pallas_call | solution.py:406
  56.0 1.6 %copy.8 = bf16[256,448]{0,1:T(8,128)(2,1)} copy(bf16[256,448]{0,1:T(8,128)(2,1)} %bitcast.5) | data formatting | bytes 458752

commit v12 on v0

v12 whole, which is shorter than its diff:
```python
import math

import jax
import jax.numpy as jnp
from jax import lax
from jax.experimental import pallas as pl
from jax.experimental.pallas import tpu as pltpu
from jax.sharding import PartitionSpec as P

NOPE = 128
ROPE = 64
VDIM = 128
LAT = 512
WIDE = LAT + ROPE
MESH = pl.DeviceIdType.MESH
SCALE = math.log2(math.e) / math.sqrt(NOPE + ROPE)
NX, NZ = 4, 8


def kernel(
    qn_hbm, qr_hbm, ak_hbm, kv_hbm, vu_hbm, wo_hbm, out_ref,
    qn, qr, ak, vu, wo, kvbuf, vbuf, query, qr_across, keys, peak, total, acc, mix,
    local_sem, kv_recv, send_z, send_y, sib_a, sib_b, v_recv, send_x, send_c, sib_v,
):
    heads, rows = ak.shape[0], qn.shape[0]
    width = 2 * rows
    o, i = lax.axis_index("outer"), lax.axis_index("inner")
    core, yh, x = lax.rem(o, 2), lax.rem(lax.div(o, 2), 2), lax.div(o, 4)
    yl, z = lax.div(i, NZ), lax.rem(i, NZ)

    def outer_of(x_, yh_, core_):
        return (x_ * 2 + yh_) * 2 + core_

    def wrap(n, size):
        return jnp.where(n >= size, n - size, n)

    def loop(first, end, body):
        def step(n, carry):
            body(n)
            return carry

        lax.fori_loop(first, end, step, 0)

    sibling = (outer_of(x, yh, 1 - core), i)
    first_a = yl * NZ
    z_up, z_down = first_a + wrap(z + 1, NZ), first_a + wrap(z + NZ - 1, NZ)
    y_up = (outer_of(x, wrap(yh + yl, 2), core), (1 - yl) * NZ + z)
    y_down = (outer_of(x, wrap(yh + 1 - yl, 2), core), (1 - yl) * NZ + z)
    o_far = outer_of(x, 1 - yh, core)
    y_far = (o_far, i)
    x_up = (outer_of(wrap(x + 1, NX), yh, core), i)
    x_down = (outer_of(wrap(x + NX - 1, NX), yh, core), i)

    locals_ = [
        pltpu.make_async_copy(src, dst, local_sem.at[n])
        for n, (src, dst) in enumerate(
            [(kv_hbm, kvbuf.at[i]), (qn_hbm, qn), (ak_hbm, ak), (qr_hbm, qr), (vu_hbm, vu), (wo_hbm, wo)]
        )
    ]
    for copy in locals_:
        copy.start()

    barrier = pltpu.get_barrier_semaphore()
    partners = (sibling, (o, z_up), (o, z_down), y_up, y_down, y_far, x_up, x_down)
    for partner in partners:
        pl.semaphore_signal(barrier, inc=1, device_id=partner, device_id_type=MESH)
    pl.semaphore_wait(barrier, len(partners))

    mine, others = 2 * core, 2 * (1 - core)

    def kv_copy(j, k, send_sem, target):
        piece = kvbuf.at[j, mine + k]
        return pltpu.make_async_remote_copy(
            src_ref=piece, dst_ref=piece, send_sem=send_sem,
            recv_sem=kv_recv.at[j, mine + k], device_id=target, device_id_type=MESH,
        )

    def kv_arrived(j, part):
        piece = kvbuf.at[j, part]
        pltpu.make_async_remote_copy(
            src_ref=piece, dst_ref=piece, send_sem=send_z.at[0, 0, 0],
            recv_sem=kv_recv.at[j, part], device_id=sibling, device_id_type=MESH,
        ).wait_recv()

    def ring(d, side):
        return wrap(jnp.where(side == 0, z + NZ - d, z + d), NZ)

    def z_forwards(d, side, k):
        return (d <= 2) | ((d == 3) & (k == side))

    def held(d, side, k):
        return ((d <= 3) & ((d >= 1) | (side == 0))) | ((d == 4) & (k == side))

    def z_send(j, d, side, k):
        return kv_copy(j, k, send_z.at[side, d, k], (o, jnp.where(side == 0, z_up, z_down)))

    def y_send(j, d, side, k):
        return kv_copy(j, k, send_y.at[side, d, k], (jnp.where(k == 0, o, o_far), NZ + z))

    def sib_a_send(j, d, side, k):
        return kv_copy(j, k, sib_a.at[side, d, k], sibling)

    def sib_b_send(j, d, side, k):
        return kv_copy(j, k, sib_b.at[side, d, k], sibling)

    def relay_a(d, k):
        def one(side):
            j = first_a + ring(d, side)
            here = held(d, side, k)

            @pl.when(here & (d >= 1))
            def _():
                kv_arrived(j, mine + k)

            @pl.when(z_forwards(d, side, k))
            def _():
                z_send(j, d, side, k).start()

            @pl.when(here & (yl == 0))
            def _():
                y_send(j, d, side, k).start()

            @pl.when(here & (j < i))
            def _():
                sib_a_send(j, d, side, k).start()

        loop(0, 2, one)

    def relay_b(d, k):
        def one(side):
            @pl.when(held(d, side, k))
            def _():
                j = ring(d, side)
                kv_arrived(j, mine + k)
                sib_b_send(j, d, side, k).start()

        loop(0, 2, one)

    def absorb(h):
        across = pl.ds(pl.multiple_of(h * rows, rows), rows)
        query[:LAT, across] = jnp.dot(
            qn[:, pl.ds(pl.multiple_of(h * NOPE, NOPE), NOPE)], ak[h],
            preferred_element_type=jnp.float32,
        ).astype(jnp.bfloat16).T
        query[LAT:, across] = qr_across[pl.ds(pl.multiple_of(h * ROPE, ROPE), ROPE)]

    def attend(j, pair, hidden_from):
        at = pl.ds(pl.multiple_of(pair * width, width), width)
        s = jnp.dot(keys[...], query[:, at], preferred_element_type=jnp.float32) * SCALE
        key = lax.broadcasted_iota(jnp.int32, s.shape, 0)
        row = lax.broadcasted_iota(jnp.int32, s.shape, 1)
        row = jnp.where(row >= rows, row - rows, row) + hidden_from
        s = jnp.where(key < row, s, jnp.float32(-1e30)).reshape(rows // 8, 8, width)
        old = peak[:, at]
        new = jnp.maximum(old, jnp.max(jnp.max(s, axis=0), axis=0, keepdims=True))
        shrink = jnp.exp2(old - new)
        w = jnp.exp2(s - new[None])
        update = jnp.dot(
            kvbuf[j].reshape(WIDE, rows)[:LAT], w.reshape(rows, width).astype(jnp.bfloat16),
            preferred_element_type=jnp.float32,
        )
        peak[:, at] = new
        total[:, at] = total[:, at] * shrink + jnp.sum(w, axis=0)
        grown = acc[:, at].reshape(LAT // 8, 8, width) * shrink[None]
        acc[:, at] = grown.reshape(LAT, width) + update

    def slot_of(e, core_):
        n = jnp.where(e >= 4, e - 4, e)
        dx = jnp.where(n == 2, 3, jnp.where(n == 3, 2, n))
        return outer_of(wrap(x + dx, NX), jnp.where(e >= 4, 1 - yh, yh), core_)

    def goes_far(e, k):
        return e <= 1

    def goes_up(e, k):
        return (e == 0) | (e == 4) | ((e == 2) & (k == 0))

    def goes_down(e, k):
        return (e == 0) | (e == 5) | ((e == 1) & (k == 1))

    def v_copy(e, k, send_sem, target):
        slot = slot_of(e, core)
        piece = vbuf.at[slot, k]
        return pltpu.make_async_remote_copy(
            src_ref=piece, dst_ref=piece, send_sem=send_sem,
            recv_sem=v_recv.at[slot, k], device_id=target, device_id_type=MESH,
        )

    def v_sends(e, k, act):
        @pl.when(goes_far(e, k))
        def _():
            act(v_copy(e, k, send_c.at[e, k], y_far))

        @pl.when(goes_up(e, k))
        def _():
            act(v_copy(e, k, send_x.at[e, k, 0], x_up))

        @pl.when(goes_down(e, k))
        def _():
            act(v_copy(e, k, send_x.at[e, k, 1], x_down))

        act(v_copy(e, k, sib_v.at[e, k], sibling))

    def v_arrived(slot, k):
        piece = vbuf.at[slot, k]
        pltpu.make_async_remote_copy(
            src_ref=piece, dst_ref=piece, send_sem=send_c.at[0, 0],
            recv_sem=v_recv.at[slot, k], device_id=sibling, device_id_type=MESH,
        ).wait_recv()

    def finish(pair):
        def one(n):
            h = 2 * pair + n
            at = pl.ds(pl.multiple_of(h * rows, rows), rows)
            whole = jnp.sum(total[:, at], axis=0, keepdims=True)
            latent_out = (acc[:, at] * (1.0 / whole)).astype(jnp.bfloat16)
            vbuf[o, pair, pl.ds(pl.multiple_of(n * VDIM, VDIM), VDIM), :] = jnp.dot(
                vu[h].T, latent_out, preferred_element_type=jnp.float32
            ).astype(jnp.bfloat16)

        loop(0, 2, one)

    def project(e):
        def one(core_):
            depth = heads * VDIM
            slot = slot_of(e, core_)
            start = pl.multiple_of(slot * depth, depth)
            mix[...] += jnp.dot(
                wo[:, pl.ds(start, depth)], vbuf[slot].reshape(depth, rows),
                preferred_element_type=jnp.float32,
            )

        loop(0, 2, one)

    locals_[0].wait()
    relay_a(0, 0)

    for n in (1, 2, 3):
        locals_[n].wait()
    qr_across[...] = qr[...].T
    loop(0, heads, absorb)
    relay_a(0, 1)

    peak[...] = jnp.full_like(peak, -1e30)
    total[...] = jnp.zeros_like(total)

    def clear(n):
        at = pl.ds(pl.multiple_of(n * 32, 32), 32)
        acc[at, :] = jnp.zeros((32, heads * rows), jnp.float32)

    loop(0, LAT // 32, clear)

    def clear_mix(n):
        at = pl.ds(pl.multiple_of(n * 64, 64), 64)
        mix[at, :] = jnp.zeros((64, rows), jnp.float32)

    loop(0, mix.shape[0] // 64, clear_mix)
    locals_[4].wait()

    def hop(d):
        def half_step(k):
            @pl.when((d >= 1) & (d <= 4))
            def _():
                relay_a(d, k)

            def group(ab):
                @pl.when((ab == 1) & (yl == 1) & (d >= 1) & (d <= 5))
                def _():
                    relay_b(d - 1, k)

                dd = d - 1 - ab
                far_end = wrap(z + 4, NZ)
                first, final = (d == 0) & (k == 0) & (ab == 0), (d == 6) & (k == 0) & (ab == 0)
                j = jnp.where(ab == 0, first_a, 0) + wrap(jnp.where(k == 0, z + NZ - dd, z + dd), NZ)
                j = jnp.where(first, i, jnp.where(final, far_end, j))
                middle = (d <= 5) & (dd >= 1) & (dd <= 3)
                in_a = (ab == 0) & (middle | ((d == 5) & (k == 0) & (yl == 1)))
                in_b = (ab == 1) & (yl == 1) & (middle | ((d == 2) & (k == 0)))
                other = (in_a | in_b | final) & (j < i)

                @pl.when(other)
                def _():
                    for part in range(2):
                        kv_arrived(j, others + part)

                @pl.when(other | first)
                def _():
                    keys[...] = kvbuf[j].reshape(WIDE, rows).T

                @pl.when(other | first | final)
                def _():
                    def each(pair):
                        @pl.when(other | first)
                        def _():
                            attend(j, pair, jnp.where(first, 1, 2 * rows))

                        @pl.when(final)
                        def _():
                            finish(pair)
                            v_sends(0, pair, lambda copy: copy.start())

                    loop(0, 2, each)

            loop(0, 2, group)

        loop(0, 2, half_step)

    loop(0, 7, hop)

    order = (
        (1, 0, None), (2, 0, None), (4, 0, 0), (1, 1, None), (2, 1, None), (4, 1, 1), (3, 0, None), (5, 0, None),
        (3, 1, 2), (6, 0, None), (5, 1, 3), (6, 1, 4), (7, 0, 5), (7, 1, 6), (None, None, 7),
    )
    locals_[5].wait()

    def event(m):
        e, k, done = 0, 0, -1
        for n, (e_, k_, done_) in enumerate(order):
            if e_ is not None:
                e, k = jnp.where(m == n, e_, e), jnp.where(m == n, k_, k)
            if done_ is not None:
                done = jnp.where(m == n, done_, done)

        @pl.when(m < len(order) - 1)
        def _():
            v_arrived(slot_of(e, core), k)
            v_sends(e, k, lambda copy: copy.start())

        @pl.when(done >= 0)
        def _():
            loop(0, 2, lambda k: v_arrived(slot_of(done, 1 - core), k))
            project(done)

    loop(0, len(order), event)
    out_ref[...] = mix[...].astype(jnp.bfloat16)

    loop(0, 8, lambda e: loop(0, 2, lambda k: v_sends(e, k, lambda copy: copy.wait_send())))

    def drain(d, k, side):
        zz = ring(d, side)
        j = first_a + zz
        here = held(d, side, k)

        @pl.when(z_forwards(d, side, k))
        def _():
            z_send(j, d, side, k).wait_send()

        @pl.when(here & (yl == 0))
        def _():
            y_send(j, d, side, k).wait_send()

        @pl.when(here & (j < i))
        def _():
            sib_a_send(j, d, side, k).wait_send()

        @pl.when(here & (yl == 1))
        def _():
            sib_b_send(zz, d, side, k).wait_send()

    loop(0, 5, lambda d: loop(0, 2, lambda k: loop(0, 2, lambda side: drain(d, k, side))))


def on_device(q_nope, q_rope, absorb_key, kv_latent, value_up, out_proj):
    rows = q_nope.shape[0]
    heads = absorb_key.shape[0]
    columns = out_proj.shape[1]
    kv_parts = kv_latent.T.reshape(4, WIDE // 4, rows)
    out_proj = out_proj.T
    dma = pltpu.SemaphoreType.DMA
    mixed = pl.pallas_call(
        kernel,
        out_shape=jax.ShapeDtypeStruct((columns, rows), jnp.bfloat16),
        in_specs=[pl.BlockSpec(memory_space=pl.ANY)] * 6,
        out_specs=pl.BlockSpec(memory_space=pltpu.VMEM),
        scratch_shapes=[
            pltpu.VMEM(q_nope.shape, jnp.bfloat16),
            pltpu.VMEM(q_rope.shape, jnp.bfloat16),
            pltpu.VMEM(absorb_key.shape, jnp.bfloat16),
            pltpu.VMEM(value_up.shape, jnp.bfloat16),
            pltpu.VMEM(out_proj.shape, jnp.bfloat16),
            pltpu.VMEM((16, 4, WIDE // 4, rows), jnp.bfloat16),
            pltpu.VMEM((16, 2, heads * VDIM // 2, rows), jnp.bfloat16),
            pltpu.VMEM((WIDE, heads * rows), jnp.bfloat16),
            pltpu.VMEM((heads * ROPE, rows), jnp.bfloat16),
            pltpu.VMEM((rows, WIDE), jnp.bfloat16),
            pltpu.VMEM((8, heads * rows), jnp.float32),
            pltpu.VMEM((8, heads * rows), jnp.float32),
            pltpu.VMEM((LAT, heads * rows), jnp.float32),
            pltpu.VMEM((columns, rows), jnp.float32),
            dma((6,)),
            dma((16, 4)),
            dma((2, 4, 2)),
            dma((2, 5, 2)),
            dma((2, 5, 2)),
            dma((2, 5, 2)),
            dma((16, 2)),
            dma((8, 2, 2)),
            dma((2, 2)),
            dma((8, 2)),
        ],
        compiler_params=pltpu.CompilerParams(
            collective_id=0, has_side_effects=True, vmem_limit_bytes=56 * 1024 * 1024
        ),
        cost_estimate=pl.CostEstimate(
            flops=12 * 10**9, bytes_accessed=10 * 10**6, transcendentals=4 * 10**6
        ),
    )(q_nope, q_rope, absorb_key, kv_parts, value_up, out_proj)
    return mixed.T


def solution(mesh):
    placed = (
        P("inner", "outer"),
        P("inner", "outer"),
        P("outer", None, None),
        P("inner", None),
        P("outer", None, None),
        P(None, "outer"),
    )
    return jax.shard_map(
        on_device, mesh=mesh, in_specs=placed, out_specs=P("inner", "outer"), check_vma=False
    )
```

time: 191 us -> 63.6 us (0.33)
  the two profiles are of different devices: /device:TPU:9 before, /device:TPU:239 now
where the time goes in v12:
time: 63.6 us; the launch traced here: 63.5 us
  Pallas kernels  61.9 us (97%)
  local copies, waits for them, and re-layouts  1.64 us (3%)
    pallas_call x1, Pallas kernels, on_device(): pl.pallas_call(kernel, out_shape=jax.ShapeDtypeStruct((columns, rows), jn...  61.9 us
    unnamed x1, local copies, waits for them, and re-layouts  1.64 us

profile of v12, /device:TPU:239, one launch (start us, length us, event | category | flops | bytes accessed | tf_op | source)
XLA Modules:
  0.0 63.5 jit_solution(16789074911998508348)
XLA Ops:
  0.0 61.9 %shard_map.64 = bf16[448,256]{1,0:T(8,128)(2,1)} custom-call(bf16[256,512]{1,0:T(8,128)(2,1)} %qn_hbm.1, bf16[256,256]{1,0:T(8,128)(2,1)} %qr_hbm.1, bf16[4,128,512]{2,1,0:T(8,128)(2,1)} %ak_hbm.1, bf16[4,144,256]{2,1,0:T(8,128)(2,1)} %bitcast.7, bf16[4,512,128]{2,1,0:T(8,128)(2,1)} %vu_hbm.1, bf16[448,8192]{1,0:T(8,128)(2,1)} %bitcast.6), custom_call_target="tpu_custom_call" | custom-call | flops 12000000000 | bytes 10000000 | tf_op jit(solution)/shard_map/pallas_call | solution.py:370
  61.9 1.6 %copy.8 = bf16[256,448]{0,1:T(8,128)(2,1)} copy(bf16[256,448]{0,1:T(8,128)(2,1)} %bitcast.5) | data formatting | bytes 458752

commit v13 on v11

--- a/solution.py
+++ b/solution.py
@@ -27,8 +27,8 @@
 
 def kernel(
     qn_hbm, qr_hbm, ak_hbm, kv_hbm, vu_hbm, wo_hbm, out_ref,
-    qn, qr, ak, vu, wo, kvbuf, vbuf, query, peak, total, acc, mix,
-    local_sem, kv_recv, send_z, send_y, sib_a, sib_b, v_recv, send_x, send_c, sib_v,
+    qn, qr, ak, vu, wo, kvbuf, vbuf, query, peak, total, acc, mix, out_here,
+    local_sem, kv_recv, send_z, send_y, sib_a, sib_b, v_recv, send_x, send_c, sib_v, out_sem,
 ):
     heads, rows = ak.shape[0], qn.shape[0]
     o, i = lax.axis_index("outer"), lax.axis_index("inner")
@@ -58,13 +58,12 @@
         [(qn_hbm, qn), (ak_hbm, ak), (qr_hbm, qr), (vu_hbm, vu), (wo_hbm, wo)]
     ):
         locals_.append(pltpu.make_async_copy(src, dst, local_sem.at[4 + n]))
-    for copy in locals_:
-        copy.start()
-
     barrier = pltpu.get_barrier_semaphore()
     partners = (sibling, z_up, z_down, y_up, y_down, y_far, x_up, x_down)
     for partner in partners:
         pl.semaphore_signal(barrier, inc=1, device_id=partner, device_id_type=MESH)
+    for copy in locals_:
+        copy.start()
     pl.semaphore_wait(barrier, len(partners))
 
     mine, others = 2 * core, 2 * (1 - core)
@@ -223,6 +222,10 @@
                 relay_a(d, k)
 
             def group(ab, carry):
+                @pl.when((ab == 1) & (yl == 1))
+                def _():
+                    relay_b(d - 1, k)
+
                 dd = d - 1 - ab
                 j = jnp.where(ab == 0, first_a, 0) + wrap(jnp.where(k == 0, z + NZ - dd, z + dd), NZ)
                 in_a = (ab == 0) & (((dd >= 1) & (dd <= 3)) | ((dd == 4) & (k == 0) & (yl == 1)))
@@ -232,10 +235,6 @@
                 def _():
                     swapped(j)
                     attend(j, False, (0, 1))
-
-                @pl.when((ab == 1) & (yl == 1))
-                def _():
-                    relay_b(d - 1, k)
 
                 return carry
 
@@ -293,6 +292,46 @@
             for way in ("up", "down", "far", "sib"):
                 send(0, h, way).start()
 
+    for k in range(2):
+        for side in range(2):
+            z_send(i, 0, side, k).wait_send()
+
+        @pl.when(yl == 0)
+        def _():
+            y_send(i, 0, 0, k).wait_send()
+
+        @pl.when(yl == 1)
+        def _():
+            sib_b_send(z, 0, 0, k).wait_send()
+
+    def drain(d, carry):
+        for k in range(2):
+            for side in range(2):
+                @pl.when(held_a(d, side, k))
+                def _():
+                    zz = ring(d, side)
+                    j = first_a + zz
+
+                    @pl.when(z_forwards(d, side, k))
+                    def _():
+                        z_send(j, d, side, k).wait_send()
+
+                    @pl.when(yl == 0)
+                    def _():
+                        y_send(j, d, side, k).wait_send()
+
+                    @pl.when(j < i)
+                    def _():
+                        sib_a_send(j, d, side, k).wait_send()
+
+                    @pl.when(yl == 1)
+                    def _():
+                        sib_b_send(zz, d, side, k).wait_send()
+
+        return carry
+
+    lax.fori_loop(1, 5, drain, 0)
+
     mix[...] = jnp.zeros_like(mix)
 
     def project(slots):
@@ -307,93 +346,68 @@
         mix[...] = term
 
     def near(k):
-        return ((1, k, "far", *(("down",) if k % 2 else ())), (2, k, *(() if k % 2 else ("up",))), (4, k, "up"))
+        if k % 2 == 0:
+            return ((1, k, "far"), (2, k, "up"), (4, k, "up"))
+        return ((2, k, "far"), (1, k, "down"), (4, k, "down"))
 
     def middle(k):
-        return ((3, k), (5, k, "down"), (6, k))
-
-    came = (
-        near(0) + near(1), near(2) + near(3), middle(0), middle(1), middle(2), middle(3) + ((7, 0),),
-        ((7, 1),), ((7, 2),), ((7, 3),),
+        if k < 2:
+            return ((3, k, "far"), (5 + k % 2, k))
+        return ((3, k), (5 + k % 2, k, ("up" if k % 2 else "down")))
+
+    steps = (
+        (near(0) + near(1), None),
+        (near(2) + near(3), 0),
+        (middle(0) + middle(1), None),
+        (middle(2) + middle(3), 1),
+        ((), 2),
+        (((6, 0), (5, 1), (6, 2), (5, 3)), 3),
+        ((), 4),
+        (((7, 0), (7, 1)), 5),
+        ((), 6),
+        (((7, 2), (7, 3)), 7),
     )
-    projected = (0, 1, 2, 4, None, 3, 5, 6, 7)
 
     def event(t, carry):
-        for n, items in enumerate(came):
-            @pl.when(t == n)
-            def _():
-                for e, k, *ways in items:
-                    v_arrived(own_slots[e], k)
-                    for way in (*ways, "sib"):
-                        send(e, k, way).start()
+        for n, (items, _) in enumerate(steps):
+            if items:
+                @pl.when(t == n)
+                def _():
+                    for e, k, *ways in items:
+                        v_arrived(own_slots[e], k)
+                        for way in (*ways, "sib"):
+                            send(e, k, way).start()
 
         @pl.when(t == 0)
         def _():
             locals_[8].wait()
 
-        @pl.when((t > 0) & (t != 1 + projected.index(None)))
+        @pl.when((t != 0) & (t != 2))
         def _():
             own_slot, sib_slot = own_slots[0], sib_slots[0]
-            for n, e in enumerate(projected):
+            for n, (_, e) in enumerate(steps):
                 if e:
-                    own_slot = jnp.where(t == n + 1, own_slots[e], own_slot)
-                    sib_slot = jnp.where(t == n + 1, sib_slots[e], sib_slot)
+                    own_slot = jnp.where(t == n, own_slots[e], own_slot)
+                    sib_slot = jnp.where(t == n, sib_slots[e], sib_slot)
             for k in range(heads):
                 v_arrived(sib_slot, k)
             project((own_slot, sib_slot))
 
         return carry
 
-    lax.fori_loop(0, len(projected) + 1, event, 0)
-    out_ref[...] = mix[...].astype(jnp.bfloat16)
+    lax.fori_loop(0, len(steps), event, 0)
+    out_here[...] = mix[...].astype(jnp.bfloat16)
+    out_copy = pltpu.make_async_copy(out_here, out_ref, out_sem.at[0])
+    out_copy.start()
 
     for k in range(heads):
         for way in ("up", "down", "far", "sib"):
             send(0, k, way).wait_send()
-    for items in came:
+    for items, _ in steps:
         for e, k, *ways in items:
             for way in (*ways, "sib"):
                 send(e, k, way).wait_send()
-
-    for k in range(2):
-        for side in range(2):
-            z_send(i, 0, side, k).wait_send()
-
-        @pl.when(yl == 0)
-        def _():
-            y_send(i, 0, 0, k).wait_send()
-
-        @pl.when(yl == 1)
-        def _():
-            sib_b_send(z, 0, 0, k).wait_send()
-
-    def drain(d, carry):
-        for k in range(2):
-            for side in range(2):
-                @pl.when(held_a(d, side, k))
-                def _():
-                    zz = ring(d, side)
-                    j = first_a + zz
-
-                    @pl.when(z_forwards(d, side, k))
-                    def _():
-                        z_send(j, d, side, k).wait_send()
-
-                    @pl.when(yl == 0)
-                    def _():
-                        y_send(j, d, side, k).wait_send()
-
-                    @pl.when(j < i)
-                    def _():
-                        sib_a_send(j, d, side, k).wait_send()
-
-                    @pl.when(yl == 1)
-                    def _():
-                        sib_b_send(zz, d, side, k).wait_send()
-
-        return carry
-
-    lax.fori_loop(1, 5, drain, 0)
+    out_copy.wait()
 
 
 def on_device(q_nope, q_rope, absorb_key, kv_latent, value_up, out_proj):
@@ -407,7 +421,7 @@
         kernel,
         out_shape=jax.ShapeDtypeStruct((columns, rows), jnp.bfloat16),
         in_specs=[pl.BlockSpec(memory_space=pl.ANY)] * 6,
-        out_specs=pl.BlockSpec(memory_space=pltpu.VMEM),
+        out_specs=pl.BlockSpec(memory_space=pl.ANY),
         scratch_shapes=[
             pltpu.VMEM(q_nope.shape, jnp.bfloat16),
             pltpu.VMEM(q_rope.shape, jnp.bfloat16),
@@ -421,6 +435,7 @@
             pltpu.VMEM((8, heads * rows), jnp.float32),
             pltpu.VMEM((LAT, heads * rows), jnp.float32),
             pltpu.VMEM((columns, rows), jnp.float32),
+            pltpu.VMEM((columns, rows), jnp.bfloat16),
             dma((9,)),
             dma((16, 4)),
             dma((2, 4, 2)),
@@ -429,8 +444,9 @@
             dma((2, 5, 2)),
             dma((16, heads)),
             dma((8, heads, 2)),
-            dma((2, heads)),
+            dma((4, heads)),
             dma((8, heads)),
+            dma((1,)),
         ],
         compiler_params=pltpu.CompilerParams(
             collective_id=0, has_side_effects=True, vmem_limit_bytes=56 * 1024 * 1024

time: 58.6 us -> 56.4 us (0.962); the launches traced: 57.6 us -> 56.1 us
  Pallas kernels: 56 us -> 54.4 us
    pallas_call x1, Pallas kernels: 56 us -> 54.4 us  [on_device(): pl.pallas_call(kernel, out_shape=jax.ShapeDtypeStruct((columns, rows), jn...]
where the time goes in v13:
time: 56.4 us; the launch traced here: 56.1 us
  Pallas kernels  54.4 us (96%)
  local copies, waits for them, and re-layouts  1.64 us (3%)
    pallas_call x1, Pallas kernels, on_device(): pl.pallas_call(kernel, out_shape=jax.ShapeDtypeStruct((columns, rows), jn...  54.4 us
    unnamed x1, local copies, waits for them, and re-layouts  1.64 us

profile of v13, /device:TPU:9, one launch (start us, length us, event | category | flops | bytes accessed | tf_op | source)
XLA Modules:
  0.0 56.1 jit_solution(13894694175702411326)
XLA Ops:
  0.0 54.4 %shard_map.64 = bf16[448,256]{1,0:T(8,128)(2,1)} custom-call(bf16[256,512]{1,0:T(8,128)(2,1)} %qn_hbm.1, bf16[256,256]{1,0:T(8,128)(2,1)} %qr_hbm.1, bf16[4,128,512]{2,1,0:T(8,128)(2,1)} %ak_hbm.1, bf16[4,144,256]{2,1,0:T(8,128)(2,1)} %bitcast.7, bf16[4,512,128]{2,1,0:T(8,128)(2,1)} %vu_hbm.1, bf16[448,8192]{1,0:T(8,128)(2,1)} %bitcast.6), custom_call_target="tpu_custom_call" | custom-call | flops 12000000000 | bytes 10000000 | tf_op jit(solution)/shard_map/pallas_call | solution.py:420
  54.4 1.6 %copy.8 = bf16[256,448]{0,1:T(8,128)(2,1)} copy(bf16[256,448]{0,1:T(8,128)(2,1)} %bitcast.5) | data formatting | bytes 458752

commit v14 on v10

--- a/solution.py
+++ b/solution.py
@@ -86,11 +86,21 @@
     def ring(d, side):
         return wrap(z + (d if side else NZ - d), NZ)
 
-    def z_forwards(d, side, k):
-        return (d <= 2) | ((d == 3) & (k == side))
-
-    def held_a(d, side, k):
-        return (d <= 3) | ((d == 4) & (k == side))
+    def z_forwards(d, side, k, src):
+        late = (
+            (src <= 2) & ((d <= 2) | ((d == 3) & (src == 0) & (k == 1)))
+            if side
+            else (z < NZ - 1) & ((d <= 2) | ((d == 3) & ((src > 0) | (k == 0))))
+        )
+        return ((yl == 0) & ((d <= 2) | ((d == 3) & (k == side)))) | ((yl == 1) & late)
+
+    def held_a(d, side, k, src):
+        late = (
+            (src <= 2) & ((d <= 3) | ((d == 4) & (src == 0) & (k == 1)))
+            if side
+            else (z >= d) & ((d <= 3) | ((d == 4) & ((src > 0) | (k == 0))))
+        )
+        return ((yl == 0) & held_b(d, side, k)) | ((yl == 1) & late)
 
     def held_b(d, side, k):
         return (d <= 3) | ((d == 4) & (k == side))
@@ -113,12 +123,14 @@
 
     def relay_a(d, k):
         for side in range(2):
-            @pl.when(held_a(d, side, k))
-            def _():
-                j = first_a + ring(d, side)
+            src = ring(d, side)
+
+            @pl.when(held_a(d, side, k, src))
+            def _():
+                j = first_a + src
                 kv_arrived(j, mine + k)
 
-                @pl.when(z_forwards(d, side, k))
+                @pl.when(z_forwards(d, side, k, src))
                 def _():
                     z_send(j, d, side, k).start()
 
@@ -148,7 +160,9 @@
 
     def own(k):
         for side in range(2):
-            z_send(i, 0, side, k).start()
+            @pl.when(z_forwards(0, side, k, z))
+            def _():
+                z_send(i, 0, side, k).start()
 
         @pl.when(yl == 0)
         def _():
@@ -350,7 +364,9 @@
 
     for k in range(2):
         for side in range(2):
-            z_send(i, 0, side, k).wait_send()
+            @pl.when(z_forwards(0, side, k, z))
+            def _():
+                z_send(i, 0, side, k).wait_send()
 
         @pl.when(yl == 0)
         def _():
@@ -363,12 +379,12 @@
     def drain(d, carry):
         for k in range(2):
             for side in range(2):
-                @pl.when(held_a(d, side, k))
-                def _():
-                    zz = ring(d, side)
-                    j = first_a + zz
-
-                    @pl.when(z_forwards(d, side, k))
+                src = ring(d, side)
+                j = first_a + src
+
+                @pl.when(held_a(d, side, k, src))
+                def _():
+                    @pl.when(z_forwards(d, side, k, src))
                     def _():
                         z_send(j, d, side, k).wait_send()
 
@@ -380,9 +396,9 @@
                     def _():
                         sib_a_send(j, d, side, k).wait_send()
 
-                    @pl.when(yl == 1)
-                    def _():
-                        sib_b_send(zz, d, side, k).wait_send()
+                @pl.when((yl == 1) & held_b(d, side, k))
+                def _():
+                    sib_b_send(src, d, side, k).wait_send()
 
         return carry
 
@@ -398,7 +414,7 @@
     dma = pltpu.SemaphoreType.DMA
     mixed = pl.pallas_call(
         kernel,
-        out_shape=jax.ShapeDtypeStruct((columns, rows), jnp.bfloat16),
+        out_shape=pltpu.VMEM((columns, rows), jnp.bfloat16),
         in_specs=[pl.BlockSpec(memory_space=pl.ANY)] * 6,
         out_specs=pl.BlockSpec(memory_space=pltpu.VMEM),
         scratch_shapes=[

time: 56.1 us -> 54.6 us (0.973)
  local copies, waits for them, and re-layouts: 1.64 us -> 0.69 us
    unnamed x1, local copies, waits for them, and re-layouts: 1.64 us -> 0.69 us
where the time goes in v14:
time: 54.6 us; the launch traced here: 54.5 us
  Pallas kernels  53.8 us (99%)
  local copies, waits for them, and re-layouts  0.69 us (1%)
    pallas_call x1, Pallas kernels, on_device(): pl.pallas_call(kernel, out_shape=pltpu.VMEM((columns, rows), jnp.bfloat16...  53.8 us

profile of v14, /device:TPU:9, one launch (start us, length us, event | category | flops | bytes accessed | tf_op | source)
XLA Modules:
  0.0 54.5 jit_solution(6612290062201714289)
XLA Ops:
  0.0 53.8 %shard_map.64 = bf16[448,256]{1,0:T(8,128)(2,1)S(1)} custom-call(bf16[256,512]{1,0:T(8,128)(2,1)} %qn_hbm.1, bf16[256,256]{1,0:T(8,128)(2,1)} %qr_hbm.1, bf16[4,128,512]{2,1,0:T(8,128)(2,1)} %ak_hbm.1, bf16[4,144,256]{2,1,0:T(8,128)(2,1)} %bitcast.7, bf16[4,512,128]{2,1,0:T(8,128)(2,1)} %vu_hbm.1, bf16[448,8192]{1,0:T(8,128)(2,1)} %bitcast.6), custom_call_target="tpu_custom_call" | custom-call | flops 12000000000 | bytes 10000000 | tf_op jit(solution)/shard_map/pallas_call | solution.py:415
  53.8 0.7 %copy.8 = bf16[256,448]{0,1:T(8,128)(2,1)} copy(bf16[256,448]{0,1:T(8,128)(2,1)S(1)} %bitcast.5) | data formatting | bytes 458752

commit v15 on v14

--- a/solution.py
+++ b/solution.py
@@ -58,13 +58,12 @@
         [(qn_hbm, qn), (ak_hbm, ak), (qr_hbm, qr), (vu_hbm, vu), (wo_hbm, wo)]
     ):
         locals_.append(pltpu.make_async_copy(src, dst, local_sem.at[4 + n]))
-    for copy in locals_:
-        copy.start()
-
     barrier = pltpu.get_barrier_semaphore()
     partners = (sibling, z_up, z_down, y_up, y_down, y_far, x_up, x_down)
     for partner in partners:
         pl.semaphore_signal(barrier, inc=1, device_id=partner, device_id_type=MESH)
+    for copy in locals_:
+        copy.start()
     pl.semaphore_wait(barrier, len(partners))
 
     mine, others = 2 * core, 2 * (1 - core)
@@ -307,6 +306,48 @@
         for way in ("up", "down", "far", "sib"):
             send(0, k, way).start()
 
+    for k in range(2):
+        for side in range(2):
+            @pl.when(z_forwards(0, side, k, z))
+            def _():
+                z_send(i, 0, side, k).wait_send()
+
+        @pl.when(yl == 0)
+        def _():
+            y_send(i, 0, 0, k).wait_send()
+
+        @pl.when(yl == 1)
+        def _():
+            sib_b_send(z, 0, 0, k).wait_send()
+
+    def drain(d, carry):
+        for k in range(2):
+            for side in range(2):
+                src = ring(d, side)
+                j = first_a + src
+
+                @pl.when(held_a(d, side, k, src))
+                def _():
+                    @pl.when(z_forwards(d, side, k, src))
+                    def _():
+                        z_send(j, d, side, k).wait_send()
+
+                    @pl.when(yl == 0)
+                    def _():
+                        y_send(j, d, side, k).wait_send()
+
+                    @pl.when(j < i)
+                    def _():
+                        sib_a_send(j, d, side, k).wait_send()
+
+                @pl.when((yl == 1) & held_b(d, side, k))
+                def _():
+                    sib_b_send(src, d, side, k).wait_send()
+
+        return carry
+
+    lax.fori_loop(1, 5, drain, 0)
+
     mix[...] = jnp.zeros_like(mix)
 
     def project(slots):
@@ -343,6 +384,16 @@
         def _():
             locals_[8].wait()
 
+        @pl.when(t == 7)
+        def _():
+            for k in range(2):
+                for way in ("up", "down", "far", "sib"):
+                    send(0, k, way).wait_send()
+            for items in came:
+                for e, k, *ways in items:
+                    for way in (*ways, *(("sib",) if e < 7 else ())):
+                        send(e, k, way).wait_send()
+
         n = jnp.where(t >= 4, t - 4, t)
         dx = jnp.where(n == 2, 3, jnp.where(n == 3, 2, n))
         place = outer_of(wrap(x + dx, NX), jnp.where(t >= 4, 1 - yh, yh), 0)
@@ -355,54 +406,7 @@
     out_ref[...] = mix[...].astype(jnp.bfloat16)
 
     for k in range(2):
-        for way in ("up", "down", "far", "sib"):
-            send(0, k, way).wait_send()
-    for items in came:
-        for e, k, *ways in items:
-            for way in (*ways, "sib"):
-                send(e, k, way).wait_send()
-
-    for k in range(2):
-        for side in range(2):
-            @pl.when(z_forwards(0, side, k, z))
-            def _():
-                z_send(i, 0, side, k).wait_send()
-
-        @pl.when(yl == 0)
-        def _():
-            y_send(i, 0, 0, k).wait_send()
-
-        @pl.when(yl == 1)
-        def _():
-            sib_b_send(z, 0, 0, k).wait_send()
-
-    def drain(d, carry):
-        for k in range(2):
-            for side in range(2):
-                src = ring(d, side)
-                j = first_a + src
-
-                @pl.when(held_a(d, side, k, src))
-                def _():
-                    @pl.when(z_forwards(d, side, k, src))
-                    def _():
-                        z_send(j, d, side, k).wait_send()
-
-                    @pl.when(yl == 0)
-                    def _():
-                        y_send(j, d, side, k).wait_send()
-
-                    @pl.when(j < i)
-                    def _():
-                        sib_a_send(j, d, side, k).wait_send()
-
-                @pl.when((yl == 1) & held_b(d, side, k))
-                def _():
-                    sib_b_send(src, d, side, k).wait_send()
-
-        return carry
-
-    lax.fori_loop(1, 5, drain, 0)
+        send(7, k, "sib").wait_send()
 
 
 def on_device(q_nope, q_rope, absorb_key, kv_latent, value_up, out_proj):

time: 54.6 us -> 54.2 us (level)
  no operation moved by 1% of the time
where the time goes in v15:
time: 54.2 us; the launch traced here: 54.1 us
  Pallas kernels  53.4 us (99%)
  local copies, waits for them, and re-layouts  0.69 us (1%)
    pallas_call x1, Pallas kernels, on_device(): pl.pallas_call(kernel, out_shape=pltpu.VMEM((columns, rows), jnp.bfloat16...  53.4 us

profile of v15, /device:TPU:9, one launch (start us, length us, event | category | flops | bytes accessed | tf_op | source)
XLA Modules:
  0.0 54.1 jit_solution(1516073091018847201)
XLA Ops:
  0.0 53.4 %shard_map.64 = bf16[448,256]{1,0:T(8,128)(2,1)S(1)} custom-call(bf16[256,512]{1,0:T(8,128)(2,1)} %qn_hbm.1, bf16[256,256]{1,0:T(8,128)(2,1)} %qr_hbm.1, bf16[4,128,512]{2,1,0:T(8,128)(2,1)} %ak_hbm.1, bf16[4,144,256]{2,1,0:T(8,128)(2,1)} %bitcast.7, bf16[4,512,128]{2,1,0:T(8,128)(2,1)} %vu_hbm.1, bf16[448,8192]{1,0:T(8,128)(2,1)} %bitcast.6), custom_call_target="tpu_custom_call" | custom-call | flops 12000000000 | bytes 10000000 | tf_op jit(solution)/shard_map/pallas_call | solution.py:419
  53.4 0.7 %copy.8 = bf16[256,448]{0,1:T(8,128)(2,1)} copy(bf16[256,448]{0,1:T(8,128)(2,1)S(1)} %bitcast.5) | data formatting | bytes 458752

commit v16 on v15

--- a/solution.py
+++ b/solution.py
@@ -28,7 +28,8 @@
 def kernel(
     qn_hbm, qr_hbm, ak_hbm, kv_hbm, vu_hbm, wo_hbm, out_ref,
     qn, qr, ak, vu, wo, kvbuf, vbuf, query, peak, total, acc, mix,
-    local_sem, kv_recv, send_z, send_y, sib_a, sib_b, v_recv, send_x, send_c, sib_v,
+    local_sem, kv_recv, send_z, send_y, sib_a, sib_b, far_z, far_y, far_x, far_sib,
+    v_recv, send_x, send_c, sib_v,
 ):
     heads, rows = ak.shape[0], qn.shape[0]
     o, i = lax.axis_index("outer"), lax.axis_index("inner")
@@ -49,6 +50,9 @@
     y_far = (outer_of(x, 1 - yh, core), i)
     x_up = (outer_of(wrap(x + 1, NX), yh, core), i)
     x_down = (outer_of(wrap(x + NX - 1, NX), yh, core), i)
+
+    x_far = (outer_of(wrap(x + 2, NX), yh, core), i)
+    z_far = (o, yl * NZ + wrap(z + 4, NZ))
 
     locals_ = [
         pltpu.make_async_copy(kv_hbm.at[part], kvbuf.at[i, part], local_sem.at[part])
@@ -59,7 +63,7 @@
     ):
         locals_.append(pltpu.make_async_copy(src, dst, local_sem.at[4 + n]))
     barrier = pltpu.get_barrier_semaphore()
-    partners = (sibling, z_up, z_down, y_up, y_down, y_far, x_up, x_down)
+    partners = (sibling, z_up, z_down, z_far, y_up, y_down, y_far, x_up, x_down, x_far)
     for partner in partners:
         pl.semaphore_signal(barrier, inc=1, device_id=partner, device_id_type=MESH)
     for copy in locals_:
@@ -68,12 +72,15 @@
 
     mine, others = 2 * core, 2 * (1 - core)
 
-    def kv_copy(j, k, send_sem, target):
-        piece = kvbuf.at[j, mine + k]
+    def part_copy(j, part, send_sem, target):
+        piece = kvbuf.at[j, part]
         return pltpu.make_async_remote_copy(
             src_ref=piece, dst_ref=piece, send_sem=send_sem,
-            recv_sem=kv_recv.at[j, mine + k], device_id=target, device_id_type=MESH,
+            recv_sem=kv_recv.at[j, part], device_id=target, device_id_type=MESH,
         )
+
+    def kv_copy(j, k, send_sem, target):
+        return part_copy(j, mine + k, send_sem, target)
 
     def kv_arrived(j, part):
         piece = kvbuf.at[j, part]
@@ -85,24 +92,13 @@
     def ring(d, side):
         return wrap(z + (d if side else NZ - d), NZ)
 
-    def z_forwards(d, side, k, src):
-        late = (
-            (src <= 2) & ((d <= 2) | ((d == 3) & (src == 0) & (k == 1)))
-            if side
-            else (z < NZ - 1) & ((d <= 2) | ((d == 3) & ((src > 0) | (k == 0))))
-        )
-        return ((yl == 0) & ((d <= 2) | ((d == 3) & (k == side)))) | ((yl == 1) & late)
-
-    def held_a(d, side, k, src):
-        late = (
-            (src <= 2) & ((d <= 3) | ((d == 4) & (src == 0) & (k == 1)))
-            if side
-            else (z >= d) & ((d <= 3) | ((d == 4) & ((src > 0) | (k == 0))))
-        )
-        return ((yl == 0) & held_b(d, side, k)) | ((yl == 1) & late)
-
-    def held_b(d, side, k):
-        return (d <= 3) | ((d == 4) & (k == side))
+    def z_forwards(d, side, src):
+        late = (src <= 2) if side else (z < NZ - 1)
+        return (d <= 2) & ((yl == 0) | late)
+
+    def held_a(d, side, src):
+        late = (src <= 2) if side else (z >= d)
+        return (d <= 3) & ((yl == 0) | late)
 
     first_a = yl * NZ
 
@@ -124,12 +120,12 @@
         for side in range(2):
             src = ring(d, side)
 
-            @pl.when(held_a(d, side, k, src))
+            @pl.when(held_a(d, side, src))
             def _():
                 j = first_a + src
                 kv_arrived(j, mine + k)
 
-                @pl.when(z_forwards(d, side, k, src))
+                @pl.when(z_forwards(d, side, src))
                 def _():
                     z_send(j, d, side, k).start()
 
@@ -147,19 +143,67 @@
             kv_arrived(z, mine + k)
             sib_b_send(z, 0, 0, k).start()
 
-        for side in range(2):
-            @pl.when((d >= 1) & held_b(d, side, k))
-            def _():
+        @pl.when(d >= 1)
+        def _():
+            for side in range(2):
                 j = ring(d, side)
                 kv_arrived(j, mine + k)
                 sib_b_send(j, d, side, k).start()
 
+    opposite = wrap(z + 4, NZ)
+    far_core = core == lax.rem(z, 2)
+    far_shards = (first_a + opposite, opposite)
+
+    def far_needed(ab):
+        return far_core & ((yl == 1) if ab else (far_shards[0] < i))
+
+    far_sent = far_core & ((yl == 0) | (z < 4))
+    far_held = far_core & ((yl == 0) | (z >= 4))
+
+    def far_z_send():
+        return part_copy(i, x, far_z.at[0], z_far)
+
+    def far_y_send():
+        return part_copy(opposite, x, far_y.at[0], (jnp.where(lax.rem(x, 2) == 0, o, o_far), NZ + z))
+
+    def far_x_sends(ab):
+        return [
+            part_copy(far_shards[ab], x, far_x.at[ab, n], target)
+            for n, target in enumerate((x_up, x_down, x_far))
+        ]
+
+    def far_sib_send(ab, n):
+        return part_copy(far_shards[ab], wrap(x + n, NX), far_sib.at[ab, n], sibling)
+
+    def far_first(ab):
+        @pl.when(((yl == 1) & far_core) if ab else far_held)
+        def _():
+            kv_arrived(far_shards[ab], x)
+
+        if ab == 0:
+            @pl.when((yl == 0) & far_core)
+            def _():
+                far_y_send().start()
+
+        @pl.when(far_needed(ab))
+        def _():
+            for copy in far_x_sends(ab):
+                copy.start()
+            far_sib_send(ab, 0).start()
+
+    def far_rest(ab):
+        @pl.when(far_needed(ab))
+        def _():
+            for n in range(1, NX):
+                kv_arrived(far_shards[ab], wrap(x + n, NX))
+                far_sib_send(ab, n).start()
+
     for part in range(4):
         locals_[part].wait()
 
     def own(k):
         for side in range(2):
-            @pl.when(z_forwards(0, side, k, z))
+            @pl.when(z_forwards(0, side, z))
             def _():
                 z_send(i, 0, side, k).start()
 
@@ -223,6 +267,11 @@
             fold(pair, pair_scores)
 
     own(1)
+
+    @pl.when(far_sent)
+    def _():
+        far_z_send().start()
+
     attend(i, True, (0, 1))
 
     def swapped(j):
@@ -231,33 +280,61 @@
 
     def hop(d, carry):
         def half_step(k, carry):
-            @pl.when(d <= 4)
+            @pl.when(d <= 3)
             def _():
                 relay_a(d, k)
 
+            @pl.when((d == 2) & (k == 1))
+            def _():
+                far_first(0)
+
+            @pl.when((d == 3) & (k == 0))
+            def _():
+                far_rest(0)
+
             def group(ab, carry):
-                @pl.when((ab == 1) & (yl == 1))
+                @pl.when((ab == 2) & (yl == 1) & (d <= 4))
                 def _():
                     relay_b(d - 1, k)
 
-                dd = d - 1 - ab
-                j = jnp.where(ab == 0, first_a, 0) + wrap(jnp.where(k == 0, z + NZ - dd, z + dd), NZ)
-                in_a = (ab == 0) & (((dd >= 1) & (dd <= 3)) | ((dd == 4) & (k == 0) & (yl == 1)))
-                in_b = (ab == 1) & (yl == 1) & (((dd >= 1) & (dd <= 3)) | ((dd == 0) & (k == 0)))
-
-                @pl.when((in_a | in_b) & (j < i))
-                def _():
-                    swapped(j)
+                @pl.when((ab == 2) & (yl == 1) & (d == 3) & (k == 1))
+                def _():
+                    far_first(1)
+
+                @pl.when((ab == 2) & (yl == 1) & (d == 4) & (k == 0))
+                def _():
+                    far_rest(1)
+
+                far = (ab == 1) | (ab == 3)
+                dd = jnp.where(ab >= 2, d - 2, d - 1)
+                zz = wrap(jnp.where(k == 0, z + NZ - dd, z + dd), NZ)
+                j = jnp.where(ab < 2, first_a, 0) + jnp.where(far, opposite, zz)
+                middle = (dd >= 1) & (dd <= 3)
+                in_a = (ab == 0) & middle & ((yl == 1) | (dd < 3) | (k == 0))
+                in_b = (ab == 2) & (yl == 1) & ((middle & ((dd < 3) | (k == 0))) | ((dd == 0) & (k == 0)))
+                in_far = ((ab == 1) & (d == 4) & (k == 0)) | ((ab == 3) & (yl == 1) & (d == 4) & (k == 1))
+
+                @pl.when((in_a | in_b | in_far) & (j < i))
+                def _():
+                    @pl.when(jnp.logical_not(far))
+                    def _():
+                        swapped(j)
+
+                    @pl.when(far & jnp.logical_not(far_core))
+                    def _():
+                        for part in range(4):
+                            kv_arrived(j, part)
+
                     attend(j, False, (0, 1))
 
                 return carry
 
-            return lax.fori_loop(0, 2, group, carry)
+            return lax.fori_loop(0, 4, group, carry)
 
         return lax.fori_loop(0, 2, half_step, carry)
 
     lax.fori_loop(1, 6, hop, 0)
-    last = wrap(z + 4, NZ)
+    last = wrap(z + 3, NZ)
 
     own_slots, sib_slots = [], []
     for there in (yh, 1 - yh):
@@ -308,7 +385,7 @@
 
     for k in range(2):
         for side in range(2):
-            @pl.when(z_forwards(0, side, k, z))
+            @pl.when(z_forwards(0, side, z))
             def _():
                 z_send(i, 0, side, k).wait_send()
 
@@ -326,9 +403,9 @@
                 src = ring(d, side)
                 j = first_a + src
 
-                @pl.when(held_a(d, side, k, src))
-                def _():
-                    @pl.when(z_forwards(d, side, k, src))
+                @pl.when(held_a(d, side, src))
+                def _():
+                    @pl.when(z_forwards(d, side, src))
                     def _():
                         z_send(j, d, side, k).wait_send()
 
@@ -340,13 +417,29 @@
                     def _():
                         sib_a_send(j, d, side, k).wait_send()
 
-                @pl.when((yl == 1) & held_b(d, side, k))
+                @pl.when(yl == 1)
                 def _():
                     sib_b_send(src, d, side, k).wait_send()
 
         return carry
 
-    lax.fori_loop(1, 5, drain, 0)
+    lax.fori_loop(1, 4, drain, 0)
+
+    @pl.when(far_sent)
+    def _():
+        far_z_send().wait_send()
+
+    @pl.when((yl == 0) & far_core)
+    def _():
+        far_y_send().wait_send()
+
+    for ab in range(2):
+        @pl.when(far_needed(ab))
+        def _():
+            for copy in far_x_sends(ab):
+                copy.wait_send()
+            for n in range(NX):
+                far_sib_send(ab, n).wait_send()
 
     mix[...] = jnp.zeros_like(mix)
 
@@ -436,10 +529,14 @@
             pltpu.VMEM((columns, rows), jnp.float32),
             dma((9,)),
             dma((16, 4)),
+            dma((2, 3, 2)),
             dma((2, 4, 2)),
-            dma((2, 5, 2)),
-            dma((2, 5, 2)),
-            dma((2, 5, 2)),
+            dma((2, 4, 2)),
+            dma((2, 4, 2)),
+            dma((1,)),
+            dma((1,)),
+            dma((2, 3)),
+            dma((2, 4)),
             dma((16, 2)),
             dma((8, 2, 2)),
             dma((2, 2)),

time: 54.2 us -> 60 us (1.11); the launches traced: 54.1 us -> 59.3 us
  Pallas kernels: 53.4 us -> 58.6 us
    pallas_call x1, Pallas kernels: 53.4 us -> 58.6 us  [on_device(): pl.pallas_call(kernel, out_shape=pltpu.VMEM((columns, rows), jnp.bfloat16...]
where the time goes in v16:
time: 60 us; the launch traced here: 59.3 us
  Pallas kernels  58.6 us (98%)
  local copies, waits for them, and re-layouts  0.69 us (1%)
    pallas_call x1, Pallas kernels, on_device(): pl.pallas_call(kernel, out_shape=pltpu.VMEM((columns, rows), jnp.bfloat16...  58.6 us

profile of v16, /device:TPU:9, one launch (start us, length us, event | category | flops | bytes accessed | tf_op | source)
XLA Modules:
  0.0 59.3 jit_solution(1925937117732181403)
XLA Ops:
  0.0 58.6 %shard_map.64 = bf16[448,256]{1,0:T(8,128)(2,1)S(1)} custom-call(bf16[256,512]{1,0:T(8,128)(2,1)} %qn_hbm.1, bf16[256,256]{1,0:T(8,128)(2,1)} %qr_hbm.1, bf16[4,128,512]{2,1,0:T(8,128)(2,1)} %ak_hbm.1, bf16[4,144,256]{2,1,0:T(8,128)(2,1)} %bitcast.7, bf16[4,512,128]{2,1,0:T(8,128)(2,1)} %vu_hbm.1, bf16[448,8192]{1,0:T(8,128)(2,1)} %bitcast.6), custom_call_target="tpu_custom_call" | custom-call | flops 12000000000 | bytes 10000000 | tf_op jit(solution)/shard_map/pallas_call | solution.py:512
  58.6 0.7 %copy.8 = bf16[256,448]{0,1:T(8,128)(2,1)} copy(bf16[256,448]{0,1:T(8,128)(2,1)S(1)} %bitcast.5) | data formatting | bytes 458752

commit v17 on v15

--- a/solution.py
+++ b/solution.py
@@ -240,7 +240,7 @@
                 def _():
                     relay_b(d - 1, k)
 
-                dd = d - 1 - ab
+                dd = d - 2 - ab
                 j = jnp.where(ab == 0, first_a, 0) + wrap(jnp.where(k == 0, z + NZ - dd, z + dd), NZ)
                 in_a = (ab == 0) & (((dd >= 1) & (dd <= 3)) | ((dd == 4) & (k == 0) & (yl == 1)))
                 in_b = (ab == 1) & (yl == 1) & (((dd >= 1) & (dd <= 3)) | ((dd == 0) & (k == 0)))
@@ -256,7 +256,7 @@
 
         return lax.fori_loop(0, 2, half_step, carry)
 
-    lax.fori_loop(1, 6, hop, 0)
+    lax.fori_loop(1, 7, hop, 0)
     last = wrap(z + 4, NZ)
 
     own_slots, sib_slots = [], []

time: 54.2 us -> 54.9 us (1.013); the launches traced: 54.1 us -> 54 us
  no operation moved by 1% of the time
where the time goes in v17:
time: 54.9 us; the launch traced here: 54 us
  Pallas kernels  53.3 us (97%)
  local copies, waits for them, and re-layouts  0.69 us (1%)
    pallas_call x1, Pallas kernels, on_device(): pl.pallas_call(kernel, out_shape=pltpu.VMEM((columns, rows), jnp.bfloat16...  53.3 us

profile of v17, /device:TPU:9, one launch (start us, length us, event | category | flops | bytes accessed | tf_op | source)
XLA Modules:
  0.0 54.0 jit_solution(17705628823043403165)
XLA Ops:
  0.0 53.3 %shard_map.64 = bf16[448,256]{1,0:T(8,128)(2,1)S(1)} custom-call(bf16[256,512]{1,0:T(8,128)(2,1)} %qn_hbm.1, bf16[256,256]{1,0:T(8,128)(2,1)} %qr_hbm.1, bf16[4,128,512]{2,1,0:T(8,128)(2,1)} %ak_hbm.1, bf16[4,144,256]{2,1,0:T(8,128)(2,1)} %bitcast.7, bf16[4,512,128]{2,1,0:T(8,128)(2,1)} %vu_hbm.1, bf16[448,8192]{1,0:T(8,128)(2,1)} %bitcast.6), custom_call_target="tpu_custom_call" | custom-call | flops 12000000000 | bytes 10000000 | tf_op jit(solution)/shard_map/pallas_call | solution.py:419
  53.3 0.7 %copy.8 = bf16[256,448]{0,1:T(8,128)(2,1)} copy(bf16[256,448]{0,1:T(8,128)(2,1)S(1)} %bitcast.5) | data formatting | bytes 458752

commit v18 on v15

--- a/solution.py
+++ b/solution.py
@@ -27,7 +27,7 @@
 
 def kernel(
     qn_hbm, qr_hbm, ak_hbm, kv_hbm, vu_hbm, wo_hbm, out_ref,
-    qn, qr, ak, vu, wo, kvbuf, vbuf, query, peak, total, acc, mix,
+    qn, qr, ak, vu, vu_across, wo, kvbuf, vbuf, query, peak, total, acc, mix,
     local_sem, kv_recv, send_z, send_y, sib_a, sib_b, v_recv, send_x, send_c, sib_v,
 ):
     heads, rows = ak.shape[0], qn.shape[0]
@@ -224,6 +224,9 @@
 
     own(1)
     attend(i, True, (0, 1))
+    locals_[7].wait()
+    for h in range(heads):
+        vu_across[h] = vu[h].T
 
     def swapped(j):
         for k in range(2):
@@ -273,7 +276,6 @@
             recv_sem=v_recv.at[slot, k], device_id=sibling, device_id_type=MESH,
         ).wait_recv()
 
-    locals_[7].wait()
 
     def send(e, k, way):
         sem = {
@@ -301,7 +303,7 @@
             whole = jnp.sum(total[:, at], axis=0, keepdims=True)
             latent_out = (acc[:, at] * (1.0 / whole)).astype(jnp.bfloat16)
             vbuf[o, k, (h % 2) * VDIM : (h % 2 + 1) * VDIM, :] = jnp.dot(
-                vu[h].T, latent_out, preferred_element_type=jnp.float32
+                vu_across[h], latent_out, preferred_element_type=jnp.float32
             ).astype(jnp.bfloat16)
         for way in ("up", "down", "far", "sib"):
             send(0, k, way).start()
@@ -350,16 +352,13 @@
 
     mix[...] = jnp.zeros_like(mix)
 
-    def project(slots):
+    def project(slot):
         depth = heads * VDIM
-        term = mix[...]
-        for slot in slots:
-            start = pl.multiple_of(slot * depth, depth)
-            term = term + jnp.dot(
-                wo[:, pl.ds(start, depth)], vbuf[slot].reshape(depth, rows),
-                preferred_element_type=jnp.float32,
-            )
-        mix[...] = term
+        start = pl.multiple_of(slot * depth, depth)
+        mix[...] += jnp.dot(
+            wo[:, pl.ds(start, depth)], vbuf[slot].reshape(depth, rows),
+            preferred_element_type=jnp.float32,
+        )
 
     came = (
         ((1, 0, "far"), (2, 0, "up"), (4, 0, "up")),
@@ -397,10 +396,17 @@
         n = jnp.where(t >= 4, t - 4, t)
         dx = jnp.where(n == 2, 3, jnp.where(n == 3, 2, n))
         place = outer_of(wrap(x + dx, NX), jnp.where(t >= 4, 1 - yh, yh), 0)
-        for k in range(2):
-            v_arrived(place + 1 - core, k)
-        project((place + core, place + 1 - core))
-        return carry
+
+        def half(n, carry):
+            @pl.when(n == 1)
+            def _():
+                for k in range(2):
+                    v_arrived(place + 1 - core, k)
+
+            project(place + jnp.where(n == 0, core, 1 - core))
+            return carry
+
+        return lax.fori_loop(0, 2, half, carry)
 
     lax.fori_loop(0, 8, event, 0)
     out_ref[...] = mix[...].astype(jnp.bfloat16)
@@ -426,6 +432,7 @@
             pltpu.VMEM(q_rope.shape, jnp.bfloat16),
             pltpu.VMEM(absorb_key.shape, jnp.bfloat16),
             pltpu.VMEM(value_up.shape, jnp.bfloat16),
+            pltpu.VMEM((heads, VDIM, LAT), jnp.bfloat16),
             pltpu.VMEM(out_proj.shape, jnp.bfloat16),
             pltpu.VMEM((16, 4, WIDE // 4, rows), jnp.bfloat16),
             pltpu.VMEM((16, 2, heads * VDIM // 2, rows), jnp.bfloat16),

time: 54.2 us -> 54.3 us (level)
  no operation moved by 1% of the time
where the time goes in v18:
time: 54.3 us
  Pallas kernels  53.6 us (99%)
  local copies, waits for them, and re-layouts  0.69 us (1%)
    pallas_call x1, Pallas kernels, on_device(): pl.pallas_call(kernel, out_shape=pltpu.VMEM((columns, rows), jnp.bfloat16...  53.6 us

profile of v18, /device:TPU:9, one launch (start us, length us, event | category | flops | bytes accessed | tf_op | source)
XLA Modules:
  0.0 54.3 jit_solution(11067070050046446591)
XLA Ops:
  0.0 53.6 %shard_map.64 = bf16[448,256]{1,0:T(8,128)(2,1)S(1)} custom-call(bf16[256,512]{1,0:T(8,128)(2,1)} %qn_hbm.1, bf16[256,256]{1,0:T(8,128)(2,1)} %qr_hbm.1, bf16[4,128,512]{2,1,0:T(8,128)(2,1)} %ak_hbm.1, bf16[4,144,256]{2,1,0:T(8,128)(2,1)} %bitcast.7, bf16[4,512,128]{2,1,0:T(8,128)(2,1)} %vu_hbm.1, bf16[448,8192]{1,0:T(8,128)(2,1)} %bitcast.6), custom_call_target="tpu_custom_call" | custom-call | flops 12000000000 | bytes 10000000 | tf_op jit(solution)/shard_map/pallas_call | solution.py:425
  53.6 0.7 %copy.8 = bf16[256,448]{0,1:T(8,128)(2,1)} copy(bf16[256,448]{0,1:T(8,128)(2,1)S(1)} %bitcast.5) | data formatting | bytes 458752

commit v19 on v18

--- a/solution.py
+++ b/solution.py
@@ -47,8 +47,9 @@
     y_up = (outer_of(x, wrap(yh + yl, 2), core), (1 - yl) * NZ + z)
     y_down = (outer_of(x, wrap(yh + 1 - yl, 2), core), (1 - yl) * NZ + z)
     y_far = (outer_of(x, 1 - yh, core), i)
-    x_up = (outer_of(wrap(x + 1, NX), yh, core), i)
-    x_down = (outer_of(wrap(x + NX - 1, NX), yh, core), i)
+    x_plus, x_minus = wrap(x + 1, NX), wrap(x + NX - 1, NX)
+    x_up = (outer_of(jnp.where(core == 0, x_plus, x_minus), yh, core), i)
+    x_down = (outer_of(jnp.where(core == 0, x_minus, x_plus), yh, core), i)
 
     locals_ = [
         pltpu.make_async_copy(kv_hbm.at[part], kvbuf.at[i, part], local_sem.at[part])
@@ -262,12 +263,10 @@
     lax.fori_loop(1, 6, hop, 0)
     last = wrap(z + 4, NZ)
 
-    own_slots, sib_slots = [], []
-    for there in (yh, 1 - yh):
-        for dx in (0, 1, 3, 2):
-            place = outer_of(wrap(x + dx, NX), there, 0)
-            own_slots.append(place + core)
-            sib_slots.append(place + 1 - core)
+    def slot_of(dx, there, core_):
+        return outer_of(wrap(jnp.where(core_ == 0, x + dx, x + NX - dx), NX), there, core_)
+
+    own_slots = [slot_of(dx, there, core) for there in (yh, 1 - yh) for dx in (0, 1, 3, 2)]
 
     def v_arrived(slot, k):
         piece = vbuf.at[slot, k]
@@ -395,15 +394,16 @@
 
         n = jnp.where(t >= 4, t - 4, t)
         dx = jnp.where(n == 2, 3, jnp.where(n == 3, 2, n))
-        place = outer_of(wrap(x + dx, NX), jnp.where(t >= 4, 1 - yh, yh), 0)
+        there = jnp.where(t >= 4, 1 - yh, yh)
+        own_slot, sib_slot = slot_of(dx, there, core), slot_of(dx, there, 1 - core)
 
         def half(n, carry):
             @pl.when(n == 1)
             def _():
                 for k in range(2):
-                    v_arrived(place + 1 - core, k)
-
-            project(place + jnp.where(n == 0, core, 1 - core))
+                    v_arrived(sib_slot, k)
+
+            project(jnp.where(n == 0, own_slot, sib_slot))
             return carry
 
         return lax.fori_loop(0, 2, half, carry)

time: 54.3 us -> 53.8 us (level)
  no operation moved by 1% of the time
where the time goes in v19:
time: 53.8 us
  Pallas kernels  53.1 us (99%)
  local copies, waits for them, and re-layouts  0.69 us (1%)
    pallas_call x1, Pallas kernels, on_device(): pl.pallas_call(kernel, out_shape=pltpu.VMEM((columns, rows), jnp.bfloat16...  53.1 us

profile of v19, /device:TPU:9, one launch (start us, length us, event | category | flops | bytes accessed | tf_op | source)
XLA Modules:
  0.0 53.8 jit_solution(3027113994674613498)
XLA Ops:
  0.0 53.1 %shard_map.64 = bf16[448,256]{1,0:T(8,128)(2,1)S(1)} custom-call(bf16[256,512]{1,0:T(8,128)(2,1)} %qn_hbm.1, bf16[256,256]{1,0:T(8,128)(2,1)} %qr_hbm.1, bf16[4,128,512]{2,1,0:T(8,128)(2,1)} %ak_hbm.1, bf16[4,144,256]{2,1,0:T(8,128)(2,1)} %bitcast.7, bf16[4,512,128]{2,1,0:T(8,128)(2,1)} %vu_hbm.1, bf16[448,8192]{1,0:T(8,128)(2,1)} %bitcast.6), custom_call_target="tpu_custom_call" | custom-call | flops 12000000000 | bytes 10000000 | tf_op jit(solution)/shard_map/pallas_call | solution.py:425
  53.1 0.7 %copy.8 = bf16[256,448]{0,1:T(8,128)(2,1)} copy(bf16[256,448]{0,1:T(8,128)(2,1)S(1)} %bitcast.5) | data formatting | bytes 458752

commit v20 on v19

--- a/solution.py
+++ b/solution.py
@@ -113,7 +113,7 @@
     o_far = outer_of(x, 1 - yh, core)
 
     def y_send(j, d, side, k):
-        return kv_copy(j, k, send_y.at[side, d, k], (jnp.where(k == 0, o, o_far), NZ + z))
+        return kv_copy(j, k, send_y.at[side, d, k], (jnp.where(k == core, o, o_far), NZ + z))
 
     def sib_a_send(j, d, side, k):
         return kv_copy(j, k, sib_a.at[side, d, k], sibling)

time: 53.8 us -> 53.8 us (level)
  no operation moved by 1% of the time
where the time goes in v20:
time: 53.8 us; the launch traced here: 53.7 us
  Pallas kernels  53 us (99%)
  local copies, waits for them, and re-layouts  0.69 us (1%)
    pallas_call x1, Pallas kernels, on_device(): pl.pallas_call(kernel, out_shape=pltpu.VMEM((columns, rows), jnp.bfloat16...  53 us

profile of v20, /device:TPU:9, one launch (start us, length us, event | category | flops | bytes accessed | tf_op | source)
XLA Modules:
  0.0 53.7 jit_solution(991187871713879319)
XLA Ops:
  0.0 53.0 %shard_map.64 = bf16[448,256]{1,0:T(8,128)(2,1)S(1)} custom-call(bf16[256,512]{1,0:T(8,128)(2,1)} %qn_hbm.1, bf16[256,256]{1,0:T(8,128)(2,1)} %qr_hbm.1, bf16[4,128,512]{2,1,0:T(8,128)(2,1)} %ak_hbm.1, bf16[4,144,256]{2,1,0:T(8,128)(2,1)} %bitcast.7, bf16[4,512,128]{2,1,0:T(8,128)(2,1)} %vu_hbm.1, bf16[448,8192]{1,0:T(8,128)(2,1)} %bitcast.6), custom_call_target="tpu_custom_call" | custom-call | flops 12000000000 | bytes 10000000 | tf_op jit(solution)/shard_map/pallas_call | solution.py:425
  53.0 0.7 %copy.8 = bf16[256,448]{0,1:T(8,128)(2,1)} copy(bf16[256,448]{0,1:T(8,128)(2,1)S(1)} %bitcast.5) | data formatting | bytes 458752
